TPU v7x, 512 devices: a whole 4x4x16 slice. The times are simulated.
512 devices in a mesh: replica: 64 (over x, z_hi, y), tensor: 8 (over z_lo, core).
Axes of the slice: x: 4, y: 4, z: 16 (z_hi: 4, z_lo: 4; z = z_hi * 4 + z_lo), core: 2. Of those that a mesh axis runs over, the one named last changes fastest.
Arguments:
- w_gate: bfloat16 [64, 1024, 3072], P('replica', None, 'tensor'), may hold values from -6 to 6
- w_up: bfloat16 [64, 1024, 3072], P('replica', None, 'tensor'), may hold values from -6 to 6
- w_down: bfloat16 [64, 3072, 1024], P('replica', 'tensor'), may hold values from -6 to 6
- pool: bfloat16 [64, 512, 1024], P('replica', None, 'tensor'), may hold values from -6 to 6
- rows_index: int32 [64, 2, 2, 128], P('replica'), may hold values from 0 to 511
- partners: int32 [2, 64], replicated, may hold values from 0 to 63, as said below
Outputs:
- new_gate: bfloat16 [64, 1024, 3072], P('replica', None, 'tensor')
- new_up: bfloat16 [64, 1024, 3072], P('replica', None, 'tensor')
- new_down: bfloat16 [64, 3072, 1024], P('replica', 'tensor')
Inputs may be any that keep to these rules, and one draw needn't show every extreme that they name: Each row pairs the 64 replicas: partners[r, partners[r, i]] equals i and partners[r, i] differs from i.
All inputs are finite; a program needn't handle non-finite values.
Results may differ from a plain program's by a relative error of at most 0.029.
Values may be sent and summed in bfloat16 or wider, within the bound.
No kernel may reach another device: no remote copies, remote signals or barrier semaphores. Data moves between devices by JAX's collectives and lax.ppermute only.
A program may use at most 128 MiB of HBM per device.

v0:
```python
import jax
import jax.numpy as jnp
from jax import lax
from jax.sharding import PartitionSpec as P

D = 1024
FF = 3072
ROUNDS = 2


inner_rate = 1.0
outer_rate = 0.5
momentum_rate = 0.9


def sent_together(arrays, axis, dim, along):
    both = jnp.concatenate(arrays, axis=along)
    whole, at, done = (lax.all_gather(both, axis, axis=dim, tiled=True), 0, [])
    for a in arrays:
        done.append(lax.slice_in_dim(whole, at, at + a.shape[along], axis=along))
        at += a.shape[along]
    return tuple(done)


def copy_for_each(x, axis):
    peers = lax.axis_size(axis)
    return lax.all_to_all(jnp.broadcast_to(x[None], (peers, *x.shape)), axis, 0, 0, tiled=True)


def of_everyone(x, axis):
    everything = copy_for_each(x, axis)
    return jnp.sum(everything.astype(jnp.float32), axis=0)


def local_step(weights, pool_cols, picked):
    w_gate, w_up, w_down = weights
    in_scale = D ** (-0.5)
    hid_scale = FF ** (-0.5)
    in_cols = jnp.take(pool_cols, picked[0], axis=0)
    out_cols = jnp.take(pool_cols, picked[1], axis=0)
    inputs, targets = sent_together((in_cols, out_cols), "tensor", 1, 0)
    gate_pre = jnp.dot(inputs, w_gate, preferred_element_type=jnp.float32) * in_scale
    up_value = jnp.dot(inputs, w_up, preferred_element_type=jnp.float32) * in_scale
    sigmoid_gate = jax.nn.sigmoid(gate_pre)
    active = gate_pre * sigmoid_gate
    hidden = (active * up_value).astype(jnp.bfloat16)
    partial_sum = jnp.dot(hidden, w_down, preferred_element_type=jnp.float32) * hid_scale
    branch = of_everyone(partial_sum.astype(jnp.bfloat16), "tensor").astype(jnp.float32)
    errors = (inputs.astype(jnp.float32) + branch - targets.astype(jnp.float32)).astype(
        jnp.bfloat16
    )
    back_grad = (
        lax.dot_general(
            errors, w_down, (((1,), (1,)), ((), ())), preferred_element_type=jnp.float32
        )
        * hid_scale
    )
    delta_gate = (
        back_grad * up_value * sigmoid_gate * (1.0 + gate_pre * (1.0 - sigmoid_gate))
    ).astype(jnp.bfloat16)
    delta_up = (back_grad * active).astype(jnp.bfloat16)
    contract_rows = (((0,), (0,)), ((), ()))
    grad_gate = (
        lax.dot_general(inputs, delta_gate, contract_rows, preferred_element_type=jnp.float32)
        * in_scale
    )
    grad_up = (
        lax.dot_general(inputs, delta_up, contract_rows, preferred_element_type=jnp.float32)
        * in_scale
    )
    grad_down = (
        lax.dot_general(hidden, errors, contract_rows, preferred_element_type=jnp.float32)
        * hid_scale
    )
    gradients = (grad_gate, grad_up, grad_down)
    return tuple(
        (
            (weight.astype(jnp.float32) - inner_rate * gradient).astype(jnp.bfloat16)
            for weight, gradient in zip(weights, gradients)
        )
    )


def outer_update(weight, stepped, partner_step, partner_moment):
    pair_mean = 0.5 * (stepped.astype(jnp.float32) + partner_step.astype(jnp.float32))
    outer_grad = weight.astype(jnp.float32) - pair_mean
    moment_new = momentum_rate * 0.5 * partner_moment.astype(jnp.float32) + outer_grad
    updated = weight.astype(jnp.float32) - outer_rate * (momentum_rate * moment_new + outer_grad)
    return (updated.astype(jnp.bfloat16), moment_new.astype(jnp.bfloat16))


def make_share(stepped, moment):
    return (0.475 * stepped.astype(jnp.float32) - 0.2025 * moment.astype(jnp.float32)).astype(
        jnp.bfloat16
    )


def final_update(weight, stepped, moment, partner_share):
    updated = (
        0.05 * weight.astype(jnp.float32)
        + 0.475 * stepped.astype(jnp.float32)
        - 0.2025 * moment.astype(jnp.float32)
        + partner_share.astype(jnp.float32)
    )
    return updated.astype(jnp.bfloat16)


def partner_copy(payload, partner_row):
    replica_count = lax.axis_size("replica")
    stacked = jnp.stack([member.reshape(replica_count, -1) for member in payload])
    placed = jnp.take(
        lax.all_to_all(stacked, "replica", split_axis=1, concat_axis=1, tiled=True),
        partner_row,
        axis=1,
    )
    arrived = lax.all_to_all(placed, "replica", split_axis=1, concat_axis=1, tiled=True)
    return tuple(
        (arrived[index_mem].reshape(initial.shape) for index_mem, initial in enumerate(payload))
    )


def body(w_gate, w_up, w_down, pool, rows_index, partners):
    weights = (w_gate[0], w_up[0], w_down[0])
    moments = tuple((jnp.zeros_like(weight) for weight in weights))
    pool_cols = pool[0]
    for outer_step in range(ROUNDS):
        partner_row = partners[outer_step]
        picked = rows_index[0, outer_step]
        last_round = outer_step == ROUNDS - 1
        partner_share = None
        if last_round:
            stepped = local_step(weights, pool_cols, picked)
            own_share = tuple(
                (make_share(stepped[index_mat], moments[index_mat]) for index_mat in range(3))
            )
            partner_share = partner_copy(own_share, partner_row)
        else:
            stepped = local_step(weights, pool_cols, picked)
            partner_step = partner_copy(stepped, partner_row)
            partner_moment = moments
        if last_round:
            weights = tuple(
                (
                    final_update(
                        weights[index_mat],
                        stepped[index_mat],
                        moments[index_mat],
                        partner_share[index_mat],
                    )
                    for index_mat in range(3)
                )
            )
        else:
            results = [
                outer_update(
                    weights[index_mat],
                    stepped[index_mat],
                    partner_step[index_mat],
                    partner_moment[index_mat],
                )
                for index_mat in range(3)
            ]
            weights = tuple((result_pair[0] for result_pair in results))
            moments = tuple((result_pair[1] for result_pair in results))
    return (weights[0][None], weights[1][None], weights[2][None])


def solution(mesh):
    return jax.shard_map(
        body,
        mesh=mesh,
        in_specs=(
            P("replica", None, "tensor"),
            P("replica", None, "tensor"),
            P("replica", "tensor", None),
            P("replica", None, "tensor"),
            P("replica", None, None, None),
            P(),
        ),
        out_specs=(
            P("replica", None, "tensor"),
            P("replica", None, "tensor"),
            P("replica", "tensor", None),
        ),
        check_vma=False,
    )
```

profile of v0, /device:TPU:1, one launch (start us, length us, event | category | flops | bytes accessed | tf_op | source)
XLA Modules:
  0.0 863.1 jit_solution(2325695560171465453)
XLA Ops:
  0.7 0.9 compare_and_fusion.2
  1.6 0.7 gather_fusion
  2.3 0.7 gather_fusion.1
  3.1 20.7 %all_gather.6 = bf16[256,1024]{1,0:T(8,128)(2,1)S(1)} all-gather(bf16[256,128]{1,0:T(8,128)(2,1)S(1)} %pad_maximum_fusion.2), channel_id=1, replica_groups=mesh['replica'=64,'tensor'=8] {'tensor'}, dimensions={1}, use_global_device_ids=true | all-gather | bytes 589824 | tf_op jit(solution)/shard_map/all_gather | solution.py:18
  23.8 0.3 convolution_multiply_fusion.7
  24.2 0.3 multiply_convert_fusion.5
  24.5 0.5 copy-done.2
  25.0 0.3 fusion.30
  25.3 0.3 broadcast_in_dim.40
  25.6 50.6 %all_to_all.30 = bf16[8,128,1024]{2,1,0:T(8,128)(2,1)S(1)} all-to-all(bf16[8,128,1024]{2,1,0:T(8,128)(2,1)S(1)} %broadcast_in_dim.40), channel_id=1, replica_groups=mesh['replica'=64,'tensor'=8] {'tensor'}, dimensions={0} | all-to-all | bytes 4194304 | tf_op jit(solution)/shard_map/all_to_all | solution.py:27
  76.2 0.4 convert_reduce_fusion.1
  76.6 0.4 convolution_multiply_fusion.5
  77.0 0.4 fusion.19
  77.4 0.4 fusion.17
  77.8 0.4 fusion.15
  78.3 1.9 stack_reshape.24
  80.2 1.8 stack_reshape.25
  82.0 1.9 stack_reshape.26
  83.9 7.8 pad_maximum_fusion
  91.8 15.5 %all-to-all-start.1 = ((bf16[3,64,6144]{2,0,1:T(4,128)(2,1)}), bf16[3,64,6144]{2,0,1:T(4,128)(2,1)S(1)}, u32[]{:S(2)}, u32[]{:S(2)}) async-start(bf16[3,64,6144]{2,0,1:T(4,128)(2,1)} %pad_maximum_fusion), calls=%async_computation.1 | async-start | bytes 6291456 | tf_op jit(solution)/shard_map/all_to_all | solution.py:112
  107.3 142.5 %all-to-all-done.1 = bf16[3,64,6144]{2,0,1:T(4,128)(2,1)S(1)} async-done(((bf16[3,64,6144]{2,0,1:T(4,128)(2,1)}), bf16[3,64,6144]{2,0,1:T(4,128)(2,1)S(1)}, u32[]{:S(2)}, u32[]{:S(2)}) %all-to-all-start.1) | async-done | bytes 2359328 | tf_op jit(solution)/shard_map/all_to_all | solution.py:112
  249.8 4.7 gather_fusion.2
  254.5 5.0 select_bitcast_fusion.1
  259.5 10.1 %all-to-all-start.2 = ((bf16[3,64,6144]{2,0,1:T(4,128)(2,1)}), bf16[3,64,6144]{2,0,1:T(4,128)(2,1)S(1)}, u32[]{:S(2)}, u32[]{:S(2)}) async-start(bf16[3,64,6144]{2,0,1:T(4,128)(2,1)} %select_bitcast_fusion.1), calls=%async_computation.2 | async-start | bytes 6291456 | tf_op jit(solution)/shard_map/all_to_all | solution.py:116
  269.7 0.7 gather_fusion.4
  270.4 0.7 gather_fusion.3
  271.2 136.3 %all_gather.7 = bf16[256,1024]{1,0:T(8,128)(2,1)} all-gather(bf16[256,128]{1,0:T(8,128)(2,1)S(1)} %pad_maximum_fusion.3), channel_id=1, replica_groups=mesh['replica'=64,'tensor'=8] {'tensor'}, dimensions={1}, use_global_device_ids=true | all-gather | bytes 589824 | tf_op jit(solution)/shard_map/all_gather | solution.py:18
  407.6 14.5 %fusion.29 = (f32[64,6144]{1,0:T(8,128)}, f32[64,6144]{1,0:T(8,128)}, f32[64,6144]{1,0:T(8,128)}) fusion(bf16[3,64,6144]{2,0,1:T(4,128)(2,1)S(1)} %all-to-all-done.2), kind=kLoop, calls=%fused_computation.65 | loop fusion | flops 1179648 | bytes 7077888 | tf_op jit(solution)/shard_map/convert_element_type | solution.py:85
  422.1 1.7 reshape.40
  423.8 2.2 fusion.20
  426.1 1.6 reshape.39
  427.7 3.3 fusion.18
  431.0 1.6 reshape.38
  432.6 2.0 fusion.16
  434.6 0.3 convolution_multiply_fusion.4
  434.9 0.3 multiply_convert_fusion.2
  435.2 0.3 fusion.31
  435.6 0.3 broadcast_in_dim.41
  435.8 57.5 %all_to_all.31 = bf16[8,128,1024]{2,1,0:T(8,128)(2,1)S(1)} all-to-all(bf16[8,128,1024]{2,1,0:T(8,128)(2,1)S(1)} %broadcast_in_dim.41), channel_id=1, replica_groups=mesh['replica'=64,'tensor'=8] {'tensor'}, dimensions={0} | all-to-all | bytes 4194304 | tf_op jit(solution)/shard_map/all_to_all | solution.py:27
  493.3 0.4 convert_reduce_fusion
  493.8 0.4 convolution_multiply_fusion.2
  494.2 0.9 copy-done.7
  495.1 0.2 copy-done.11
  495.3 2.2 subtract_convert_fusion
  497.5 2.2 subtract_convert_fusion.1
  499.7 2.2 subtract_convert_fusion.2
  502.0 4.4 stack_reshape.27
  506.4 5.4 stack_reshape.28
  511.8 1.9 stack_reshape.29
  513.8 7.7 pad_maximum_fusion.1
  521.5 15.7 %all-to-all-start.4 = ((bf16[3,64,6144]{2,0,1:T(4,128)(2,1)}), bf16[3,64,6144]{2,0,1:T(4,128)(2,1)}, u32[]{:S(2)}, u32[]{:S(2)}) async-start(bf16[3,64,6144]{2,0,1:T(4,128)(2,1)} %pad_maximum_fusion.1), calls=%async_computation.4 | async-start | bytes 6291456 | tf_op jit(solution)/shard_map/all_to_all | solution.py:112
  537.2 142.4 %all-to-all-done.4 = bf16[3,64,6144]{2,0,1:T(4,128)(2,1)} async-done(((bf16[3,64,6144]{2,0,1:T(4,128)(2,1)}), bf16[3,64,6144]{2,0,1:T(4,128)(2,1)}, u32[]{:S(2)}, u32[]{:S(2)}) %all-to-all-start.4) | async-done | bytes 2359328 | tf_op jit(solution)/shard_map/all_to_all | solution.py:112
  679.6 6.6 gather_fusion.5
  686.2 3.4 select_bitcast_fusion
  689.6 145.4 %all_to_all.32 = bf16[3,64,6144]{2,0,1:T(4,128)(2,1)S(1)} all-to-all(bf16[3,64,6144]{2,0,1:T(4,128)(2,1)S(1)} %select_bitcast_fusion), channel_id=1, replica_groups=mesh['replica'=64,'tensor'=8] {'replica'}, dimensions={1} | all-to-all | bytes 4718592 | tf_op jit(solution)/shard_map/all_to_all | solution.py:116
  835.0 14.0 %fusion.24 = (f32[64,6144]{1,0:T(8,128)}, f32[64,6144]{1,0:T(8,128)}, f32[64,6144]{1,0:T(8,128)S(1)}) fusion(bf16[3,64,6144]{2,0,1:T(4,128)(2,1)S(1)} %all_to_all.32), kind=kLoop, calls=%fused_computation.55 | loop fusion | flops 1179648 | bytes 7077888 | tf_op jit(solution)/shard_map/convert_element_type | solution.py:103
  849.0 2.7 reshape.43
  851.7 2.6 reshape.42
  854.3 1.4 reshape.41
  855.7 3.2 fusion.35
  859.0 1.4 fusion.36
  860.4 0.5 copy-done.21
  861.1 0.2 copy-done.25
  861.3 1.4 fusion.37
  (73 shorter events, 0.8 us)
Async XLA Ops:
  0.6 0.9 copy-start
  0.6 23.2 %copy-start.12 = (bf16[1,1024,384]{2,1,0:T(8,128)(2,1)S(1)}, bf16[1,1024,384]{2,1,0:T(8,128)(2,1)}, u32[]{:S(2)}) copy-start(bf16[1,1024,384]{2,1,0:T(8,128)(2,1)} %param.10) | copy-start | bytes 2359300
  0.7 23.5 %copy-start.29 = (bf16[1,1024,384]{2,1,0:T(8,128)(2,1)S(1)}, bf16[1,1024,384]{2,1,0:T(8,128)(2,1)}, u32[]{:S(2)}) copy-start(bf16[1,1024,384]{2,1,0:T(8,128)(2,1)} %param.11) | copy-start | bytes 2359300
  23.8 1.1 copy-start.2
  77.4 4.6 copy-start.10
  77.8 2.4 copy-start.18
  78.3 3.7 copy-start.14
  91.8 15.5 %copy-start.31 = (s32[2,64]{1,0:T(2,128)S(1)}, s32[2,64]{1,0:T(2,128)}, u32[]{:S(2)}) copy-start(s32[2,64]{1,0:T(2,128)} %param.15) | copy-start | bytes 1540
  91.8 158.0 %all-to-all-start.1 = ((bf16[3,64,6144]{2,0,1:T(4,128)(2,1)}), bf16[3,64,6144]{2,0,1:T(4,128)(2,1)S(1)}, u32[]{:S(2)}, u32[]{:S(2)}) async-start(bf16[3,64,6144]{2,0,1:T(4,128)(2,1)} %pad_maximum_fusion), calls=%async_computation.1 | async-start | bytes 6291456 | tf_op jit(solution)/shard_map/all_to_all | solution.py:112
  259.5 148.0 %all-to-all-start.2 = ((bf16[3,64,6144]{2,0,1:T(4,128)(2,1)}), bf16[3,64,6144]{2,0,1:T(4,128)(2,1)S(1)}, u32[]{:S(2)}, u32[]{:S(2)}) async-start(bf16[3,64,6144]{2,0,1:T(4,128)(2,1)} %select_bitcast_fusion.1), calls=%async_computation.2 | async-start | bytes 6291456 | tf_op jit(solution)/shard_map/all_to_all | solution.py:116
  422.1 1.7 copy-start.3
  423.8 2.2 copy-start.6
  427.7 3.4 copy-start.4
  432.6 2.0 copy-start.20
  432.6 2.3 copy-start.16
  434.6 65.1 %copy-start.8 = (bf16[1024,384]{1,0:T(8,128)(2,1)}, bf16[1024,384]{1,0:T(8,128)(2,1)S(1)}, u32[]{:S(2)}) copy-start(bf16[1024,384]{1,0:T(8,128)(2,1)S(1)} %fusion.16) | copy-start | bytes 2359300
  493.7 1.4 copy-start.7
  493.7 1.6 copy-start.11
  495.3 2.2 copy-start.5
  495.3 2.2 copy-start.19
  495.3 2.2 copy-start.30
  497.5 2.2 copy-start.13
  497.5 2.2 copy-start.15
  506.4 5.4 copy-start.26
  521.5 158.2 %all-to-all-start.4 = ((bf16[3,64,6144]{2,0,1:T(4,128)(2,1)}), bf16[3,64,6144]{2,0,1:T(4,128)(2,1)}, u32[]{:S(2)}, u32[]{:S(2)}) async-start(bf16[3,64,6144]{2,0,1:T(4,128)(2,1)} %pad_maximum_fusion.1), calls=%async_computation.4 | async-start | bytes 6291456 | tf_op jit(solution)/shard_map/all_to_all | solution.py:112
  854.3 1.4 copy-start.23
  855.7 3.2 copy-start.17
  855.7 3.2 copy-start.22
  855.7 3.2 copy-start.27
  855.7 3.2 copy-start.28
  858.9 1.4 copy-start.9
  858.9 1.9 copy-start.21
  858.9 2.1 copy-start.24
  859.0 2.3 copy-start.25
  860.4 2.3 copy-start.1
where the time goes:
time: 870 us; the launch traced here: 863 us
  blocking collectives  411 us (47%)
  waiting for transfers between devices  285 us (33%)
  other arithmetic  68 us (8%)
  local copies, waits for them, and re-layouts  46.2 us (5%)
  starting transfers between devices  41.4 us (5%)
  matrix products  10.4 us (1%)
    all_to_all x2, waiting for transfers between devices, partner_copy(): lax.all_to_all(stacked, 'replica', split_axis=1, concat_axis=1, tiled=True)  285 us
    all_gather x2, blocking collectives, sent_together(): whole, at, done = (lax.all_gather(both, axis, axis=dim, tiled=True), 0, [])  157 us
    all_to_all x1, blocking collectives, partner_copy(): lax.all_to_all(placed, 'replica', split_axis=1, concat_axis=1, tiled=True)  145 us
    all_to_all x2, blocking collectives, copy_for_each(): lax.all_to_all(jnp.broadcast_to(x[None], (peers, *x.shape)), axis, 0, 0,...  108 us
    all_to_all x2, starting transfers between devices, partner_copy(): lax.all_to_all(stacked, 'replica', split_axis=1, concat_axis=1, tiled=True)  31.3 us
    another operation x6, local copies, waits for them, and re-layouts, partner_copy(): jnp.stack([member.reshape(replica_count, -1) for member in payload])  17.4 us
  transfers between devices with their start and end apart: 3, of which 2 were waited for; matrix products, arithmetic and copies ran while one was open for 0% of the time, Pallas kernels for 0%

commit v1 on v0

v1 whole, which is shorter than its diff:
```python
import jax
import jax.numpy as jnp
from jax import lax
from jax.experimental import pallas as pl
from jax.experimental.pallas import tpu as pltpu
from jax.sharding import Mesh, PartitionSpec as P

D = 1024
FF = 3072
REPLICAS = 64
N_TENSOR = 8
PLANE = 16
PLANES = 4
ROUNDS = 2
IN_SCALE = D**-0.5
HID_SCALE = FF**-0.5

inner_rate = 1.0
outer_rate = 0.5
momentum_rate = 0.9

REPLICA = ("x", "h", "y")
FLAT = ("x", "y")
TENSOR = ("l", "c")

NEXT_SLOTS = (5, 6, 7, 8)
FAR_SLOTS = (4, 5, 6, 8)
SLOTS = [(n, f) for n in NEXT_SLOTS for f in FAR_SLOTS] + [(PLANE, PLANE)]


def routes(partners):
    me = lax.axis_index("h")
    ids = jnp.arange(REPLICAS, dtype=jnp.int32)
    plane = (ids // 4) % PLANES
    flat = (ids // PLANE) * 4 + ids % 4
    to_plane = (partners // 4) % PLANES
    off = (to_plane - plane + PLANES) % PLANES
    same = (plane[:, None] == plane[None, :]) & (flat[None, :] < flat[:, None])
    rank = jnp.sum((same & (off[:, :, None] == off[:, None, :])).astype(jnp.int32), axis=2)
    slots = jnp.arange(PLANE, dtype=jnp.int32)
    offs = jnp.array([1, 3, 2], jnp.int32)
    here = (plane == me)[None, None, None, :]
    sends = here & (off[:, None, None, :] == offs[None, :, None, None])
    sends = sends & (rank[:, None, None, :] == slots[None, None, :, None])
    send_index = jnp.sum(jnp.where(sends, flat, 0), axis=3)
    home = (slots // 4) * PLANE + me * 4 + slots % 4
    wanted = partners[:, None, :] == home[None, :, None]
    come_from = (plane[None, :] - me + PLANES) % PLANES
    kind = jnp.sum(jnp.where(wanted, come_from[:, None, :], 0), axis=2)
    place = jnp.where(off == 0, flat[None, :], rank)
    slot = jnp.sum(jnp.where(wanted, place[:, None, :], 0), axis=2)
    most_next = jnp.max(jnp.where(off % 2 == 1, rank + 1, 0), axis=1)
    most_far = jnp.max(jnp.where(off == 2, rank + 1, 0), axis=1)
    case_next = sum((most_next > n).astype(jnp.int32) for n in NEXT_SLOTS[:-1])
    case_far = sum((most_far > n).astype(jnp.int32) for n in FAR_SLOTS[:-1])
    fits = (most_next <= NEXT_SLOTS[-1]) & (most_far <= FAR_SLOTS[-1])
    case = jnp.where(fits, case_next * len(FAR_SLOTS) + case_far, len(SLOTS) - 1)
    return case, send_index, jnp.stack([kind, slot], axis=1)


def pick_kernel(index, chunks, *rest):
    outs, sem = rest[:3], rest[3]
    copies, at = [], 0
    for o, out in enumerate(outs):
        for k in range(out.shape[0]):
            copies.append(pltpu.make_async_copy(chunks.at[index[o, k]], out.at[k], sem.at[at]))
            at += 1
    for copy in copies:
        copy.start()
    for copy in copies:
        copy.wait()


def pick(index, chunks, counts):
    anywhere = pl.BlockSpec(memory_space=pl.ANY)
    return pl.pallas_call(
        pick_kernel,
        out_shape=tuple(
            jax.ShapeDtypeStruct((n, *chunks.shape[1:]), chunks.dtype) for n in counts
        ),
        grid_spec=pltpu.PrefetchScalarGridSpec(
            num_scalar_prefetch=1,
            grid=(1,),
            in_specs=[anywhere],
            out_specs=(anywhere,) * 3,
            scratch_shapes=[pltpu.SemaphoreType.DMA((sum(counts),))],
        ),
        cost_estimate=pl.CostEstimate(
            flops=0, bytes_accessed=4 * PLANE * chunks[0].size, transcendentals=0
        ),
    )(index, chunks)


def place_kernel(where, own, ahead, behind, far, out, sem):
    sources = (own, ahead, far, behind)
    for d in range(PLANE):
        for kind, source in enumerate(sources):

            @pl.when(where[0, d] == kind)
            def _(d=d, source=source):
                pltpu.make_async_copy(source.at[where[1, d]], out.at[d], sem.at[d]).start()

    for d in range(PLANE):
        pltpu.make_async_copy(own.at[0], out.at[d], sem.at[d]).wait()


def place(where, own, ahead, behind, far):
    anywhere = pl.BlockSpec(memory_space=pl.ANY)
    return pl.pallas_call(
        place_kernel,
        out_shape=jax.ShapeDtypeStruct(own.shape, own.dtype),
        grid_spec=pltpu.PrefetchScalarGridSpec(
            num_scalar_prefetch=1,
            grid=(1,),
            in_specs=[anywhere] * 4,
            out_specs=anywhere,
            scratch_shapes=[pltpu.SemaphoreType.DMA((PLANE,))],
        ),
        cost_estimate=pl.CostEstimate(
            flops=0, bytes_accessed=4 * own.size, transcendentals=0
        ),
    )(where, own, ahead, behind, far)


def step_by(n):
    return [(i, (i + n) % PLANES) for i in range(PLANES)]


def swap(arrays, send_index, where, n_next, n_far):
    shares = [
        lax.all_to_all(a.reshape(PLANE, a.shape[0] // PLANE, a.shape[1]), FLAT, 0, 0, tiled=True)
        for a in arrays
    ]
    moved = []
    for share in shares:
        up, down, across = pick(send_index, share, (n_next, n_next, n_far))
        from_behind = lax.ppermute(up, "h", step_by(1))
        from_ahead = lax.ppermute(down, "h", step_by(-1))
        from_far = lax.ppermute(across, "h", step_by(2))
        moved.append((from_ahead, from_behind, from_far))
    got = []
    for a, share, parts in zip(arrays, shares, moved):
        placed = place(where, share, *parts)
        got.append(lax.all_to_all(placed, FLAT, 0, 0, tiled=True).reshape(a.shape))
    return tuple(got)


def partner_copy(arrays, route):
    case, send_index, where = route
    branches = [
        lambda arrays, s, w, n=n, f=f: swap(arrays, s, w, n, f) for n, f in SLOTS
    ]
    return lax.switch(case, branches, arrays, send_index, where)


def local_step(weights, inputs, in_cols, out_cols):
    w_gate, w_up, w_down = weights
    gate_pre = jnp.dot(inputs, w_gate, preferred_element_type=jnp.float32) * IN_SCALE
    up_value = jnp.dot(inputs, w_up, preferred_element_type=jnp.float32) * IN_SCALE
    sigmoid_gate = jax.nn.sigmoid(gate_pre)
    active = gate_pre * sigmoid_gate
    hidden = (active * up_value).astype(jnp.bfloat16)
    term = jnp.dot(hidden, w_down, preferred_element_type=jnp.float32) * HID_SCALE
    cols = D // N_TENSOR
    term = term.astype(jnp.bfloat16)
    blocks = jnp.stack([term[:, k * cols : (k + 1) * cols] for k in range(N_TENSOR)])
    terms = lax.all_to_all(blocks, TENSOR, 0, 0, tiled=True)
    branch = jnp.sum(terms.astype(jnp.float32), axis=0)
    error_cols = (in_cols.astype(jnp.float32) + branch - out_cols.astype(jnp.float32)).astype(
        jnp.bfloat16
    )
    errors = lax.all_gather(error_cols, TENSOR, axis=1, tiled=True)
    back = (
        lax.dot_general(
            errors, w_down, (((1,), (1,)), ((), ())), preferred_element_type=jnp.float32
        )
        * HID_SCALE
    )
    delta_gate = (back * up_value * sigmoid_gate * (1.0 + gate_pre * (1.0 - sigmoid_gate))).astype(
        jnp.bfloat16
    )
    delta_up = (back * active).astype(jnp.bfloat16)
    rows = (((0,), (0,)), ((), ()))

    def grad(a, b, scale):
        return lax.dot_general(a, b, rows, preferred_element_type=jnp.float32) * scale

    gradients = (
        grad(inputs, delta_gate, IN_SCALE),
        grad(inputs, delta_up, IN_SCALE),
        grad(hidden, errors, HID_SCALE),
    )
    return tuple(
        (w.astype(jnp.float32) - inner_rate * g).astype(jnp.bfloat16)
        for w, g in zip(weights, gradients)
    )


def outer_update(weight, stepped, partner_step):
    weight = weight.astype(jnp.float32)
    pair_mean = 0.5 * (stepped.astype(jnp.float32) + partner_step.astype(jnp.float32))
    outer_grad = weight - pair_mean
    moment_new = outer_grad
    updated = weight - outer_rate * (momentum_rate * moment_new + outer_grad)
    return updated.astype(jnp.bfloat16), moment_new.astype(jnp.bfloat16)


def make_share(stepped, moment):
    return (0.475 * stepped.astype(jnp.float32) - 0.2025 * moment.astype(jnp.float32)).astype(
        jnp.bfloat16
    )


def final_update(weight, stepped, moment, partner_share):
    updated = (
        0.05 * weight.astype(jnp.float32)
        + 0.475 * stepped.astype(jnp.float32)
        - 0.2025 * moment.astype(jnp.float32)
        + partner_share.astype(jnp.float32)
    )
    return updated.astype(jnp.bfloat16)


def body(w_gate, w_up, w_down, pool, rows_index, partners):
    weights = (w_gate[0], w_up[0], w_down[0])
    case, send_index, where = routes(partners)
    picked = jnp.take(pool[0], rows_index[0].reshape(-1), axis=0)
    picked = picked.reshape(ROUNDS, 2, -1, picked.shape[-1])
    in_cols, out_cols = picked[:, 0], picked[:, 1]
    inputs = lax.all_gather(in_cols, TENSOR, axis=2, tiled=True)

    stepped = local_step(weights, inputs[0], in_cols[0], out_cols[0])
    theirs = partner_copy(stepped, (case[0], send_index[0], where[0]))
    results = [outer_update(*each) for each in zip(weights, stepped, theirs)]
    weights = tuple(r[0] for r in results)
    moments = tuple(r[1] for r in results)

    stepped = local_step(weights, inputs[1], in_cols[1], out_cols[1])
    shares = tuple(make_share(s, m) for s, m in zip(stepped, moments))
    theirs = partner_copy(shares, (case[1], send_index[1], where[1]))
    new = [final_update(*each) for each in zip(weights, stepped, moments, theirs)]
    return tuple(w[None] for w in new)


def solution(mesh):
    grid = Mesh(mesh.devices.reshape(4, 4, 4, 4, 2), ("x", "h", "y", "l", "c"))
    return jax.shard_map(
        body,
        mesh=grid,
        in_specs=(
            P(REPLICA, None, TENSOR),
            P(REPLICA, None, TENSOR),
            P(REPLICA, TENSOR, None),
            P(REPLICA, None, TENSOR),
            P(REPLICA, None, None, None),
            P(),
        ),
        out_specs=(
            P(REPLICA, None, TENSOR),
            P(REPLICA, None, TENSOR),
            P(REPLICA, TENSOR, None),
        ),
        check_vma=False,
    )
```

time: 870 us -> 1020 us (1.17)
  the two profiles are of different devices: /device:TPU:1 before, /device:TPU:64 now
where the time goes in v1:
time: 1020 us; the launch traced here: 1010 us
  Pallas kernels  332 us (33%)
  waiting for transfers between devices  265 us (26%)
  starting transfers between devices  175 us (17%)
  blocking collectives  118 us (12%)
  loops' own time  52.5 us (5%)
  other arithmetic  26.9 us (3%)
  local copies, waits for them, and re-layouts  22.8 us (2%)
  matrix products  13.6 us (1%)
    pallas_call x6, Pallas kernels, pick(): pl.pallas_call(pick_kernel, out_shape=tuple((jax.ShapeDtypeStruct((n, *ch...  177 us
    pallas_call x6, Pallas kernels, place(): pl.pallas_call(place_kernel, out_shape=jax.ShapeDtypeStruct(own.shape, ow...  155 us
    ppermute x6, waiting for transfers between devices, swap(): from_ahead = lax.ppermute(down, 'h', step_by(-1))  108 us
    ppermute x6, waiting for transfers between devices, swap(): from_far = lax.ppermute(across, 'h', step_by(2))  103 us
    all_to_all x4, blocking collectives, swap(): lax.all_to_all(a.reshape(PLANE, a.shape[0] // PLANE, a.shape[1]), FLAT, 0...  72.6 us
    unnamed x2, loops' own time  52.5 us
    ppermute x6, starting transfers between devices, swap(): from_far = lax.ppermute(across, 'h', step_by(2))  44.9 us
    all_to_all x6, starting transfers between devices, swap(): got.append(lax.all_to_all(placed, FLAT, 0, 0, tiled=True).reshape(a.shape))  42 us
  transfers between devices with their start and end apart: 28, of which 11 were waited for; matrix products, arithmetic and copies ran while one was open for 1% of the time, Pallas kernels for 33%

profile of v1, /device:TPU:64, one launch (start us, length us, event | category | flops | bytes accessed | tf_op | source)
XLA Modules:
  0.0 1007.3 jit_solution(8188509837789326733)
XLA Ops:
  3.7 17.0 %all-gather = bf16[2,1,128,1024]{3,2,1,0:T(8,128)(2,1)S(1)} all-gather(bf16[2,1,128,128]{3,2,1,0:T(8,128)(2,1)S(1)} %slice.355), channel_id=2, replica_groups=mesh['x'=4,'h'=4,'y'=4,'l'=4,'c'=2] {'l','c'}, dimensions={3}, use_global_device_ids=true | all-gather | bytes 589824 | tf_op jit(solution)/shard_map/all_gather | solution.py:230
  27.3 5.4 all-to-all-start.204
  35.0 4.2 all-to-all-done.204
  39.3 14.3 %all_gather.10 = bf16[128,1024]{1,0:T(8,128)(2,1)S(1)} all-gather(bf16[128,128]{1,0:T(8,128)(2,1)S(1)} %fusion.41), channel_id=1, replica_groups=mesh['x'=4,'h'=4,'y'=4,'l'=4,'c'=2] {'l','c'}, dimensions={1}, use_global_device_ids=true | all-gather | bytes 294912 | tf_op jit(solution)/shard_map/all_gather | solution.py:172
  56.5 455.0 %conditional.6 = (f32[1024,384]{1,0:T(8,128)}, f32[1024,384]{1,0:T(8,128)}, f32[384,1024]{1,0:T(8,128)}) conditional(s32[]{:T(128)} %bitcast.291, (s32[2,2,16]{2,0,1:T(2,128)S(1)}, bf16[1024,384]{1,0:T(8,128)(2,1)S(1)}, s32[2,3,16]{2,1,0:T(4,128)S(1)}, bf16[1024,384]{1,0:T(8,128)(2,1)S(1)}, ...), branch_computations={%region_7.8_spmd, %region_8.9_spmd, %region_9.10_spmd, %region_10.... | conditional | flops 1179648 | bytes 61343420
  56.7 18.2 %all_to_all.832.chunks.own = bf16[16,64,384]{2,1,0:T(8,128)(2,1)} all-to-all(bf16[16,64,384]{2,1,0:T(8,128)(2,1)S(1)} %bitcast.739), channel_id=1, replica_groups=mesh['x'=4,'h'=4,'y'=4,'l'=4,'c'=2] {'x','y'}, dimensions={0} | all-to-all | bytes 1572864 | tf_op jit(solution)/shard_map/cond/branch_3_fun/all_to_all | solution.py:131
  74.9 17.3 %all_to_all.833.chunks.own = bf16[16,64,384]{2,1,0:T(8,128)(2,1)} all-to-all(bf16[16,64,384]{2,1,0:T(8,128)(2,1)S(1)} %bitcast.722), channel_id=1, replica_groups=mesh['x'=4,'h'=4,'y'=4,'l'=4,'c'=2] {'x','y'}, dimensions={0} | all-to-all | bytes 1572864 | tf_op jit(solution)/shard_map/cond/branch_3_fun/all_to_all | solution.py:131
  92.2 3.7 all-to-all-start.22
  96.5 28.8 %branch_3_fun.12 = (bf16[5,64,384]{2,1,0:T(8,128)(2,1)}, bf16[5,64,384]{2,1,0:T(8,128)(2,1)}, bf16[8,64,384]{2,1,0:T(8,128)(2,1)}) custom-call(s32[3,16]{1,0:T(4,128)} %slice_bitcast_fusion.6.index, bf16[16,64,384]{2,1,0:T(8,128)(2,1)} %all_to_all.833.chunks.own), custom_call_target="tpu_custom_call" | custom-call | bytes 1572864 | tf_op jit(solution)/shard_map/cond/branch_3_fun/pallas_call | solution.py:76
  125.2 13.2 %collective-permute-start.29 = (bf16[8,64,384]{2,1,0:T(8,128)(2,1)}, bf16[8,64,384]{2,1,0:T(8,128)(2,1)}, u32[]{:S(2)}, u32[]{:S(2)}) collective-permute-start(bf16[8,64,384]{2,1,0:T(8,128)(2,1)} %get-tuple-element.559), channel_id=1, source_target_pairs={{0,64},{32,96},{64,0},{96,32},{1,65},{33,97},{65,1},{97,33},{2,66}... | collective-permute-start | bytes 1179656 | tf_op jit(solution)/shard_map/cond/branch_3_fun/ppermute | solution.py:139
  140.5 7.8 collective-permute-start.28
  148.8 42.1 %collective-permute-done.27.ahead = bf16[5,64,384]{2,1,0:T(8,128)(2,1)S(1)} collective-permute-done((bf16[5,64,384]{2,1,0:T(8,128)(2,1)}, bf16[5,64,384]{2,1,0:T(8,128)(2,1)S(1)}, u32[]{:S(2)}, u32[]{:S(2)}) %collective-permute-start.27) | collective-permute-done | bytes 245792 | tf_op jit(solution)/shard_map/cond/branch_3_fun/ppermute | solution.py:138
  191.6 25.8 %branch_3_fun.13 = bf16[16,64,384]{2,1,0:T(8,128)(2,1)} custom-call(s32[2,16]{1,0:T(2,128)} %slice_bitcast_fusion.7.where, bf16[16,64,384]{2,1,0:T(8,128)(2,1)} %all_to_all.833.chunks.own, bf16[5,64,384]{2,1,0:T(8,128)(2,1)} %copy-done.150, bf16[5,64,384]{2,1,0:T(8,128)(2,1)} %collective-permute-done.28.behind, bf16[8,64,384]{2,1,0:T(8,128)(2,1)} %collective-permute-done.29.far), custom_call_target="tpu_custom_call" | custom-call | bytes 1572864 | tf_op jit(solution)/shard_map/cond/branch_3_fun/pallas_call | solution.py:109
  217.4 7.0 all-to-all-start.19
  224.4 28.8 %branch_3_fun.16 = (bf16[5,24,1024]{2,1,0:T(8,128)(2,1)}, bf16[5,24,1024]{2,1,0:T(8,128)(2,1)}, bf16[8,24,1024]{2,1,0:T(8,128)(2,1)}) custom-call(s32[3,16]{1,0:T(4,128)} %slice_bitcast_fusion.6.index, bf16[16,24,1024]{2,1,0:T(8,128)(2,1)} %copy-done.20), custom_call_target="tpu_custom_call" | custom-call | bytes 1572864 | tf_op jit(solution)/shard_map/cond/branch_3_fun/pallas_call | solution.py:76
  253.2 5.2 collective-permute-start.35
  258.4 9.8 collective-permute-start.33
  270.1 45.5 %collective-permute-done.33.ahead = bf16[5,24,1024]{2,1,0:T(8,128)(2,1)S(1)} collective-permute-done((bf16[5,24,1024]{2,1,0:T(8,128)(2,1)}, bf16[5,24,1024]{2,1,0:T(8,128)(2,1)S(1)}, u32[]{:S(2)}, u32[]{:S(2)}) %collective-permute-start.33) | collective-permute-done | bytes 245792 | tf_op jit(solution)/shard_map/cond/branch_3_fun/ppermute | solution.py:138
  317.2 25.8 %branch_3_fun.17 = bf16[16,24,1024]{2,1,0:T(8,128)(2,1)} custom-call(s32[2,16]{1,0:T(2,128)} %slice_bitcast_fusion.7.where, bf16[16,24,1024]{2,1,0:T(8,128)(2,1)} %copy-done.20, bf16[5,24,1024]{2,1,0:T(8,128)(2,1)} %copy-done.158, bf16[5,24,1024]{2,1,0:T(8,128)(2,1)} %copy-done.175, bf16[8,24,1024]{2,1,0:T(8,128)(2,1)} %copy-done.102), custom_call_target="tpu_custom_call" | custom-call | bytes 1572864 | tf_op jit(solution)/shard_map/cond/branch_3_fun/pallas_call | solution.py:109
  342.9 6.9 all-to-all-start.23
  349.9 28.8 %branch_3_fun.14 = (bf16[5,64,384]{2,1,0:T(8,128)(2,1)}, bf16[5,64,384]{2,1,0:T(8,128)(2,1)}, bf16[8,64,384]{2,1,0:T(8,128)(2,1)}) custom-call(s32[3,16]{1,0:T(4,128)} %slice_bitcast_fusion.6.index, bf16[16,64,384]{2,1,0:T(8,128)(2,1)} %all_to_all.832.chunks.own), custom_call_target="tpu_custom_call" | custom-call | bytes 1572864 | tf_op jit(solution)/shard_map/cond/branch_3_fun/pallas_call | solution.py:76
  378.6 6.5 collective-permute-start.32
  385.1 3.4 collective-permute-start.30
  388.5 6.6 collective-permute-start.31
  395.1 20.0 %collective-permute-done.30.ahead = bf16[5,64,384]{2,1,0:T(8,128)(2,1)S(1)} collective-permute-done((bf16[5,64,384]{2,1,0:T(8,128)(2,1)}, bf16[5,64,384]{2,1,0:T(8,128)(2,1)S(1)}, u32[]{:S(2)}, u32[]{:S(2)}) %collective-permute-start.30) | collective-permute-done | bytes 245792 | tf_op jit(solution)/shard_map/cond/branch_3_fun/ppermute | solution.py:138
  415.1 20.9 %collective-permute-done.31.behind = bf16[5,64,384]{2,1,0:T(8,128)(2,1)} collective-permute-done((bf16[5,64,384]{2,1,0:T(8,128)(2,1)}, bf16[5,64,384]{2,1,0:T(8,128)(2,1)}, u32[]{:S(2)}, u32[]{:S(2)}) %collective-permute-start.31) | collective-permute-done | bytes 245792 | tf_op jit(solution)/shard_map/cond/branch_3_fun/ppermute | solution.py:137
  436.0 25.8 %branch_3_fun.15 = bf16[16,64,384]{2,1,0:T(8,128)(2,1)} custom-call(s32[2,16]{1,0:T(2,128)} %slice_bitcast_fusion.7.where, bf16[16,64,384]{2,1,0:T(8,128)(2,1)} %all_to_all.832.chunks.own, bf16[5,64,384]{2,1,0:T(8,128)(2,1)} %copy-done.154, bf16[5,64,384]{2,1,0:T(8,128)(2,1)} %collective-permute-done.31.behind, bf16[8,64,384]{2,1,0:T(8,128)(2,1)} %collective-permute-done.32.far), custom_call_target="tpu_custom_call" | custom-call | bytes 1572864 | tf_op jit(solution)/shard_map/cond/branch_3_fun/pallas_call | solution.py:109
  461.7 7.0 all-to-all-start.21
  468.7 2.4 bitcast_convert_fusion.11
  472.5 10.9 %all-to-all-done.21 = bf16[16,64,384]{2,1,0:T(8,128)(2,1)} async-done(((bf16[16,64,384]{2,1,0:T(8,128)(2,1)}), bf16[16,64,384]{2,1,0:T(8,128)(2,1)}, u32[]{:S(2)}, u32[]{:S(2)}) %all-to-all-start.21) | async-done | bytes 786464 | tf_op jit(solution)/shard_map/cond/branch_3_fun/all_to_all | solution.py:144
  483.4 2.4 bitcast_convert_fusion.10
  511.5 2.3 fusion.20
  523.2 12.6 %all-to-all-start.205 = ((bf16[8,128,128]{2,1,0:T(8,128)(2,1)}), bf16[8,128,128]{2,1,0:T(8,128)(2,1)}, u32[]{:S(2)}, u32[]{:S(2)}) async-start(bf16[8,128,128]{2,1,0:T(8,128)(2,1)} %fusion.44), calls=%async_computation.205 | async-start | bytes 524288 | tf_op jit(solution)/shard_map/all_to_all | solution.py:167
  536.4 5.9 all-to-all-done.205
  544.1 14.4 %all_gather.11 = bf16[128,1024]{1,0:T(8,128)(2,1)S(1)} all-gather(bf16[128,128]{1,0:T(8,128)(2,1)S(1)} %fusion.40), channel_id=1, replica_groups=mesh['x'=4,'h'=4,'y'=4,'l'=4,'c'=2] {'l','c'}, dimensions={1}, use_global_device_ids=true | all-gather | bytes 294912 | tf_op jit(solution)/shard_map/all_gather | solution.py:172
  558.5 4.0 subtract_convert_fusion
  563.6 2.3 subtract_convert_fusion.1
  565.9 2.3 subtract_convert_fusion.2
  568.1 431.0 %conditional.7 = (f32[1024,384]{1,0:T(8,128)}, f32[1024,384]{1,0:T(8,128)S(1)}, f32[384,1024]{1,0:T(8,128)}) conditional(s32[]{:T(128)} %bitcast.305, (s32[2,2,16]{2,0,1:T(2,128)S(1)}, bf16[1024,384]{1,0:T(8,128)(2,1)}, s32[2,3,16]{2,1,0:T(4,128)S(1)}, bf16[1024,384]{1,0:T(8,128)(2,1)}, ...), branch_computations={%region_25.26_spmd, %region_26.27_spmd, %region_27.28_spmd, %regio... | conditional | flops 1179648 | bytes 64489176
  576.9 19.2 %all_to_all.877.chunks.own = bf16[16,64,384]{2,1,0:T(8,128)(2,1)} all-to-all(bf16[16,64,384]{2,1,0:T(8,128)(2,1)} %bitcast.212), channel_id=1, replica_groups=mesh['x'=4,'h'=4,'y'=4,'l'=4,'c'=2] {'x','y'}, dimensions={0} | all-to-all | bytes 1572864 | tf_op jit(solution)/shard_map/cond/branch_9_fun/all_to_all | solution.py:131
  596.1 17.9 %all_to_all.878.chunks.own = bf16[16,64,384]{2,1,0:T(8,128)(2,1)} all-to-all(bf16[16,64,384]{2,1,0:T(8,128)(2,1)} %bitcast.209), channel_id=1, replica_groups=mesh['x'=4,'h'=4,'y'=4,'l'=4,'c'=2] {'x','y'}, dimensions={0} | all-to-all | bytes 1572864 | tf_op jit(solution)/shard_map/cond/branch_9_fun/all_to_all | solution.py:131
  613.9 3.7 all-to-all-start.160
  618.2 30.3 %branch_9_fun.18 = (bf16[7,64,384]{2,1,0:T(8,128)(2,1)}, bf16[7,64,384]{2,1,0:T(8,128)(2,1)}, bf16[5,64,384]{2,1,0:T(8,128)(2,1)}) custom-call(s32[3,16]{1,0:T(4,128)} %slice_bitcast_fusion.52.index, bf16[16,64,384]{2,1,0:T(8,128)(2,1)} %all_to_all.878.chunks.own), custom_call_target="tpu_custom_call" | custom-call | bytes 1572864 | tf_op jit(solution)/shard_map/cond/branch_9_fun/pallas_call | solution.py:76
  650.4 7.8 collective-permute-start.235
  658.2 2.7 collective-permute-start.236
  661.5 42.8 %collective-permute-done.236.far = bf16[5,64,384]{2,1,0:T(8,128)(2,1)S(1)} collective-permute-done((bf16[5,64,384]{2,1,0:T(8,128)(2,1)}, bf16[5,64,384]{2,1,0:T(8,128)(2,1)S(1)}, u32[]{:S(2)}, u32[]{:S(2)}) %collective-permute-start.236) | collective-permute-done | bytes 245792 | tf_op jit(solution)/shard_map/cond/branch_9_fun/ppermute | solution.py:139
  705.8 25.8 %branch_9_fun.19 = bf16[16,64,384]{2,1,0:T(8,128)(2,1)} custom-call(s32[2,16]{1,0:T(2,128)} %slice_bitcast_fusion.53.where, bf16[16,64,384]{2,1,0:T(8,128)(2,1)} %all_to_all.878.chunks.own, bf16[7,64,384]{2,1,0:T(8,128)(2,1)} %copy-done.105, bf16[7,64,384]{2,1,0:T(8,128)(2,1)} %copy-done.112, bf16[5,64,384]{2,1,0:T(8,128)(2,1)} %copy-done.167), custom_call_target="tpu_custom_call" | custom-call | bytes 1572864 | tf_op jit(solution)/shard_map/cond/branch_9_fun/pallas_call | solution.py:109
  731.6 6.9 all-to-all-start.157
  738.6 30.3 %branch_9_fun.22 = (bf16[7,24,1024]{2,1,0:T(8,128)(2,1)}, bf16[7,24,1024]{2,1,0:T(8,128)(2,1)}, bf16[5,24,1024]{2,1,0:T(8,128)(2,1)}) custom-call(s32[3,16]{1,0:T(4,128)} %slice_bitcast_fusion.52.index, bf16[16,24,1024]{2,1,0:T(8,128)(2,1)} %copy-done.37), custom_call_target="tpu_custom_call" | custom-call | bytes 1572864 | tf_op jit(solution)/shard_map/cond/branch_9_fun/pallas_call | solution.py:76
  768.8 7.0 collective-permute-start.240
  775.9 4.2 collective-permute-start.241
  780.1 10.3 %collective-permute-start.242 = (bf16[5,24,1024]{2,1,0:T(8,128)(2,1)}, bf16[5,24,1024]{2,1,0:T(8,128)(2,1)S(1)}, u32[]{:S(2)}, u32[]{:S(2)}) collective-permute-start(bf16[5,24,1024]{2,1,0:T(8,128)(2,1)} %get-tuple-element.889), channel_id=1, source_target_pairs={{0,64},{32,96},{64,0},{96,32},{1,65},{33,97},{65,1},{97,33},{2,66}... | collective-permute-start | bytes 737288 | tf_op jit(solution)/shard_map/cond/branch_9_fun/ppermute | solution.py:139
  790.4 37.3 %collective-permute-done.242.far = bf16[5,24,1024]{2,1,0:T(8,128)(2,1)S(1)} collective-permute-done((bf16[5,24,1024]{2,1,0:T(8,128)(2,1)}, bf16[5,24,1024]{2,1,0:T(8,128)(2,1)S(1)}, u32[]{:S(2)}, u32[]{:S(2)}) %collective-permute-start.242) | collective-permute-done | bytes 245792 | tf_op jit(solution)/shard_map/cond/branch_9_fun/ppermute | solution.py:139
  829.3 25.8 %branch_9_fun.23 = bf16[16,24,1024]{2,1,0:T(8,128)(2,1)} custom-call(s32[2,16]{1,0:T(2,128)} %slice_bitcast_fusion.53.where, bf16[16,24,1024]{2,1,0:T(8,128)(2,1)} %copy-done.37, bf16[7,24,1024]{2,1,0:T(8,128)(2,1)} %copy-done.113, bf16[7,24,1024]{2,1,0:T(8,128)(2,1)} %copy-done.122, bf16[5,24,1024]{2,1,0:T(8,128)(2,1)} %copy-done.181), custom_call_target="tpu_custom_call" | custom-call | bytes 1572864 | tf_op jit(solution)/shard_map/cond/branch_9_fun/pallas_call | solution.py:109
  855.1 7.2 all-to-all-start.161
  862.3 30.3 %branch_9_fun.20 = (bf16[7,64,384]{2,1,0:T(8,128)(2,1)}, bf16[7,64,384]{2,1,0:T(8,128)(2,1)}, bf16[5,64,384]{2,1,0:T(8,128)(2,1)}) custom-call(s32[3,16]{1,0:T(4,128)} %slice_bitcast_fusion.52.index, bf16[16,64,384]{2,1,0:T(8,128)(2,1)} %all_to_all.877.chunks.own), custom_call_target="tpu_custom_call" | custom-call | bytes 1572864 | tf_op jit(solution)/shard_map/cond/branch_9_fun/pallas_call | solution.py:76
  894.5 7.8 collective-permute-start.238
  902.3 7.0 collective-permute-start.239
  909.3 23.0 %collective-permute-done.239.far = bf16[5,64,384]{2,1,0:T(8,128)(2,1)S(1)} collective-permute-done((bf16[5,64,384]{2,1,0:T(8,128)(2,1)}, bf16[5,64,384]{2,1,0:T(8,128)(2,1)S(1)}, u32[]{:S(2)}, u32[]{:S(2)}) %collective-permute-start.239) | collective-permute-done | bytes 245792 | tf_op jit(solution)/shard_map/cond/branch_9_fun/ppermute | solution.py:139
  933.0 25.8 %branch_9_fun.21 = bf16[16,64,384]{2,1,0:T(8,128)(2,1)} custom-call(s32[2,16]{1,0:T(2,128)} %slice_bitcast_fusion.53.where, bf16[16,64,384]{2,1,0:T(8,128)(2,1)} %all_to_all.877.chunks.own, bf16[7,64,384]{2,1,0:T(8,128)(2,1)} %collective-permute-done.237.ahead, bf16[7,64,384]{2,1,0:T(8,128)(2,1)} %collective-permute-done.238.behind, ...), custom_call_target="tpu_custom_call" | custom-call | bytes 1572864 | tf_op jit(solution)/shard_map/cond/branch_9_fun/pallas_call | solution.py:109
  958.8 7.0 all-to-all-start.159
  968.5 12.0 %all-to-all-done.159 = bf16[16,64,384]{2,1,0:T(8,128)(2,1)} async-done(((bf16[16,64,384]{2,1,0:T(8,128)(2,1)}), bf16[16,64,384]{2,1,0:T(8,128)(2,1)}, u32[]{:S(2)}, u32[]{:S(2)}) %all-to-all-start.159) | async-done | bytes 786464 | tf_op jit(solution)/shard_map/cond/branch_9_fun/all_to_all | solution.py:144
  999.2 3.4 fusion.29
  1002.6 3.0 fusion.31
  (178 shorter events, 49.2 us)
Async XLA Ops:
  0.6 1.5 copy-start
  0.6 20.0 %copy-start.44 = (bf16[1,1024,384]{2,1,0:T(8,128)(2,1)S(1)}, bf16[1,1024,384]{2,1,0:T(8,128)(2,1)}, u32[]{:S(2)}) copy-start(bf16[1,1024,384]{2,1,0:T(8,128)(2,1)} %param.41) | copy-start | bytes 2359300
  2.1 18.8 %copy-start.67 = (bf16[1,1024,384]{2,1,0:T(8,128)(2,1)S(1)}, bf16[1,1024,384]{2,1,0:T(8,128)(2,1)}, u32[]{:S(2)}) copy-start(bf16[1,1024,384]{2,1,0:T(8,128)(2,1)} %param.42) | copy-start | bytes 2359300
  3.6 35.6 %copy-start.70 = (bf16[2,2,128,128]{3,2,1,0:T(8,128)(2,1)}, bf16[2,2,128,128]{3,2,1,0:T(8,128)(2,1)S(1)}, u32[]{:S(2)}) copy-start(bf16[2,2,128,128]{3,2,1,0:T(8,128)(2,1)S(1)} %broadcast_select_fusion) | copy-start | bytes 393220
  20.6 1.3 copy-start.51
  20.6 1.3 copy-start.2
  22.0 10.8 %copy-start.223 = (s32[2,64]{1,0:T(2,128)S(1)}, s32[2,64]{1,0:T(2,128)}, u32[]{:S(2)}) copy-start(s32[2,64]{1,0:T(2,128)} %param.46) | copy-start | bytes 1540
  22.0 12.8 %copy-start.224 = (s32[3]{0:T(128)S(1)}, s32[3]{0:T(128)}, u32[]{:S(2)}) copy-start(s32[3]{0:T(128)} %constant.204.clone) | copy-start | bytes 40
  27.3 11.9 %all-to-all-start.204 = ((bf16[8,128,128]{2,1,0:T(8,128)(2,1)}), bf16[8,128,128]{2,1,0:T(8,128)(2,1)S(1)}, u32[]{:S(2)}, u32[]{:S(2)}) async-start(bf16[8,128,128]{2,1,0:T(8,128)(2,1)} %fusion.52), calls=%async_computation.204 | async-start | bytes 524288 | tf_op jit(solution)/shard_map/all_to_all | solution.py:167
  53.6 1.0 copy-start.52
  53.6 1.3 copy-start.68
  54.9 1.1 copy-start.45
  54.9 1.2 copy-start.225
  92.2 125.2 %all-to-all-start.22 = ((bf16[16,24,1024]{2,1,0:T(8,128)(2,1)S(1)}), bf16[16,24,1024]{2,1,0:T(8,128)(2,1)S(1)}, u32[]{:S(2)}, u32[]{:S(2)}) async-start(bf16[16,24,1024]{2,1,0:T(8,128)(2,1)S(1)} %bitcast.705), calls=%async_computation.22 | async-start | bytes 1572864 | tf_op jit(solution)/shard_map/cond/branch_3_fun/all_to_all | solution.py:131
  125.2 65.7 %collective-permute-start.29 = (bf16[8,64,384]{2,1,0:T(8,128)(2,1)}, bf16[8,64,384]{2,1,0:T(8,128)(2,1)}, u32[]{:S(2)}, u32[]{:S(2)}) collective-permute-start(bf16[8,64,384]{2,1,0:T(8,128)(2,1)} %get-tuple-element.559), channel_id=1, source_target_pairs={{0,64},{32,96},{64,0},{96,32},{1,65},{33,97},{65,1},{97,33},{2,66}... | collective-permute-start | bytes 1179656 | tf_op jit(solution)/shard_map/cond/branch_3_fun/ppermute | solution.py:139
  138.5 52.4 %collective-permute-start.27 = (bf16[5,64,384]{2,1,0:T(8,128)(2,1)}, bf16[5,64,384]{2,1,0:T(8,128)(2,1)S(1)}, u32[]{:S(2)}, u32[]{:S(2)}) collective-permute-start(bf16[5,64,384]{2,1,0:T(8,128)(2,1)} %get-tuple-element.557), channel_id=1, source_target_pairs={{0,96},{32,0},{64,32},{96,64},{1,97},{33,1},{65,33},{97,65},{2,98}... | collective-permute-start | bytes 737288 | tf_op jit(solution)/shard_map/cond/branch_3_fun/ppermute | solution.py:138
  140.5 50.5 %collective-permute-start.28 = (bf16[5,64,384]{2,1,0:T(8,128)(2,1)}, bf16[5,64,384]{2,1,0:T(8,128)(2,1)}, u32[]{:S(2)}, u32[]{:S(2)}) collective-permute-start(bf16[5,64,384]{2,1,0:T(8,128)(2,1)} %get-tuple-element.558), channel_id=1, source_target_pairs={{0,32},{32,64},{64,96},{96,0},{1,33},{33,65},{65,97},{97,1},{2,34}... | collective-permute-start | bytes 737288 | tf_op jit(solution)/shard_map/cond/branch_3_fun/ppermute | solution.py:137
  217.4 7.0 copy-start.20
  217.4 125.5 %all-to-all-start.19 = ((bf16[16,64,384]{2,1,0:T(8,128)(2,1)}), bf16[16,64,384]{2,1,0:T(8,128)(2,1)}, u32[]{:S(2)}, u32[]{:S(2)}) async-start(bf16[16,64,384]{2,1,0:T(8,128)(2,1)} %branch_3_fun.13), calls=%async_computation.19 | async-start | bytes 1572864 | tf_op jit(solution)/shard_map/cond/branch_3_fun/all_to_all | solution.py:144
  253.2 62.5 %collective-permute-start.35 = (bf16[8,24,1024]{2,1,0:T(8,128)(2,1)}, bf16[8,24,1024]{2,1,0:T(8,128)(2,1)S(1)}, u32[]{:S(2)}, u32[]{:S(2)}) collective-permute-start(bf16[8,24,1024]{2,1,0:T(8,128)(2,1)} %get-tuple-element.567), channel_id=1, source_target_pairs={{0,64},{32,96},{64,0},{96,32},{1,65},{33,97},{65,1},{97,33},{2,66}... | collective-permute-start | bytes 1179656 | tf_op jit(solution)/shard_map/cond/branch_3_fun/ppermute | solution.py:139
  258.4 57.3 %collective-permute-start.33 = (bf16[5,24,1024]{2,1,0:T(8,128)(2,1)}, bf16[5,24,1024]{2,1,0:T(8,128)(2,1)S(1)}, u32[]{:S(2)}, u32[]{:S(2)}) collective-permute-start(bf16[5,24,1024]{2,1,0:T(8,128)(2,1)} %get-tuple-element.565), channel_id=1, source_target_pairs={{0,96},{32,0},{64,32},{96,64},{1,97},{33,1},{65,33},{97,65},{2,98}... | collective-permute-start | bytes 737288 | tf_op jit(solution)/shard_map/cond/branch_3_fun/ppermute | solution.py:138
  268.2 47.5 %collective-permute-start.34 = (bf16[5,24,1024]{2,1,0:T(8,128)(2,1)}, bf16[5,24,1024]{2,1,0:T(8,128)(2,1)S(1)}, u32[]{:S(2)}, u32[]{:S(2)}) collective-permute-start(bf16[5,24,1024]{2,1,0:T(8,128)(2,1)} %get-tuple-element.566), channel_id=1, source_target_pairs={{0,32},{32,64},{64,96},{96,0},{1,33},{33,65},{65,97},{97,1},{2,34}... | collective-permute-start | bytes 737288 | tf_op jit(solution)/shard_map/cond/branch_3_fun/ppermute | solution.py:137
  342.9 118.8 %all-to-all-start.23 = ((bf16[16,24,1024]{2,1,0:T(8,128)(2,1)}), bf16[16,24,1024]{2,1,0:T(8,128)(2,1)S(1)}, u32[]{:S(2)}, u32[]{:S(2)}) async-start(bf16[16,24,1024]{2,1,0:T(8,128)(2,1)} %branch_3_fun.17), calls=%async_computation.23 | async-start | bytes 1572864 | tf_op jit(solution)/shard_map/cond/branch_3_fun/all_to_all | solution.py:144
  378.6 57.3 %collective-permute-start.32 = (bf16[8,64,384]{2,1,0:T(8,128)(2,1)}, bf16[8,64,384]{2,1,0:T(8,128)(2,1)}, u32[]{:S(2)}, u32[]{:S(2)}) collective-permute-start(bf16[8,64,384]{2,1,0:T(8,128)(2,1)} %get-tuple-element.563), channel_id=1, source_target_pairs={{0,64},{32,96},{64,0},{96,32},{1,65},{33,97},{65,1},{97,33},{2,66}... | collective-permute-start | bytes 1179656 | tf_op jit(solution)/shard_map/cond/branch_3_fun/ppermute | solution.py:139
  385.1 30.0 %collective-permute-start.30 = (bf16[5,64,384]{2,1,0:T(8,128)(2,1)}, bf16[5,64,384]{2,1,0:T(8,128)(2,1)S(1)}, u32[]{:S(2)}, u32[]{:S(2)}) collective-permute-start(bf16[5,64,384]{2,1,0:T(8,128)(2,1)} %get-tuple-element.561), channel_id=1, source_target_pairs={{0,96},{32,0},{64,32},{96,64},{1,97},{33,1},{65,33},{97,65},{2,98}... | collective-permute-start | bytes 737288 | tf_op jit(solution)/shard_map/cond/branch_3_fun/ppermute | solution.py:138
  388.5 47.4 %collective-permute-start.31 = (bf16[5,64,384]{2,1,0:T(8,128)(2,1)}, bf16[5,64,384]{2,1,0:T(8,128)(2,1)}, u32[]{:S(2)}, u32[]{:S(2)}) collective-permute-start(bf16[5,64,384]{2,1,0:T(8,128)(2,1)} %get-tuple-element.562), channel_id=1, source_target_pairs={{0,32},{32,64},{64,96},{96,0},{1,33},{33,65},{65,97},{97,1},{2,34}... | collective-permute-start | bytes 737288 | tf_op jit(solution)/shard_map/cond/branch_3_fun/ppermute | solution.py:137
  415.1 20.9 %copy-start.154 = (bf16[5,64,384]{2,1,0:T(8,128)(2,1)}, bf16[5,64,384]{2,1,0:T(8,128)(2,1)S(1)}, u32[]{:S(2)}) copy-start(bf16[5,64,384]{2,1,0:T(8,128)(2,1)S(1)} %collective-permute-done.30.ahead) | copy-start | bytes 737284 | tf_op jit(solution)/shard_map/conditional.2
  461.7 21.7 %all-to-all-start.21 = ((bf16[16,64,384]{2,1,0:T(8,128)(2,1)}), bf16[16,64,384]{2,1,0:T(8,128)(2,1)}, u32[]{:S(2)}, u32[]{:S(2)}) async-start(bf16[16,64,384]{2,1,0:T(8,128)(2,1)} %branch_3_fun.15), calls=%async_computation.21 | async-start | bytes 1572864 | tf_op jit(solution)/shard_map/cond/branch_3_fun/all_to_all | solution.py:144
  511.5 2.3 copy-start.3
  511.5 2.6 copy-start.5
  511.5 2.8 copy-start.46
  514.3 2.3 copy-start.53
  516.5 1.3 copy-start.7
  516.5 1.3 copy-start.48
  523.2 19.1 %all-to-all-start.205 = ((bf16[8,128,128]{2,1,0:T(8,128)(2,1)}), bf16[8,128,128]{2,1,0:T(8,128)(2,1)}, u32[]{:S(2)}, u32[]{:S(2)}) async-start(bf16[8,128,128]{2,1,0:T(8,128)(2,1)} %fusion.44), calls=%async_computation.205 | async-start | bytes 524288 | tf_op jit(solution)/shard_map/all_to_all | solution.py:167
  558.5 4.3 copy-start.6
  558.5 4.4 copy-start.54
  558.5 4.4 copy-start.69
  562.4 1.1 copy-start.49
  563.6 2.3 copy-start.4
  563.6 2.3 copy-start.8
  563.6 2.3 copy-start.47
  563.6 2.3 copy-start.198
  613.9 117.7 %all-to-all-start.160 = ((bf16[16,24,1024]{2,1,0:T(8,128)(2,1)}), bf16[16,24,1024]{2,1,0:T(8,128)(2,1)S(1)}, u32[]{:S(2)}, u32[]{:S(2)}) async-start(bf16[16,24,1024]{2,1,0:T(8,128)(2,1)} %bitcast.214), calls=%async_computation.160 | async-start | bytes 1572864 | tf_op jit(solution)/shard_map/cond/branch_9_fun/all_to_all | solution.py:131
  648.4 55.8 %collective-permute-start.234 = (bf16[7,64,384]{2,1,0:T(8,128)(2,1)}, bf16[7,64,384]{2,1,0:T(8,128)(2,1)S(1)}, u32[]{:S(2)}, u32[]{:S(2)}) collective-permute-start(bf16[7,64,384]{2,1,0:T(8,128)(2,1)} %get-tuple-element.879), channel_id=1, source_target_pairs={{0,96},{32,0},{64,32},{96,64},{1,97},{33,1},{65,33},{97,65},{2,98}... | collective-permute-start | bytes 1032200 | tf_op jit(solution)/shard_map/cond/branch_9_fun/ppermute | solution.py:138
  650.4 53.9 %collective-permute-start.235 = (bf16[7,64,384]{2,1,0:T(8,128)(2,1)}, bf16[7,64,384]{2,1,0:T(8,128)(2,1)S(1)}, u32[]{:S(2)}, u32[]{:S(2)}) collective-permute-start(bf16[7,64,384]{2,1,0:T(8,128)(2,1)} %get-tuple-element.880), channel_id=1, source_target_pairs={{0,32},{32,64},{64,96},{96,0},{1,33},{33,65},{65,97},{97,1},{2,34}... | collective-permute-start | bytes 1032200 | tf_op jit(solution)/shard_map/cond/branch_9_fun/ppermute | solution.py:137
  658.2 46.1 %collective-permute-start.236 = (bf16[5,64,384]{2,1,0:T(8,128)(2,1)}, bf16[5,64,384]{2,1,0:T(8,128)(2,1)S(1)}, u32[]{:S(2)}, u32[]{:S(2)}) collective-permute-start(bf16[5,64,384]{2,1,0:T(8,128)(2,1)} %get-tuple-element.881), channel_id=1, source_target_pairs={{0,64},{32,96},{64,0},{96,32},{1,65},{33,97},{65,1},{97,33},{2,66}... | collective-permute-start | bytes 737288 | tf_op jit(solution)/shard_map/cond/branch_9_fun/ppermute | solution.py:139
  731.6 7.0 copy-start.37
  731.6 123.4 %all-to-all-start.157 = ((bf16[16,64,384]{2,1,0:T(8,128)(2,1)}), bf16[16,64,384]{2,1,0:T(8,128)(2,1)S(1)}, u32[]{:S(2)}, u32[]{:S(2)}) async-start(bf16[16,64,384]{2,1,0:T(8,128)(2,1)} %branch_9_fun.19), calls=%async_computation.157 | async-start | bytes 1572864 | tf_op jit(solution)/shard_map/cond/branch_9_fun/all_to_all | solution.py:144
  768.8 58.8 %collective-permute-start.240 = (bf16[7,24,1024]{2,1,0:T(8,128)(2,1)}, bf16[7,24,1024]{2,1,0:T(8,128)(2,1)S(1)}, u32[]{:S(2)}, u32[]{:S(2)}) collective-permute-start(bf16[7,24,1024]{2,1,0:T(8,128)(2,1)} %get-tuple-element.887), channel_id=1, source_target_pairs={{0,96},{32,0},{64,32},{96,64},{1,97},{33,1},{65,33},{97,65},{2,98}... | collective-permute-start | bytes 1032200 | tf_op jit(solution)/shard_map/cond/branch_9_fun/ppermute | solution.py:138
  775.9 51.8 %collective-permute-start.241 = (bf16[7,24,1024]{2,1,0:T(8,128)(2,1)}, bf16[7,24,1024]{2,1,0:T(8,128)(2,1)S(1)}, u32[]{:S(2)}, u32[]{:S(2)}) collective-permute-start(bf16[7,24,1024]{2,1,0:T(8,128)(2,1)} %get-tuple-element.888), channel_id=1, source_target_pairs={{0,32},{32,64},{64,96},{96,0},{1,33},{33,65},{65,97},{97,1},{2,34}... | collective-permute-start | bytes 1032200 | tf_op jit(solution)/shard_map/cond/branch_9_fun/ppermute | solution.py:137
  780.1 47.6 %collective-permute-start.242 = (bf16[5,24,1024]{2,1,0:T(8,128)(2,1)}, bf16[5,24,1024]{2,1,0:T(8,128)(2,1)S(1)}, u32[]{:S(2)}, u32[]{:S(2)}) collective-permute-start(bf16[5,24,1024]{2,1,0:T(8,128)(2,1)} %get-tuple-element.889), channel_id=1, source_target_pairs={{0,64},{32,96},{64,0},{96,32},{1,65},{33,97},{65,1},{97,33},{2,66}... | collective-permute-start | bytes 737288 | tf_op jit(solution)/shard_map/cond/branch_9_fun/ppermute | solution.py:139
  827.7 0.9 copy-start.113
  855.1 103.7 %all-to-all-start.161 = ((bf16[16,24,1024]{2,1,0:T(8,128)(2,1)}), bf16[16,24,1024]{2,1,0:T(8,128)(2,1)S(1)}, u32[]{:S(2)}, u32[]{:S(2)}) async-start(bf16[16,24,1024]{2,1,0:T(8,128)(2,1)} %branch_9_fun.23), calls=%async_computation.161 | async-start | bytes 1572864 | tf_op jit(solution)/shard_map/cond/branch_9_fun/all_to_all | solution.py:144
  892.6 39.7 %collective-permute-start.237 = (bf16[7,64,384]{2,1,0:T(8,128)(2,1)}, bf16[7,64,384]{2,1,0:T(8,128)(2,1)}, u32[]{:S(2)}, u32[]{:S(2)}) collective-permute-start(bf16[7,64,384]{2,1,0:T(8,128)(2,1)} %get-tuple-element.883), channel_id=1, source_target_pairs={{0,96},{32,0},{64,32},{96,64},{1,97},{33,1},{65,33},{97,65},{2,98}... | collective-permute-start | bytes 1032200 | tf_op jit(solution)/shard_map/cond/branch_9_fun/ppermute | solution.py:138
  894.5 37.8 %collective-permute-start.238 = (bf16[7,64,384]{2,1,0:T(8,128)(2,1)}, bf16[7,64,384]{2,1,0:T(8,128)(2,1)}, u32[]{:S(2)}, u32[]{:S(2)}) collective-permute-start(bf16[7,64,384]{2,1,0:T(8,128)(2,1)} %get-tuple-element.884), channel_id=1, source_target_pairs={{0,32},{32,64},{64,96},{96,0},{1,33},{33,65},{65,97},{97,1},{2,34}... | collective-permute-start | bytes 1032200 | tf_op jit(solution)/shard_map/cond/branch_9_fun/ppermute | solution.py:137
  902.3 30.0 %collective-permute-start.239 = (bf16[5,64,384]{2,1,0:T(8,128)(2,1)}, bf16[5,64,384]{2,1,0:T(8,128)(2,1)S(1)}, u32[]{:S(2)}, u32[]{:S(2)}) collective-permute-start(bf16[5,64,384]{2,1,0:T(8,128)(2,1)} %get-tuple-element.885), channel_id=1, source_target_pairs={{0,64},{32,96},{64,0},{96,32},{1,65},{33,97},{65,1},{97,33},{2,66}... | collective-permute-start | bytes 737288 | tf_op jit(solution)/shard_map/cond/branch_9_fun/ppermute | solution.py:139
  958.8 21.7 %all-to-all-start.159 = ((bf16[16,64,384]{2,1,0:T(8,128)(2,1)}), bf16[16,64,384]{2,1,0:T(8,128)(2,1)}, u32[]{:S(2)}, u32[]{:S(2)}) async-start(bf16[16,64,384]{2,1,0:T(8,128)(2,1)} %branch_9_fun.21), calls=%async_computation.159 | async-start | bytes 1572864 | tf_op jit(solution)/shard_map/cond/branch_9_fun/all_to_all | solution.py:144
  999.2 3.5 copy-start.55
  999.2 3.4 copy-start.56
  1002.6 3.0 copy-start.50
  1002.6 3.0 copy-start.65
  1002.6 3.0 copy-start.66
  1005.6 1.4 copy-start.1
  (10 other events, 7.3 us)

commit v2 on v1

v2 whole, which is shorter than its diff:
```python
import functools

import jax
import jax.numpy as jnp
from jax import lax
from jax.experimental import pallas as pl
from jax.experimental.pallas import tpu as pltpu
from jax.sharding import Mesh, PartitionSpec as P

D = 1024
FF = 3072
HID = 384
REPLICAS = 64
N_TENSOR = 8
COLS = D // N_TENSOR
PLANE = 16
PLANES = 4
ROUNDS = 2
IN_SCALE = D**-0.5
HID_SCALE = FF**-0.5

inner_rate = 1.0
outer_rate = 0.5
momentum_rate = 0.9

REPLICA = ("x", "h", "y")
FLAT = ("x", "y")
TENSOR = ("l", "c")

NEXT = 6
FAR = 6
MORE = 2
VMEM = 48 << 20


def routes(partners):
    me = lax.axis_index("h")
    ids = jnp.arange(REPLICAS, dtype=jnp.int32)
    plane = (ids // 4) % PLANES
    flat = (ids // PLANE) * 4 + ids % 4
    to_plane = (partners // 4) % PLANES
    off = (to_plane - plane + PLANES) % PLANES
    same = (plane[:, None] == plane[None, :]) & (flat[None, :] < flat[:, None])
    rank = jnp.sum((same & (off[:, :, None] == off[:, None, :])).astype(jnp.int32), axis=2)
    places = jnp.arange(PLANE, dtype=jnp.int32)
    slots = jnp.arange(PLANE + 2 * MORE, dtype=jnp.int32)
    offs = jnp.array([1, 3, 2], jnp.int32)
    here = (plane == me)[None, None, None, :]
    sends = here & (off[:, None, None, :] == offs[None, :, None, None])
    sends = sends & (rank[:, None, None, :] == slots[None, None, :, None])
    send_index = jnp.sum(jnp.where(sends, flat, 0), axis=3)
    home = (places // 4) * PLANE + me * 4 + places % 4
    wanted = partners[:, None, :] == home[None, :, None]
    come_from = (plane[None, :] - me + PLANES) % PLANES
    kind = jnp.sum(jnp.where(wanted, come_from[:, None, :], 0), axis=2)
    place = jnp.where(off == 0, flat[None, :], rank)
    slot = jnp.sum(jnp.where(wanted, place[:, None, :], 0), axis=2)
    extra = jnp.where(off == 2, rank + 1 - FAR, jnp.where(off == 0, 0, rank + 1 - NEXT))
    trips = jnp.maximum((jnp.max(extra, axis=1) + MORE - 1) // MORE, 0)
    where = jnp.stack([kind, slot], axis=1)
    return [(send_index[r], where[r], trips[r]) for r in range(ROUNDS)]


def kernel_call(kernel, out_shape, index_args, args, name):
    scalars = [pl.BlockSpec(memory_space=pltpu.SMEM)] * len(index_args)
    whole = pl.BlockSpec(memory_space=pltpu.VMEM)
    size = sum(a.size * a.dtype.itemsize for a in (*args, *out_shape))
    return pl.pallas_call(
        kernel,
        out_shape=out_shape,
        in_specs=scalars + [whole] * len(args),
        out_specs=(whole,) * len(out_shape),
        compiler_params=pltpu.CompilerParams(vmem_limit_bytes=VMEM),
        cost_estimate=pl.CostEstimate(flops=size, bytes_accessed=size, transcendentals=0),
        name=name,
    )(*index_args, *args)


def pick_kernel(index, chunks, *outs):
    for o, out in enumerate(outs):

        @pl.loop(0, out.shape[0])
        def _(k, o=o, out=out):
            out[k] = chunks[index[o, k]]


def pick(index, chunks, counts):
    out_shape = tuple(jax.ShapeDtypeStruct((n, *chunks.shape[1:]), chunks.dtype) for n in counts)
    return kernel_call(pick_kernel, out_shape, (index,), (chunks,), "pick")


def merge_kernel(fn, first, n_own, n_out, where, low, *refs):
    ahead, behind, far, own = refs[:3] + (refs[3:],)
    own, before, outs = own[:n_own], own[n_own:-n_out], own[-n_out:]

    @pl.loop(0, PLANE)
    def _(d):
        kind, slot = where[0, d], where[1, d]

        def use(theirs):
            for out, value in zip(outs, fn(theirs, *(o[d] for o in own))):
                out[d] = value.astype(out.dtype)

        if not first:
            for out, old in zip(outs, before):
                out[d] = old[d]
        else:

            @pl.when(kind == 0)
            def _():
                use(own[0][slot])

        for number, source in ((1, ahead), (2, far), (3, behind)):
            at = slot - low[number // 2 % 2 if number < 3 else 0]

            @pl.when((kind == number) & (at >= 0) & (at < source.shape[0]))
            def _(source=source, at=at):
                use(source[at])


def merge(fn, where, low, arrived, own, outs, before=()):
    kernel = functools.partial(merge_kernel, fn, not before, len(own), outs)
    out_shape = (jax.ShapeDtypeStruct(own[0].shape, own[0].dtype),) * outs
    return kernel_call(kernel, out_shape, (where, low), (*arrived, *own, *before), "merge")


def step_by(n):
    return [(i, (i + n) % PLANES) for i in range(PLANES)]


def hop(index, chunks, n_next, n_far):
    up, down, across = pick(index, chunks, (n_next, n_next, n_far))
    from_far = lax.ppermute(across, "h", step_by(2))
    from_behind = lax.ppermute(up, "h", step_by(1))
    from_ahead = lax.ppermute(down, "h", step_by(-1))
    return from_ahead, from_behind, from_far


def depart(route, chunks):
    return hop(route[0], chunks, NEXT, FAR)


def arrive(route, fn, outs, arrived, own):
    send_index, where, trips = route
    low = jnp.array([NEXT, FAR], jnp.int32)
    done = [merge(fn, where, 0 * low, a, o, outs) for a, o in zip(arrived, own)]

    def late(state):
        i, done = state
        at = low + MORE * i
        index = jnp.stack(
            [lax.dynamic_slice(send_index[o], (at[o // 2],), (MORE,)) for o in range(3)]
        )
        done = [
            merge(fn, where, at, hop(index, o[0], MORE, MORE), o, outs, before=b)
            for o, b in zip(own, done)
        ]
        return i + 1, done

    return lax.while_loop(lambda s: s[0] < trips, late, (jnp.int32(0), done))[1]


def over_plane(chunks):
    return lax.all_to_all(chunks, FLAT, 0, 0, tiled=True)


def spread(a):
    return over_plane(a.reshape(PLANE, a.shape[0] // PLANE, a.shape[1]))


def back_home(chunks):
    return over_plane(chunks).reshape(-1, chunks.shape[-1])


rows = (((0,), (0,)), ((), ()))


def grad(a, b):
    return lax.dot_general(a, b, rows, preferred_element_type=jnp.float32)


def local_step(both, down, inputs, in_cols, out_cols):
    pre = jnp.dot(inputs, both, preferred_element_type=jnp.float32) * IN_SCALE
    gate_pre, up_value = pre[:, :HID], pre[:, HID:]
    sigmoid_gate = jax.nn.sigmoid(gate_pre)
    active = gate_pre * sigmoid_gate
    hidden = (active * up_value).astype(jnp.bfloat16)
    term = jnp.dot(hidden, down, preferred_element_type=jnp.float32) * HID_SCALE
    term = term.astype(jnp.bfloat16)
    blocks = term.reshape(-1, N_TENSOR, COLS).transpose(1, 0, 2)
    terms = lax.all_to_all(blocks, TENSOR, 0, 0, tiled=True)
    branch = jnp.sum(terms.astype(jnp.float32), axis=0)
    error_cols = (in_cols.astype(jnp.float32) + branch - out_cols.astype(jnp.float32)).astype(
        jnp.bfloat16
    )
    errors = lax.all_gather(error_cols, TENSOR, axis=1, tiled=True)
    back = (
        lax.dot_general(errors, down, (((1,), (1,)), ((), ())), preferred_element_type=jnp.float32)
        * HID_SCALE
    )
    delta_gate = back * up_value * sigmoid_gate * (1.0 + gate_pre * (1.0 - sigmoid_gate))
    delta_up = back * active
    deltas = jnp.concatenate([delta_gate, delta_up], axis=1).astype(jnp.bfloat16)
    return deltas, hidden, errors, error_cols


def outer_update(theirs, stepped, weight):
    weight = weight.astype(jnp.float32)
    pair_mean = 0.5 * (stepped.astype(jnp.float32) + theirs.astype(jnp.float32))
    outer_grad = weight - pair_mean
    moment = outer_grad.astype(jnp.bfloat16).astype(jnp.float32)
    updated = weight - outer_rate * (momentum_rate * outer_grad + outer_grad)
    updated = updated.astype(jnp.bfloat16)
    return updated, 0.475 * updated.astype(jnp.float32) - 0.2025 * moment


def pair_sum(theirs, own):
    return (theirs.astype(jnp.float32) + own.astype(jnp.float32),)


def partners_own(theirs, own):
    return (theirs,)


def body(w_gate, w_up, w_down, pool, rows_index, partners):
    both = jnp.concatenate([w_gate[0], w_up[0]], axis=1)
    down = w_down[0]
    first, last = routes(partners)
    picked = jnp.take(pool[0], rows_index[0].reshape(-1), axis=0)
    picked = picked.reshape(ROUNDS, 2, -1, COLS)
    in_cols, out_cols = picked[:, 0], picked[:, 1]
    inputs = lax.all_gather(in_cols, TENSOR, axis=2, tiled=True)
    start = [spread(both), spread(down)]

    deltas, hidden, errors, _ = local_step(both, down, inputs[0], in_cols[0], out_cols[0])
    step_down = (down.astype(jnp.float32) - HID_SCALE * grad(hidden, errors)).astype(jnp.bfloat16)
    step_both = (both.astype(jnp.float32) - IN_SCALE * grad(inputs[0], deltas)).astype(jnp.bfloat16)
    stepped = [spread(step_both), spread(step_down)]
    arrived = [depart(first, s) for s in stepped]
    done = arrive(first, outer_update, 2, arrived, list(zip(stepped, start)))

    shares = [share for _, share in done]
    arrived = [depart(last, s) for s in shares]
    both, down = (back_home(new) for new, _ in done)
    deltas, hidden, errors, error_cols = local_step(
        both, down, inputs[1], in_cols[1], out_cols[1]
    )
    factors = jnp.concatenate([deltas, hidden, error_cols, in_cols[1]], axis=1)
    arrived, factors = lax.optimization_barrier((arrived, factors))
    factors = spread(factors)
    on_way = depart(last, factors)
    sums = arrive(last, pair_sum, 1, arrived, [(s,) for s in shares])
    sum_both, sum_down = (back_home(s[0]) for s in sums)
    theirs = back_home(arrive(last, partners_own, 1, [on_way], [(factors,)])[0][0])
    cols = theirs[:, 3 * HID :].reshape(-1, 2, COLS).transpose(1, 0, 2)
    cols = lax.all_gather(cols, TENSOR, axis=2, tiled=True)

    def pair(mine, other):
        return jnp.concatenate([mine, other], axis=0)

    deltas = pair(deltas, theirs[:, : 2 * HID])
    hidden = pair(hidden, theirs[:, 2 * HID : 3 * HID])
    errors = pair(errors, cols[0])
    inputs = pair(inputs[1], cols[1])

    def final(weight, known, a, b, scale):
        new = 0.05 * weight.astype(jnp.float32) + known.astype(jnp.float32)
        return (new - (0.475 * inner_rate * scale) * grad(a, b)).astype(jnp.bfloat16)[None]

    return (
        final(both[:, :HID], sum_both[:, :HID], inputs, deltas[:, :HID], IN_SCALE),
        final(both[:, HID:], sum_both[:, HID:], inputs, deltas[:, HID:], IN_SCALE),
        final(down, sum_down, hidden, errors, HID_SCALE),
    )


def solution(mesh):
    grid = Mesh(mesh.devices.reshape(4, 4, 4, 4, 2), ("x", "h", "y", "l", "c"))
    return jax.shard_map(
        body,
        mesh=grid,
        in_specs=(
            P(REPLICA, None, TENSOR),
            P(REPLICA, None, TENSOR),
            P(REPLICA, TENSOR, None),
            P(REPLICA, None, TENSOR),
            P(REPLICA, None, None, None),
            P(),
        ),
        out_specs=(
            P(REPLICA, None, TENSOR),
            P(REPLICA, None, TENSOR),
            P(REPLICA, TENSOR, None),
        ),
        check_vma=False,
    )
```

time: 1020 us -> 745 us (0.73)
  the two profiles are of different devices: /device:TPU:64 before, /device:TPU:1 now
where the time goes in v2:
time: 745 us; the launch traced here: 742 us
  waiting for transfers between devices  235 us (32%)
  blocking collectives  229 us (31%)
  starting transfers between devices  193 us (26%)
  Pallas kernels  39.3 us (5%)
  matrix products  18.6 us (2%)
  local copies, waits for them, and re-layouts  10.8 us (1%)
  other arithmetic  9.69 us (1%)
    all_gather x2, blocking collectives, local_step(): errors = lax.all_gather(error_cols, TENSOR, axis=1, tiled=True)  132 us
    ppermute x8, waiting for transfers between devices, hop(): from_ahead = lax.ppermute(down, 'h', step_by(-1))  101 us
    ppermute x8, waiting for transfers between devices, hop(): from_far = lax.ppermute(across, 'h', step_by(2))  58.8 us
    ppermute x8, starting transfers between devices, hop(): from_far = lax.ppermute(across, 'h', step_by(2))  55 us
    ppermute x8, starting transfers between devices, hop(): from_ahead = lax.ppermute(down, 'h', step_by(-1))  53.8 us
    all_to_all x2, blocking collectives, over_plane(): return lax.all_to_all(chunks, FLAT, 0, 0, tiled=True)  49.6 us
    all_to_all x8, waiting for transfers between devices, over_plane(): return lax.all_to_all(chunks, FLAT, 0, 0, tiled=True)  39.8 us
    ppermute x8, starting transfers between devices, hop(): from_behind = lax.ppermute(up, 'h', step_by(1))  39.6 us
  transfers between devices with their start and end apart: 33, of which 12 were waited for; matrix products, arithmetic and copies ran while one was open for 3% of the time, Pallas kernels for 4%

profile of v2, /device:TPU:1, one launch (start us, length us, event | category | flops | bytes accessed | tf_op | source)
XLA Modules:
  0.0 741.6 jit_solution(2474972639452260545)
XLA Ops:
  3.7 20.7 %all-gather = bf16[2,1,128,1024]{3,2,1,0:T(8,128)(2,1)S(1)} all-gather(bf16[2,1,128,128]{3,2,1,0:T(8,128)(2,1)S(1)} %slice.209), channel_id=2, replica_groups=mesh['x'=4,'h'=4,'y'=4,'l'=4,'c'=2] {'l','c'}, dimensions={3}, use_global_device_ids=true | all-gather | bytes 589824 | tf_op jit(solution)/shard_map/all_gather | solution.py:232
  26.5 11.3 %all_to_all.60 = bf16[8,128,128]{2,1,0:T(8,128)(2,1)S(1)} all-to-all(bf16[8,128,128]{2,1,0:T(8,128)(2,1)S(1)} %bitcast.110), channel_id=1, replica_groups=mesh['x'=4,'h'=4,'y'=4,'l'=4,'c'=2] {'l','c'}, dimensions={0} | all-to-all | bytes 524288 | tf_op jit(solution)/shard_map/all_to_all | solution.py:191
  37.8 3.6 all-to-all-start.4
  41.5 14.0 %all_gather.13 = bf16[128,1024]{1,0:T(8,128)(2,1)S(1)} all-gather(bf16[128,128]{1,0:T(8,128)(2,1)S(1)} %fusion.25), channel_id=1, replica_groups=mesh['x'=4,'h'=4,'y'=4,'l'=4,'c'=2] {'l','c'}, dimensions={1}, use_global_device_ids=true | all-gather | bytes 294912 | tf_op jit(solution)/shard_map/all_gather | solution.py:196
  55.4 2.4 subtract_convert_fusion.3
  57.8 6.9 all-to-all-start.3
  68.3 9.1 %all-to-all-done.3.chunks.refs_3_ = bf16[16,24,1024]{2,1,0:T(8,128)(2,1)S(1)} async-done(((bf16[16,24,1024]{2,1,0:T(8,128)(2,1)}), bf16[16,24,1024]{2,1,0:T(8,128)(2,1)S(1)}, u32[]{:S(2)}, u32[]{:S(2)}) %all-to-all-start.3) | async-done | bytes 786464 | tf_op jit(solution)/shard_map/all_to_all | solution.py:164
  77.4 4.7 all-to-all-start.1
  82.2 2.5 pad_maximum_fusion.1
  84.8 17.7 %all-to-all-done.1.chunks.refs_3_ = bf16[16,64,768]{2,1,0:T(8,128)(2,1)S(1)} async-done(((bf16[16,64,768]{2,1,0:T(8,128)(2,1)}), bf16[16,64,768]{2,1,0:T(8,128)(2,1)S(1)}, u32[]{:S(2)}, u32[]{:S(2)}) %all-to-all-start.1) | async-done | bytes 1572896 | tf_op jit(solution)/shard_map/all_to_all | solution.py:164
  103.6 4.6 all-to-all-start.2
  111.4 10.4 %collective-permute-start.18 = (bf16[6,24,1024]{2,1,0:T(8,128)(2,1)}, bf16[6,24,1024]{2,1,0:T(8,128)(2,1)S(1)}, u32[]{:S(2)}, u32[]{:S(2)}) collective-permute-start(bf16[6,24,1024]{2,1,0:T(8,128)(2,1)} %get-tuple-element.211), channel_id=1, source_target_pairs={{0,96},{32,0},{64,32},{96,64},{1,97},{33,1},{65,33},{97,65},{2,98}... | collective-permute-start | bytes 884744 | tf_op jit(solution)/shard_map/ppermute | solution.py:135
  121.8 2.5 pick.10
  124.3 5.2 collective-permute-start.15
  129.5 4.0 collective-permute-start.16
  133.5 5.4 collective-permute-start.17
  139.2 6.8 collective-permute-start.19
  145.9 93.1 %collective-permute-done.18.refs_0_ = bf16[6,24,1024]{2,1,0:T(8,128)(2,1)S(1)} collective-permute-done((bf16[6,24,1024]{2,1,0:T(8,128)(2,1)}, bf16[6,24,1024]{2,1,0:T(8,128)(2,1)S(1)}, u32[]{:S(2)}, u32[]{:S(2)}) %collective-permute-start.18) | collective-permute-done | bytes 294944 | tf_op jit(solution)/shard_map/ppermute | solution.py:135
  239.0 8.4 %collective-permute-start.20 = (bf16[6,24,1024]{2,1,0:T(8,128)(2,1)}, bf16[6,24,1024]{2,1,0:T(8,128)(2,1)S(1)}, u32[]{:S(2)}, u32[]{:S(2)}) collective-permute-start(bf16[6,24,1024]{2,1,0:T(8,128)(2,1)} %copy-done.5), channel_id=1, source_target_pairs={{0,64},{32,96},{64,0},{96,32},{1,65},{33,97},{65,1},{97,33},{2,66}... | collective-permute-start | bytes 884744 | tf_op jit(solution)/shard_map/ppermute | solution.py:133
  248.2 34.6 %collective-permute-done.20.refs_2_ = bf16[6,24,1024]{2,1,0:T(8,128)(2,1)S(1)} collective-permute-done((bf16[6,24,1024]{2,1,0:T(8,128)(2,1)}, bf16[6,24,1024]{2,1,0:T(8,128)(2,1)S(1)}, u32[]{:S(2)}, u32[]{:S(2)}) %collective-permute-start.20) | collective-permute-done | bytes 294944 | tf_op jit(solution)/shard_map/ppermute | solution.py:133
  282.8 4.2 merge.11
  287.0 6.1 merge.10
  293.7 28.2 %all_to_all.61 = bf16[16,64,768]{2,1,0:T(8,128)(2,1)S(1)} all-to-all(bf16[16,64,768]{2,1,0:T(8,128)(2,1)} %get-tuple-element.216), channel_id=1, replica_groups=mesh['x'=4,'h'=4,'y'=4,'l'=4,'c'=2] {'x','y'}, dimensions={0} | all-to-all | bytes 3145728 | tf_op jit(solution)/shard_map/all_to_all | solution.py:164
  321.9 3.9 all-to-all-start.6
  327.1 10.8 %all-to-all-done.6 = bf16[16,24,1024]{2,1,0:T(8,128)(2,1)S(1)} async-done(((bf16[16,24,1024]{2,1,0:T(8,128)(2,1)}), bf16[16,24,1024]{2,1,0:T(8,128)(2,1)S(1)}, u32[]{:S(2)}, u32[]{:S(2)}) %all-to-all-start.6) | async-done | bytes 786464 | tf_op jit(solution)/shard_map/all_to_all | solution.py:164
  338.9 7.3 all-to-all-start.7
  346.2 2.6 pick.12
  348.9 14.2 %collective-permute-start.21 = (bf16[6,64,768]{2,1,0:T(8,128)(2,1)}, bf16[6,64,768]{2,1,0:T(8,128)(2,1)S(1)}, u32[]{:S(2)}, u32[]{:S(2)}) collective-permute-start(bf16[6,64,768]{2,1,0:T(8,128)(2,1)} %get-tuple-element.218), channel_id=1, source_target_pairs={{0,96},{32,0},{64,32},{96,64},{1,97},{33,1},{65,33},{97,65},{2,98}... | collective-permute-start | bytes 1769480 | tf_op jit(solution)/shard_map/ppermute | solution.py:135
  365.0 7.0 collective-permute-start.23
  374.8 5.5 collective-permute-start.24
  381.3 117.7 %all_gather.14 = bf16[128,1024]{1,0:T(8,128)(2,1)S(1)} all-gather(bf16[128,128]{1,0:T(8,128)(2,1)S(1)} %fusion.24), channel_id=1, replica_groups=mesh['x'=4,'h'=4,'y'=4,'l'=4,'c'=2] {'l','c'}, dimensions={1}, use_global_device_ids=true | all-gather | bytes 294912 | tf_op jit(solution)/shard_map/all_gather | solution.py:196
  499.0 2.4 constant_dynamic-update-slice_fusion.3
  503.1 2.6 collective-permute-start.25
  505.8 7.4 collective-permute-start.26
  513.2 35.9 %collective-permute-done.25.refs_1_ = bf16[6,24,1024]{2,1,0:T(8,128)(2,1)S(1)} collective-permute-done((bf16[6,24,1024]{2,1,0:T(8,128)(2,1)}, bf16[6,24,1024]{2,1,0:T(8,128)(2,1)S(1)}, u32[]{:S(2)}, u32[]{:S(2)}) %collective-permute-start.25) | collective-permute-done | bytes 294944 | tf_op jit(solution)/shard_map/ppermute | solution.py:134
  549.1 9.6 %collective-permute-done.26.refs_2_ = bf16[6,24,1024]{2,1,0:T(8,128)(2,1)S(1)} collective-permute-done((bf16[6,24,1024]{2,1,0:T(8,128)(2,1)S(1)}, bf16[6,24,1024]{2,1,0:T(8,128)(2,1)S(1)}, u32[]{:S(2)}, u32[]{:S(2)}) %collective-permute-start.26) | collective-permute-done | bytes 294944 | tf_op jit(solution)/shard_map/ppermute | solution.py:133
  558.8 3.6 all-to-all-start.9
  562.4 2.9 merge.13
  565.3 3.6 merge.12
  573.2 60.7 %while.42 = (s32[]{:T(128)}, bf16[16,64,768]{2,1,0:T(8,128)(2,1)}, bf16[16,24,1024]{2,1,0:T(8,128)(2,1)}, s32[]{:T(128)}, s32[3,20]{1,0:T(4,128)S(1)}, /*index=5...) while((s32[]{:T(128)}, bf16[16,64,768]{2,1,0:T(8,128)(2,1)}, ...), condition=%wide.region_10.11_spmd.clone, body=%wide.region_9.10_spmd.sunk.clone.sunk | while | flops 11206675 | bytes 22610968 | solution.py:160
  576.0 10.0 %collective-permute-start.10 = (bf16[2,24,1024]{2,1,0:T(8,128)(2,1)S(1)}, bf16[2,24,1024]{2,1,0:T(8,128)(2,1)S(1)}, u32[]{:S(2)}, u32[]{:S(2)}) collective-permute-start(bf16[2,24,1024]{2,1,0:T(8,128)(2,1)S(1)} %get-tuple-element.669), channel_id=1, source_target_pairs={{0,32},{32,64},{64,96},{96,0},{1,33},{33,65},{65,97},{97,1},{2,34}... | collective-permute-start | bytes 294920 | tf_op jit(solution)/shard_map/while/body/ppermute | solution.py:134
  590.2 7.3 collective-permute-start.7
  597.5 5.9 collective-permute-start.8
  603.4 8.1 %collective-permute-start.11 = (bf16[2,24,1024]{2,1,0:T(8,128)(2,1)}, bf16[2,24,1024]{2,1,0:T(8,128)(2,1)S(1)}, u32[]{:S(2)}, u32[]{:S(2)}) collective-permute-start(bf16[2,24,1024]{2,1,0:T(8,128)(2,1)} %get-tuple-element.670), channel_id=1, source_target_pairs={{0,64},{32,96},{64,0},{96,32},{1,65},{33,97},{65,1},{97,33},{2,66}... | collective-permute-start | bytes 294920 | tf_op jit(solution)/shard_map/while/body/ppermute | solution.py:133
  615.1 4.7 collective-permute-done.11.refs_2_
  619.8 7.6 %collective-permute-done.9.refs_0_ = bf16[2,24,1024]{2,1,0:T(8,128)(2,1)S(1)} collective-permute-done((bf16[2,24,1024]{2,1,0:T(8,128)(2,1)}, bf16[2,24,1024]{2,1,0:T(8,128)(2,1)S(1)}, u32[]{:S(2)}, u32[]{:S(2)}) %collective-permute-start.9) | collective-permute-done | bytes 98336 | tf_op jit(solution)/shard_map/while/body/ppermute | solution.py:135
  627.3 2.7 merge.18
  630.0 3.2 merge.17
  634.0 5.7 collective-permute-start.27
  639.7 3.6 collective-permute-start.28
  643.3 5.4 collective-permute-start.29
  648.7 5.8 all-to-all-start.11
  654.5 3.9 collective-permute-done.29.refs_2_
  659.7 29.4 %while.43 = (s32[]{:T(128)}, bf16[16,8,1408]{2,1,0:T(8,128)(2,1)S(1)}, s32[]{:T(128)}, s32[3,20]{1,0:T(4,128)S(1)}, bf16[16,8,1408]{2,1,0:T(8,128)(2,1)S(1)}, /*...) while((s32[]{:T(128)}, ...), condition=%wide.region_12.13_spmd.clone, body=%wide.region_11.12_spmd.sunk.clone.sunk | while | flops 1712147 | bytes 2974579 | solution.py:160
  661.2 9.0 %collective-permute-start.12 = (bf16[2,8,1408]{2,1,0:T(8,128)(2,1)S(1)}, bf16[2,8,1408]{2,1,0:T(8,128)(2,1)S(1)}, u32[]{:S(2)}, u32[]{:S(2)}) collective-permute-start(bf16[2,8,1408]{2,1,0:T(8,128)(2,1)S(1)} %get-tuple-element.682), channel_id=1, source_target_pairs={{0,96},{32,0},{64,32},{96,64},{1,97},{33,1},{65,33},{97,65},{2,98}... | collective-permute-start | bytes 135176 | tf_op jit(solution)/shard_map/while/body/ppermute | solution.py:135
  670.2 3.4 collective-permute-start.13
  673.7 7.5 %collective-permute-start.14 = (bf16[2,8,1408]{2,1,0:T(8,128)(2,1)S(1)}, bf16[2,8,1408]{2,1,0:T(8,128)(2,1)S(1)}, u32[]{:S(2)}, u32[]{:S(2)}) collective-permute-start(bf16[2,8,1408]{2,1,0:T(8,128)(2,1)S(1)} %get-tuple-element.684), channel_id=1, source_target_pairs={{0,64},{32,96},{64,0},{96,32},{1,65},{33,97},{65,1},{97,33},{2,66}... | collective-permute-start | bytes 135176 | tf_op jit(solution)/shard_map/while/body/ppermute | solution.py:133
  681.2 6.0 collective-permute-done.14.refs_2_
  689.1 21.4 %all_to_all.62 = bf16[16,8,1408]{2,1,0:T(8,128)(2,1)S(1)} all-to-all(bf16[16,8,1408]{2,1,0:T(8,128)(2,1)S(1)} %get-tuple-element.237), channel_id=1, replica_groups=mesh['x'=4,'h'=4,'y'=4,'l'=4,'c'=2] {'x','y'}, dimensions={0} | all-to-all | bytes 720896 | tf_op jit(solution)/shard_map/all_to_all | solution.py:164
  710.5 4.5 all-to-all-start.8
  716.9 16.2 %all_gather.15 = bf16[2,128,1024]{2,1,0:T(8,128)(2,1)S(1)} all-gather(bf16[2,128,128]{2,1,0:T(8,128)(2,1)S(1)} %bitcast.123), channel_id=1, replica_groups=mesh['x'=4,'h'=4,'y'=4,'l'=4,'c'=2] {'l','c'}, dimensions={2}, use_global_device_ids=true | all-gather | bytes 589824 | tf_op jit(solution)/shard_map/all_gather | solution.py:256
  733.8 2.4 fusion.4
  736.3 2.8 fusion.3
  739.1 2.5 fusion.2
  (174 shorter events, 44.3 us)
Async XLA Ops:
  0.6 23.8 %copy-start.31 = (bf16[1,1024,384]{2,1,0:T(8,128)(2,1)S(1)}, bf16[1,1024,384]{2,1,0:T(8,128)(2,1)}, u32[]{:S(2)}) copy-start(bf16[1,1024,384]{2,1,0:T(8,128)(2,1)} %param.16) | copy-start | bytes 2359300
  0.7 23.8 %copy-start.30 = (bf16[1,1024,384]{2,1,0:T(8,128)(2,1)S(1)}, bf16[1,1024,384]{2,1,0:T(8,128)(2,1)}, u32[]{:S(2)}) copy-start(bf16[1,1024,384]{2,1,0:T(8,128)(2,1)} %param.17) | copy-start | bytes 2359300
  3.7 37.7 %copy-start.28 = (bf16[2,2,128,128]{3,2,1,0:T(8,128)(2,1)}, bf16[2,2,128,128]{3,2,1,0:T(8,128)(2,1)S(1)}, u32[]{:S(2)}) copy-start(bf16[2,2,128,128]{3,2,1,0:T(8,128)(2,1)S(1)} %broadcast_select_fusion) | copy-start | bytes 393220
  24.4 42.0 %copy-start.25 = (bf16[2,1,128,1024]{3,2,1,0:T(8,128)(2,1)}, bf16[2,1,128,1024]{3,2,1,0:T(8,128)(2,1)S(1)}, u32[]{:S(2)}) copy-start(bf16[2,1,128,1024]{3,2,1,0:T(8,128)(2,1)S(1)} %all-gather) | copy-start | bytes 1572868
  24.8 12.9 %copy-start.35 = (f32[128,768]{1,0:T(8,128)}, f32[128,768]{1,0:T(8,128)S(1)}, u32[]{:S(2)}) copy-start(f32[128,768]{1,0:T(8,128)S(1)} %convolution_multiply_fusion.3) | copy-start | bytes 1179652
  37.8 20.1 %all-to-all-start.4 = ((bf16[16,24,1024]{2,1,0:T(8,128)(2,1)}), bf16[16,24,1024]{2,1,0:T(8,128)(2,1)S(1)}, u32[]{:S(2)}, u32[]{:S(2)}) async-start(bf16[16,24,1024]{2,1,0:T(8,128)(2,1)} %bitcast.19), calls=%async_computation.4 | async-start | bytes 1572864 | tf_op jit(solution)/shard_map/all_to_all | solution.py:164
  57.8 8.6 %copy-start.18 = (bf16[16,24,1024]{2,1,0:T(8,128)(2,1)}, bf16[16,24,1024]{2,1,0:T(8,128)(2,1)S(1)}, u32[]{:S(2)}) copy-start(bf16[16,24,1024]{2,1,0:T(8,128)(2,1)S(1)} %all-to-all-done.4.refs_4_) | copy-start | bytes 2359300
  57.8 19.5 %all-to-all-start.3 = ((bf16[16,24,1024]{2,1,0:T(8,128)(2,1)}), bf16[16,24,1024]{2,1,0:T(8,128)(2,1)S(1)}, u32[]{:S(2)}, u32[]{:S(2)}) async-start(bf16[16,24,1024]{2,1,0:T(8,128)(2,1)} %bitcast.18), calls=%async_computation.3 | async-start | bytes 1572864 | tf_op jit(solution)/shard_map/all_to_all | solution.py:164
  77.4 32.6 %copy-start.13 = (bf16[16,24,1024]{2,1,0:T(8,128)(2,1)}, bf16[16,24,1024]{2,1,0:T(8,128)(2,1)S(1)}, u32[]{:S(2)}) copy-start(bf16[16,24,1024]{2,1,0:T(8,128)(2,1)S(1)} %all-to-all-done.3.chunks.refs_3_) | copy-start | bytes 2359300
  77.4 25.1 %all-to-all-start.1 = ((bf16[16,64,768]{2,1,0:T(8,128)(2,1)}), bf16[16,64,768]{2,1,0:T(8,128)(2,1)S(1)}, u32[]{:S(2)}, u32[]{:S(2)}) async-start(bf16[16,64,768]{2,1,0:T(8,128)(2,1)} %bitcast.106), calls=%async_computation.1 | async-start | bytes 3145728 | tf_op jit(solution)/shard_map/all_to_all | solution.py:164
  82.1 2.5 copy-start.43
  82.2 2.5 copy-start.44
  103.6 183.4 %all-to-all-start.2 = ((bf16[16,64,768]{2,1,0:T(8,128)(2,1)}), bf16[16,64,768]{2,1,0:T(8,128)(2,1)}, u32[]{:S(2)}, u32[]{:S(2)}) async-start(bf16[16,64,768]{2,1,0:T(8,128)(2,1)} %pad_maximum_fusion.1), calls=%async_computation.2 | async-start | bytes 3145728 | tf_op jit(solution)/shard_map/all_to_all | solution.py:164
  111.4 27.5 %copy-start.5 = (bf16[6,24,1024]{2,1,0:T(8,128)(2,1)}, bf16[6,24,1024]{2,1,0:T(8,128)(2,1)S(1)}, u32[]{:S(2)}) copy-start(bf16[6,24,1024]{2,1,0:T(8,128)(2,1)S(1)} %get-tuple-element.213) | copy-start | bytes 884740
  111.4 27.5 %copy-start.6 = (bf16[6,24,1024]{2,1,0:T(8,128)(2,1)}, bf16[6,24,1024]{2,1,0:T(8,128)(2,1)S(1)}, u32[]{:S(2)}) copy-start(bf16[6,24,1024]{2,1,0:T(8,128)(2,1)S(1)} %get-tuple-element.212) | copy-start | bytes 884740
  111.4 127.6 %collective-permute-start.18 = (bf16[6,24,1024]{2,1,0:T(8,128)(2,1)}, bf16[6,24,1024]{2,1,0:T(8,128)(2,1)S(1)}, u32[]{:S(2)}, u32[]{:S(2)}) collective-permute-start(bf16[6,24,1024]{2,1,0:T(8,128)(2,1)} %get-tuple-element.211), channel_id=1, source_target_pairs={{0,96},{32,0},{64,32},{96,64},{1,97},{33,1},{65,33},{97,65},{2,98}... | collective-permute-start | bytes 884744 | tf_op jit(solution)/shard_map/ppermute | solution.py:135
  124.3 162.7 %collective-permute-start.15 = (bf16[6,64,768]{2,1,0:T(8,128)(2,1)}, bf16[6,64,768]{2,1,0:T(8,128)(2,1)S(1)}, u32[]{:S(2)}, u32[]{:S(2)}) collective-permute-start(bf16[6,64,768]{2,1,0:T(8,128)(2,1)} %get-tuple-element.206), channel_id=1, source_target_pairs={{0,96},{32,0},{64,32},{96,64},{1,97},{33,1},{65,33},{97,65},{2,98}... | collective-permute-start | bytes 1769480 | tf_op jit(solution)/shard_map/ppermute | solution.py:135
  129.5 157.5 %collective-permute-start.16 = (bf16[6,64,768]{2,1,0:T(8,128)(2,1)S(1)}, bf16[6,64,768]{2,1,0:T(8,128)(2,1)S(1)}, u32[]{:S(2)}, u32[]{:S(2)}) collective-permute-start(bf16[6,64,768]{2,1,0:T(8,128)(2,1)S(1)} %get-tuple-element.207), channel_id=1, source_target_pairs={{0,32},{32,64},{64,96},{96,0},{1,33},{33,65},{65,97},{97,1},{2,34}... | collective-permute-start | bytes 1769480 | tf_op jit(solution)/shard_map/ppermute | solution.py:134
  133.5 153.5 %collective-permute-start.17 = (bf16[6,64,768]{2,1,0:T(8,128)(2,1)S(1)}, bf16[6,64,768]{2,1,0:T(8,128)(2,1)S(1)}, u32[]{:S(2)}, u32[]{:S(2)}) collective-permute-start(bf16[6,64,768]{2,1,0:T(8,128)(2,1)S(1)} %get-tuple-element.208), channel_id=1, source_target_pairs={{0,64},{32,96},{64,0},{96,32},{1,65},{33,97},{65,1},{97,33},{2,66}... | collective-permute-start | bytes 1769480 | tf_op jit(solution)/shard_map/ppermute | solution.py:133
  139.2 109.0 %collective-permute-start.19 = (bf16[6,24,1024]{2,1,0:T(8,128)(2,1)}, bf16[6,24,1024]{2,1,0:T(8,128)(2,1)S(1)}, u32[]{:S(2)}, u32[]{:S(2)}) collective-permute-start(bf16[6,24,1024]{2,1,0:T(8,128)(2,1)} %copy-done.6), channel_id=1, source_target_pairs={{0,32},{32,64},{64,96},{96,0},{1,33},{33,65},{65,97},{97,1},{2,34}... | collective-permute-start | bytes 884744 | tf_op jit(solution)/shard_map/ppermute | solution.py:134
  239.0 43.7 %collective-permute-start.20 = (bf16[6,24,1024]{2,1,0:T(8,128)(2,1)}, bf16[6,24,1024]{2,1,0:T(8,128)(2,1)S(1)}, u32[]{:S(2)}, u32[]{:S(2)}) collective-permute-start(bf16[6,24,1024]{2,1,0:T(8,128)(2,1)} %copy-done.5), channel_id=1, source_target_pairs={{0,64},{32,96},{64,0},{96,32},{1,65},{33,97},{65,1},{97,33},{2,66}... | collective-permute-start | bytes 884744 | tf_op jit(solution)/shard_map/ppermute | solution.py:133
  321.9 4.3 copy-start.19
  321.9 3.9 copy-start.26
  321.9 15.9 %all-to-all-start.6 = ((bf16[16,24,1024]{2,1,0:T(8,128)(2,1)}), bf16[16,24,1024]{2,1,0:T(8,128)(2,1)S(1)}, u32[]{:S(2)}, u32[]{:S(2)}) async-start(bf16[16,24,1024]{2,1,0:T(8,128)(2,1)} %get-tuple-element.225), calls=%async_computation.6 | async-start | bytes 1572864 | tf_op jit(solution)/shard_map/all_to_all | solution.py:164
  327.1 21.8 %copy-start.36 = (bf16[128,384]{1,0:T(8,128)(2,1)}, bf16[128,384]{1,0:T(8,128)(2,1)S(1)}, u32[]{:S(2)}) copy-start(bf16[128,384]{1,0:T(8,128)(2,1)S(1)} %multiply_convert_fusion.2) | copy-start | bytes 294916
  337.8 8.4 %copy-start.23 = (bf16[16,24,1024]{2,1,0:T(8,128)(2,1)}, bf16[16,24,1024]{2,1,0:T(8,128)(2,1)S(1)}, u32[]{:S(2)}) copy-start(bf16[16,24,1024]{2,1,0:T(8,128)(2,1)S(1)} %all-to-all-done.6) | copy-start | bytes 2359300
  338.9 42.3 %copy-start.29 = (bf16[2,2,128,128]{3,2,1,0:T(8,128)(2,1)S(1)}, bf16[2,2,128,128]{3,2,1,0:T(8,128)(2,1)}, u32[]{:S(2)}) copy-start(bf16[2,2,128,128]{3,2,1,0:T(8,128)(2,1)} %copy-done.28) | copy-start | bytes 393220
  338.9 41.3 %all-to-all-start.7 = ((bf16[8,128,128]{2,1,0:T(8,128)(2,1)}), bf16[8,128,128]{2,1,0:T(8,128)(2,1)}, u32[]{:S(2)}, u32[]{:S(2)}) async-start(bf16[8,128,128]{2,1,0:T(8,128)(2,1)} %bitcast.96), calls=%async_computation.7 | async-start | bytes 524288 | tf_op jit(solution)/shard_map/all_to_all | solution.py:191
  348.9 209.9 %collective-permute-start.21 = (bf16[6,64,768]{2,1,0:T(8,128)(2,1)}, bf16[6,64,768]{2,1,0:T(8,128)(2,1)S(1)}, u32[]{:S(2)}, u32[]{:S(2)}) collective-permute-start(bf16[6,64,768]{2,1,0:T(8,128)(2,1)} %get-tuple-element.218), channel_id=1, source_target_pairs={{0,96},{32,0},{64,32},{96,64},{1,97},{33,1},{65,33},{97,65},{2,98}... | collective-permute-start | bytes 1769480 | tf_op jit(solution)/shard_map/ppermute | solution.py:135
  363.0 195.7 %collective-permute-start.22 = (bf16[6,64,768]{2,1,0:T(8,128)(2,1)}, bf16[6,64,768]{2,1,0:T(8,128)(2,1)S(1)}, u32[]{:S(2)}, u32[]{:S(2)}) collective-permute-start(bf16[6,64,768]{2,1,0:T(8,128)(2,1)} %get-tuple-element.219), channel_id=1, source_target_pairs={{0,32},{32,64},{64,96},{96,0},{1,33},{33,65},{65,97},{97,1},{2,34}... | collective-permute-start | bytes 1769480 | tf_op jit(solution)/shard_map/ppermute | solution.py:134
  365.0 193.8 %collective-permute-start.23 = (bf16[6,64,768]{2,1,0:T(8,128)(2,1)S(1)}, bf16[6,64,768]{2,1,0:T(8,128)(2,1)S(1)}, u32[]{:S(2)}, u32[]{:S(2)}) collective-permute-start(bf16[6,64,768]{2,1,0:T(8,128)(2,1)S(1)} %get-tuple-element.220), channel_id=1, source_target_pairs={{0,64},{32,96},{64,0},{96,32},{1,65},{33,97},{65,1},{97,33},{2,66}... | collective-permute-start | bytes 1769480 | tf_op jit(solution)/shard_map/ppermute | solution.py:133
  374.8 131.0 %collective-permute-start.24 = (bf16[6,24,1024]{2,1,0:T(8,128)(2,1)S(1)}, bf16[6,24,1024]{2,1,0:T(8,128)(2,1)S(1)}, u32[]{:S(2)}, u32[]{:S(2)}) collective-permute-start(bf16[6,24,1024]{2,1,0:T(8,128)(2,1)S(1)} %get-tuple-element.222), channel_id=1, source_target_pairs={{0,96},{32,0},{64,32},{96,64},{1,97},{33,1},{65,33},{97,65},{2,98}... | collective-permute-start | bytes 884744 | tf_op jit(solution)/shard_map/ppermute | solution.py:135
  381.3 121.8 %copy-start.22 = (f32[128,768]{1,0:T(8,128)S(1)}, f32[128,768]{1,0:T(8,128)}, u32[]{:S(2)}) copy-start(f32[128,768]{1,0:T(8,128)} %copy-done.21) | copy-start | bytes 1179652
  499.0 4.1 copy-start.39
  499.0 6.7 copy-start.8
  503.1 46.0 %collective-permute-start.25 = (bf16[6,24,1024]{2,1,0:T(8,128)(2,1)}, bf16[6,24,1024]{2,1,0:T(8,128)(2,1)S(1)}, u32[]{:S(2)}, u32[]{:S(2)}) collective-permute-start(bf16[6,24,1024]{2,1,0:T(8,128)(2,1)} %get-tuple-element.223), channel_id=1, source_target_pairs={{0,32},{32,64},{64,96},{96,0},{1,33},{33,65},{65,97},{97,1},{2,34}... | collective-permute-start | bytes 884744 | tf_op jit(solution)/shard_map/ppermute | solution.py:134
  505.8 53.0 %collective-permute-start.26 = (bf16[6,24,1024]{2,1,0:T(8,128)(2,1)S(1)}, bf16[6,24,1024]{2,1,0:T(8,128)(2,1)S(1)}, u32[]{:S(2)}, u32[]{:S(2)}) collective-permute-start(bf16[6,24,1024]{2,1,0:T(8,128)(2,1)S(1)} %copy-done.8), channel_id=1, source_target_pairs={{0,64},{32,96},{64,0},{96,32},{1,65},{33,97},{65,1},{97,33},{2,66}... | collective-permute-start | bytes 884744 | tf_op jit(solution)/shard_map/ppermute | solution.py:133
  513.2 45.6 %copy-start.38 = (bf16[128,1408]{1,0:T(8,128)(2,1)}, bf16[128,1408]{1,0:T(8,128)(2,1)S(1)}, u32[]{:S(2)}) copy-start(bf16[128,1408]{1,0:T(8,128)(2,1)S(1)} %fusion.27) | copy-start | bytes 1081348
  558.8 12.4 %all-to-all-start.9 = ((bf16[16,8,1408]{2,1,0:T(8,128)(2,1)}), bf16[16,8,1408]{2,1,0:T(8,128)(2,1)S(1)}, u32[]{:S(2)}, u32[]{:S(2)}) async-start(bf16[16,8,1408]{2,1,0:T(8,128)(2,1)} %bitcast.122), calls=%async_computation.9 | async-start | bytes 720896 | tf_op jit(solution)/shard_map/all_to_all | solution.py:164
  571.2 2.0 copy-start.14
  576.0 35.5 %collective-permute-start.10 = (bf16[2,24,1024]{2,1,0:T(8,128)(2,1)S(1)}, bf16[2,24,1024]{2,1,0:T(8,128)(2,1)S(1)}, u32[]{:S(2)}, u32[]{:S(2)}) collective-permute-start(bf16[2,24,1024]{2,1,0:T(8,128)(2,1)S(1)} %get-tuple-element.669), channel_id=1, source_target_pairs={{0,32},{32,64},{64,96},{96,0},{1,33},{33,65},{65,97},{97,1},{2,34}... | collective-permute-start | bytes 294920 | tf_op jit(solution)/shard_map/while/body/ppermute | solution.py:134
  588.3 41.7 %collective-permute-start.6 = (bf16[2,64,768]{2,1,0:T(8,128)(2,1)}, bf16[2,64,768]{2,1,0:T(8,128)(2,1)S(1)}, u32[]{:S(2)}, u32[]{:S(2)}) collective-permute-start(bf16[2,64,768]{2,1,0:T(8,128)(2,1)} %get-tuple-element.665), channel_id=1, source_target_pairs={{0,96},{32,0},{64,32},{96,64},{1,97},{33,1},{65,33},{97,65},{2,98}... | collective-permute-start | bytes 589832 | tf_op jit(solution)/shard_map/while/body/ppermute | solution.py:135
  590.2 39.8 %collective-permute-start.7 = (bf16[2,64,768]{2,1,0:T(8,128)(2,1)}, bf16[2,64,768]{2,1,0:T(8,128)(2,1)S(1)}, u32[]{:S(2)}, u32[]{:S(2)}) collective-permute-start(bf16[2,64,768]{2,1,0:T(8,128)(2,1)} %get-tuple-element.666), channel_id=1, source_target_pairs={{0,32},{32,64},{64,96},{96,0},{1,33},{33,65},{65,97},{97,1},{2,34}... | collective-permute-start | bytes 589832 | tf_op jit(solution)/shard_map/while/body/ppermute | solution.py:134
  597.5 32.5 %collective-permute-start.8 = (bf16[2,64,768]{2,1,0:T(8,128)(2,1)}, bf16[2,64,768]{2,1,0:T(8,128)(2,1)S(1)}, u32[]{:S(2)}, u32[]{:S(2)}) collective-permute-start(bf16[2,64,768]{2,1,0:T(8,128)(2,1)} %get-tuple-element.667), channel_id=1, source_target_pairs={{0,64},{32,96},{64,0},{96,32},{1,65},{33,97},{65,1},{97,33},{2,66}... | collective-permute-start | bytes 589832 | tf_op jit(solution)/shard_map/while/body/ppermute | solution.py:133
  603.4 16.3 %collective-permute-start.11 = (bf16[2,24,1024]{2,1,0:T(8,128)(2,1)}, bf16[2,24,1024]{2,1,0:T(8,128)(2,1)S(1)}, u32[]{:S(2)}, u32[]{:S(2)}) collective-permute-start(bf16[2,24,1024]{2,1,0:T(8,128)(2,1)} %get-tuple-element.670), channel_id=1, source_target_pairs={{0,64},{32,96},{64,0},{96,32},{1,65},{33,97},{65,1},{97,33},{2,66}... | collective-permute-start | bytes 294920 | tf_op jit(solution)/shard_map/while/body/ppermute | solution.py:133
  611.5 15.8 %collective-permute-start.9 = (bf16[2,24,1024]{2,1,0:T(8,128)(2,1)}, bf16[2,24,1024]{2,1,0:T(8,128)(2,1)S(1)}, u32[]{:S(2)}, u32[]{:S(2)}) collective-permute-start(bf16[2,24,1024]{2,1,0:T(8,128)(2,1)} %get-tuple-element.668), channel_id=1, source_target_pairs={{0,96},{32,0},{64,32},{96,64},{1,97},{33,1},{65,33},{97,65},{2,98}... | collective-permute-start | bytes 294920 | tf_op jit(solution)/shard_map/while/body/ppermute | solution.py:135
  633.9 24.4 %copy-start.15 = (bf16[16,8,1408]{2,1,0:T(8,128)(2,1)S(1)}, bf16[16,8,1408]{2,1,0:T(8,128)(2,1)}, u32[]{:S(2)}) copy-start(bf16[16,8,1408]{2,1,0:T(8,128)(2,1)} %copy-done.14) | copy-start | bytes 1081348
  634.0 20.6 %collective-permute-start.27 = (bf16[6,8,1408]{2,1,0:T(8,128)(2,1)}, bf16[6,8,1408]{2,1,0:T(8,128)(2,1)S(1)}, u32[]{:S(2)}, u32[]{:S(2)}) collective-permute-start(bf16[6,8,1408]{2,1,0:T(8,128)(2,1)} %copy-done.10), channel_id=1, source_target_pairs={{0,96},{32,0},{64,32},{96,64},{1,97},{33,1},{65,33},{97,65},{2,98}... | collective-permute-start | bytes 405512 | tf_op jit(solution)/shard_map/ppermute | solution.py:135
  639.7 14.8 %collective-permute-start.28 = (bf16[6,8,1408]{2,1,0:T(8,128)(2,1)}, bf16[6,8,1408]{2,1,0:T(8,128)(2,1)S(1)}, u32[]{:S(2)}, u32[]{:S(2)}) collective-permute-start(bf16[6,8,1408]{2,1,0:T(8,128)(2,1)} %copy-done.9), channel_id=1, source_target_pairs={{0,32},{32,64},{64,96},{96,0},{1,33},{33,65},{65,97},{97,1},{2,34}... | collective-permute-start | bytes 405512 | tf_op jit(solution)/shard_map/ppermute | solution.py:134
  643.3 15.1 %collective-permute-start.29 = (bf16[6,8,1408]{2,1,0:T(8,128)(2,1)S(1)}, bf16[6,8,1408]{2,1,0:T(8,128)(2,1)S(1)}, u32[]{:S(2)}, u32[]{:S(2)}) collective-permute-start(bf16[6,8,1408]{2,1,0:T(8,128)(2,1)S(1)} %get-tuple-element.236), channel_id=1, source_target_pairs={{0,64},{32,96},{64,0},{96,32},{1,65},{33,97},{65,1},{97,33},{2,66}... | collective-permute-start | bytes 405512 | tf_op jit(solution)/shard_map/ppermute | solution.py:133
  648.7 40.4 %all-to-all-start.11 = ((bf16[16,24,1024]{2,1,0:T(8,128)(2,1)}), bf16[16,24,1024]{2,1,0:T(8,128)(2,1)S(1)}, u32[]{:S(2)}, u32[]{:S(2)}) async-start(bf16[16,24,1024]{2,1,0:T(8,128)(2,1)} %get-tuple-element.238), calls=%async_computation.11 | async-start | bytes 1572864 | tf_op jit(solution)/shard_map/all_to_all | solution.py:164
  661.2 20.0 %collective-permute-start.12 = (bf16[2,8,1408]{2,1,0:T(8,128)(2,1)S(1)}, bf16[2,8,1408]{2,1,0:T(8,128)(2,1)S(1)}, u32[]{:S(2)}, u32[]{:S(2)}) collective-permute-start(bf16[2,8,1408]{2,1,0:T(8,128)(2,1)S(1)} %get-tuple-element.682), channel_id=1, source_target_pairs={{0,96},{32,0},{64,32},{96,64},{1,97},{33,1},{65,33},{97,65},{2,98}... | collective-permute-start | bytes 135176 | tf_op jit(solution)/shard_map/while/body/ppermute | solution.py:135
  670.2 10.9 %collective-permute-start.13 = (bf16[2,8,1408]{2,1,0:T(8,128)(2,1)S(1)}, bf16[2,8,1408]{2,1,0:T(8,128)(2,1)S(1)}, u32[]{:S(2)}, u32[]{:S(2)}) collective-permute-start(bf16[2,8,1408]{2,1,0:T(8,128)(2,1)S(1)} %get-tuple-element.683), channel_id=1, source_target_pairs={{0,32},{32,64},{64,96},{96,0},{1,33},{33,65},{65,97},{97,1},{2,34}... | collective-permute-start | bytes 135176 | tf_op jit(solution)/shard_map/while/body/ppermute | solution.py:134
  673.7 13.5 %collective-permute-start.14 = (bf16[2,8,1408]{2,1,0:T(8,128)(2,1)S(1)}, bf16[2,8,1408]{2,1,0:T(8,128)(2,1)S(1)}, u32[]{:S(2)}, u32[]{:S(2)}) collective-permute-start(bf16[2,8,1408]{2,1,0:T(8,128)(2,1)S(1)} %get-tuple-element.684), channel_id=1, source_target_pairs={{0,64},{32,96},{64,0},{96,32},{1,65},{33,97},{65,1},{97,33},{2,66}... | collective-permute-start | bytes 135176 | tf_op jit(solution)/shard_map/while/body/ppermute | solution.py:133
  710.5 4.5 copy-start.27
  710.5 5.6 copy-start.33
  710.5 5.6 copy-start.42
  710.5 25.8 %all-to-all-start.8 = ((bf16[16,64,768]{2,1,0:T(8,128)(2,1)}), bf16[16,64,768]{2,1,0:T(8,128)(2,1)}, u32[]{:S(2)}, u32[]{:S(2)}) async-start(bf16[16,64,768]{2,1,0:T(8,128)(2,1)} %get-tuple-element.232), calls=%async_computation.8 | async-start | bytes 3145728 | tf_op jit(solution)/shard_map/all_to_all | solution.py:164
  715.8 18.0 %copy-start.24 = (bf16[16,24,1024]{2,1,0:T(8,128)(2,1)S(1)}, bf16[16,24,1024]{2,1,0:T(8,128)(2,1)}, u32[]{:S(2)}) copy-start(bf16[16,24,1024]{2,1,0:T(8,128)(2,1)} %copy-done.23) | copy-start | bytes 2359300
  715.8 18.0 %copy-start.37 = (bf16[128,384]{1,0:T(8,128)(2,1)S(1)}, bf16[128,384]{1,0:T(8,128)(2,1)}, u32[]{:S(2)}) copy-start(bf16[128,384]{1,0:T(8,128)(2,1)} %copy-done.36) | copy-start | bytes 294916
  733.8 2.4 copy-start.20
  736.2 2.8 copy-start.34
  736.2 2.8 copy-start.40
  736.3 2.8 copy-start.41
  (8 other events, 8.9 us)

commit v3 on v2

--- a/solution.py
+++ b/solution.py
@@ -128,48 +128,48 @@
     return [(i, (i + n) % PLANES) for i in range(PLANES)]
 
 
-def hop(index, chunks, n_next, n_far):
-    up, down, across = pick(index, chunks, (n_next, n_next, n_far))
+def hop(sends):
+    up, down, across = sends
     from_far = lax.ppermute(across, "h", step_by(2))
     from_behind = lax.ppermute(up, "h", step_by(1))
     from_ahead = lax.ppermute(down, "h", step_by(-1))
     return from_ahead, from_behind, from_far
 
 
-def depart(route, chunks):
-    return hop(route[0], chunks, NEXT, FAR)
-
-
-def arrive(route, fn, outs, arrived, own):
+def over_plane(chunks):
+    return lax.all_to_all(chunks, FLAT, 0, 0, tiled=True)
+
+
+def arrive(route, arrived, own):
     send_index, where, trips = route
     low = jnp.array([NEXT, FAR], jnp.int32)
-    done = [merge(fn, where, 0 * low, a, o, outs) for a, o in zip(arrived, own)]
+    placed = merge(partners_own, where, 0 * low, arrived, (own,), 1)
 
     def late(state):
-        i, done = state
+        i, placed = state
         at = low + MORE * i
         index = jnp.stack(
             [lax.dynamic_slice(send_index[o], (at[o // 2],), (MORE,)) for o in range(3)]
         )
-        done = [
-            merge(fn, where, at, hop(index, o[0], MORE, MORE), o, outs, before=b)
-            for o, b in zip(own, done)
-        ]
-        return i + 1, done
-
-    return lax.while_loop(lambda s: s[0] < trips, late, (jnp.int32(0), done))[1]
-
-
-def over_plane(chunks):
-    return lax.all_to_all(chunks, FLAT, 0, 0, tiled=True)
-
-
-def spread(a):
-    return over_plane(a.reshape(PLANE, a.shape[0] // PLANE, a.shape[1]))
-
-
-def back_home(chunks):
-    return over_plane(chunks).reshape(-1, chunks.shape[-1])
+        parts = hop(pick(index, own, (MORE,) * 3))
+        return i + 1, merge(partners_own, where, at, parts, (own,), 1, before=placed)
+
+    return lax.while_loop(lambda s: s[0] < trips, late, (jnp.int32(0), placed))[1]
+
+
+def swap(route, arrays):
+    arrays = [a.reshape(PLANE, a.shape[0] // PLANE, a.shape[1]) for a in arrays]
+    shares, moved = [], []
+    for i, a in enumerate(arrays):
+        if i:
+            a, _ = lax.optimization_barrier((a, shares[-1]))
+        share = over_plane(a)
+        sends = pick(route[0], share, (NEXT, NEXT, FAR))
+        if i:
+            moved[-1], _ = lax.optimization_barrier((moved[-1], sends))
+        shares.append(share)
+        moved.append(hop(sends))
+    return [over_plane(arrive(route, m, s)[0]) for m, s in zip(moved, shares)]
 
 
 rows = (((0,), (0,)), ((), ()))
@@ -179,15 +179,15 @@
     return lax.dot_general(a, b, rows, preferred_element_type=jnp.float32)
 
 
-def local_step(both, down, inputs, in_cols, out_cols):
-    pre = jnp.dot(inputs, both, preferred_element_type=jnp.float32) * IN_SCALE
-    gate_pre, up_value = pre[:, :HID], pre[:, HID:]
+def local_step(weights, inputs, in_cols, out_cols):
+    w_gate, w_up, w_down = weights
+    gate_pre = jnp.dot(inputs, w_gate, preferred_element_type=jnp.float32) * IN_SCALE
+    up_value = jnp.dot(inputs, w_up, preferred_element_type=jnp.float32) * IN_SCALE
     sigmoid_gate = jax.nn.sigmoid(gate_pre)
     active = gate_pre * sigmoid_gate
     hidden = (active * up_value).astype(jnp.bfloat16)
-    term = jnp.dot(hidden, down, preferred_element_type=jnp.float32) * HID_SCALE
-    term = term.astype(jnp.bfloat16)
-    blocks = term.reshape(-1, N_TENSOR, COLS).transpose(1, 0, 2)
+    term = jnp.dot(hidden, w_down, preferred_element_type=jnp.float32) * HID_SCALE
+    blocks = term.astype(jnp.bfloat16).reshape(-1, N_TENSOR, COLS).transpose(1, 0, 2)
     terms = lax.all_to_all(blocks, TENSOR, 0, 0, tiled=True)
     branch = jnp.sum(terms.astype(jnp.float32), axis=0)
     error_cols = (in_cols.astype(jnp.float32) + branch - out_cols.astype(jnp.float32)).astype(
@@ -195,83 +195,80 @@
     )
     errors = lax.all_gather(error_cols, TENSOR, axis=1, tiled=True)
     back = (
-        lax.dot_general(errors, down, (((1,), (1,)), ((), ())), preferred_element_type=jnp.float32)
+        lax.dot_general(
+            errors, w_down, (((1,), (1,)), ((), ())), preferred_element_type=jnp.float32
+        )
         * HID_SCALE
     )
-    delta_gate = back * up_value * sigmoid_gate * (1.0 + gate_pre * (1.0 - sigmoid_gate))
-    delta_up = back * active
-    deltas = jnp.concatenate([delta_gate, delta_up], axis=1).astype(jnp.bfloat16)
-    return deltas, hidden, errors, error_cols
-
-
-def outer_update(theirs, stepped, weight):
-    weight = weight.astype(jnp.float32)
-    pair_mean = 0.5 * (stepped.astype(jnp.float32) + theirs.astype(jnp.float32))
-    outer_grad = weight - pair_mean
-    moment = outer_grad.astype(jnp.bfloat16).astype(jnp.float32)
-    updated = weight - outer_rate * (momentum_rate * outer_grad + outer_grad)
-    updated = updated.astype(jnp.bfloat16)
-    return updated, 0.475 * updated.astype(jnp.float32) - 0.2025 * moment
-
-
-def pair_sum(theirs, own):
-    return (theirs.astype(jnp.float32) + own.astype(jnp.float32),)
+    delta_gate = (back * up_value * sigmoid_gate * (1.0 + gate_pre * (1.0 - sigmoid_gate))).astype(
+        jnp.bfloat16
+    )
+    delta_up = (back * active).astype(jnp.bfloat16)
+    gradients = (
+        grad(inputs, delta_gate) * IN_SCALE,
+        grad(inputs, delta_up) * IN_SCALE,
+        grad(hidden, errors) * HID_SCALE,
+    )
+    return tuple(
+        (w.astype(jnp.float32) - inner_rate * g).astype(jnp.bfloat16)
+        for w, g in zip(weights, gradients)
+    )
+
+
+def partner_copy(route, arrays):
+    gate, up, down = arrays
+    down_in, gate_in, up_in = swap(route, [down, gate, up])
+    return tuple(g.reshape(a.shape) for g, a in zip((gate_in, up_in, down_in), arrays))
 
 
 def partners_own(theirs, own):
     return (theirs,)
 
 
+def outer_update(weight, stepped, partner_step):
+    weight = weight.astype(jnp.float32)
+    pair_mean = 0.5 * (stepped.astype(jnp.float32) + partner_step.astype(jnp.float32))
+    outer_grad = weight - pair_mean
+    moment_new = outer_grad
+    updated = weight - outer_rate * (momentum_rate * moment_new + outer_grad)
+    return updated.astype(jnp.bfloat16), moment_new.astype(jnp.bfloat16)
+
+
+def make_share(stepped, moment):
+    return (0.475 * stepped.astype(jnp.float32) - 0.2025 * moment.astype(jnp.float32)).astype(
+        jnp.bfloat16
+    )
+
+
+def final_update(weight, stepped, moment, partner_share):
+    updated = (
+        0.05 * weight.astype(jnp.float32)
+        + 0.475 * stepped.astype(jnp.float32)
+        - 0.2025 * moment.astype(jnp.float32)
+        + partner_share.astype(jnp.float32)
+    )
+    return updated.astype(jnp.bfloat16)
+
+
 def body(w_gate, w_up, w_down, pool, rows_index, partners):
-    both = jnp.concatenate([w_gate[0], w_up[0]], axis=1)
-    down = w_down[0]
+    weights = (w_gate[0], w_up[0], w_down[0])
     first, last = routes(partners)
     picked = jnp.take(pool[0], rows_index[0].reshape(-1), axis=0)
     picked = picked.reshape(ROUNDS, 2, -1, COLS)
     in_cols, out_cols = picked[:, 0], picked[:, 1]
     inputs = lax.all_gather(in_cols, TENSOR, axis=2, tiled=True)
-    start = [spread(both), spread(down)]
-
-    deltas, hidden, errors, _ = local_step(both, down, inputs[0], in_cols[0], out_cols[0])
-    step_down = (down.astype(jnp.float32) - HID_SCALE * grad(hidden, errors)).astype(jnp.bfloat16)
-    step_both = (both.astype(jnp.float32) - IN_SCALE * grad(inputs[0], deltas)).astype(jnp.bfloat16)
-    stepped = [spread(step_both), spread(step_down)]
-    arrived = [depart(first, s) for s in stepped]
-    done = arrive(first, outer_update, 2, arrived, list(zip(stepped, start)))
-
-    shares = [share for _, share in done]
-    arrived = [depart(last, s) for s in shares]
-    both, down = (back_home(new) for new, _ in done)
-    deltas, hidden, errors, error_cols = local_step(
-        both, down, inputs[1], in_cols[1], out_cols[1]
-    )
-    factors = jnp.concatenate([deltas, hidden, error_cols, in_cols[1]], axis=1)
-    arrived, factors = lax.optimization_barrier((arrived, factors))
-    factors = spread(factors)
-    on_way = depart(last, factors)
-    sums = arrive(last, pair_sum, 1, arrived, [(s,) for s in shares])
-    sum_both, sum_down = (back_home(s[0]) for s in sums)
-    theirs = back_home(arrive(last, partners_own, 1, [on_way], [(factors,)])[0][0])
-    cols = theirs[:, 3 * HID :].reshape(-1, 2, COLS).transpose(1, 0, 2)
-    cols = lax.all_gather(cols, TENSOR, axis=2, tiled=True)
-
-    def pair(mine, other):
-        return jnp.concatenate([mine, other], axis=0)
-
-    deltas = pair(deltas, theirs[:, : 2 * HID])
-    hidden = pair(hidden, theirs[:, 2 * HID : 3 * HID])
-    errors = pair(errors, cols[0])
-    inputs = pair(inputs[1], cols[1])
-
-    def final(weight, known, a, b, scale):
-        new = 0.05 * weight.astype(jnp.float32) + known.astype(jnp.float32)
-        return (new - (0.475 * inner_rate * scale) * grad(a, b)).astype(jnp.bfloat16)[None]
-
-    return (
-        final(both[:, :HID], sum_both[:, :HID], inputs, deltas[:, :HID], IN_SCALE),
-        final(both[:, HID:], sum_both[:, HID:], inputs, deltas[:, HID:], IN_SCALE),
-        final(down, sum_down, hidden, errors, HID_SCALE),
-    )
+
+    stepped = local_step(weights, inputs[0], in_cols[0], out_cols[0])
+    theirs = partner_copy(first, stepped)
+    results = [outer_update(*each) for each in zip(weights, stepped, theirs)]
+    weights = tuple(r[0] for r in results)
+    moments = tuple(r[1] for r in results)
+
+    stepped = local_step(weights, inputs[1], in_cols[1], out_cols[1])
+    shares = tuple(make_share(s, m) for s, m in zip(stepped, moments))
+    theirs = partner_copy(last, shares)
+    new = [final_update(*each) for each in zip(weights, stepped, moments, theirs)]
+    return tuple(w[None] for w in new)
 
 
 def solution(mesh):

time: 745 us -> 700 us (0.940); the launches traced: 742 us -> 689 us
  blocking collectives: 229 us -> 73.7 us
  starting transfers between devices: 193 us -> 256 us
  waiting for transfers between devices: 235 us -> 268 us
  other arithmetic: 9.69 us -> 20.5 us
    all_gather x2, blocking collectives: 132 us -> 27.9 us  [local_step(): errors = lax.all_gather(error_cols, TENSOR, axis=1, tiled=True)]
    all_to_all x2 -> x0, blocking collectives: 49.6 us -> none  [over_plane(): return lax.all_to_all(chunks, FLAT, 0, 0, tiled=True)]
    ppermute x8 -> x9, waiting for transfers between devices: 36 us -> 5.97 us  [hop(): from_behind = lax.ppermute(up, 'h', step_by(1))]
    ppermute x8 -> x9, starting transfers between devices: 53.8 us -> 83.4 us  [hop(): from_ahead = lax.ppermute(down, 'h', step_by(-1))]
    all_to_all x8 -> x12, starting transfers between devices: 37.7 us -> 66.2 us  [over_plane(): return lax.all_to_all(chunks, FLAT, 0, 0, tiled=True)]
    ppermute x8 -> x9, waiting for transfers between devices: 101 us -> 125 us  [hop(): from_ahead = lax.ppermute(down, 'h', step_by(-1))]
    ppermute x8 -> x9, waiting for transfers between devices: 58.8 us -> 79.9 us  [hop(): from_far = lax.ppermute(across, 'h', step_by(2))]
    all_gather x1 -> x0, blocking collectives: 16.2 us -> none  [body(): cols = lax.all_gather(cols, TENSOR, axis=2, tiled=True)]
  transfers between devices with their start and end apart: 33 -> 40, of which waited for: 12 -> 22; matrix products, arithmetic and copies ran while one was open for 3% -> 4% of each run, Pallas kernels for 4% -> 4%
where the time goes in v3:
time: 700 us; the launch traced here: 689 us
  waiting for transfers between devices  268 us (38%)
  starting transfers between devices  256 us (37%)
  blocking collectives  73.7 us (11%)
  Pallas kernels  34.6 us (5%)
  other arithmetic  20.5 us (3%)
  matrix products  18.5 us (3%)
  local copies, waits for them, and re-layouts  10.3 us (1%)
    ppermute x9, waiting for transfers between devices, hop(): from_ahead = lax.ppermute(down, 'h', step_by(-1))  125 us
    ppermute x9, starting transfers between devices, hop(): from_ahead = lax.ppermute(down, 'h', step_by(-1))  83.4 us
    ppermute x9, waiting for transfers between devices, hop(): from_far = lax.ppermute(across, 'h', step_by(2))  79.9 us
    ppermute x9, starting transfers between devices, hop(): from_far = lax.ppermute(across, 'h', step_by(2))  66.6 us
    all_to_all x12, starting transfers between devices, over_plane(): return lax.all_to_all(chunks, FLAT, 0, 0, tiled=True)  66.2 us
    all_to_all x12, waiting for transfers between devices, over_plane(): return lax.all_to_all(chunks, FLAT, 0, 0, tiled=True)  49.3 us
    ppermute x9, starting transfers between devices, hop(): from_behind = lax.ppermute(up, 'h', step_by(1))  36.1 us
    pallas_call x18, Pallas kernels, kernel_call(): pl.pallas_call(kernel, out_shape=out_shape, in_specs=scalars + [whole] *...  34.6 us
  transfers between devices with their start and end apart: 40, of which 22 were waited for; matrix products, arithmetic and copies ran while one was open for 4% of the time, Pallas kernels for 4%

profile of v3, /device:TPU:1, one launch (start us, length us, event | category | flops | bytes accessed | tf_op | source)
XLA Modules:
  0.0 688.8 jit_solution(1057081257658624661)
XLA Ops:
  3.6 20.9 %all-gather = bf16[2,1,128,1024]{3,2,1,0:T(8,128)(2,1)S(1)} all-gather(bf16[2,1,128,128]{3,2,1,0:T(8,128)(2,1)S(1)} %slice.221), channel_id=2, replica_groups=mesh['x'=4,'h'=4,'y'=4,'l'=4,'c'=2] {'l','c'}, dimensions={3}, use_global_device_ids=true | all-gather | bytes 589824 | tf_op jit(solution)/shard_map/all_gather | solution.py:259
  27.1 3.5 all-to-all-start
  31.4 7.9 %all-to-all-done = bf16[8,128,128]{2,1,0:T(8,128)(2,1)S(1)} async-done(((bf16[8,128,128]{2,1,0:T(8,128)(2,1)}), bf16[8,128,128]{2,1,0:T(8,128)(2,1)S(1)}, u32[]{:S(2)}, u32[]{:S(2)}) %all-to-all-start) | async-done | bytes 262176 | tf_op jit(solution)/shard_map/all_to_all | solution.py:191
  39.4 14.0 %all_gather.10 = bf16[128,1024]{1,0:T(8,128)(2,1)S(1)} all-gather(bf16[128,128]{1,0:T(8,128)(2,1)S(1)} %fusion.46), channel_id=1, replica_groups=mesh['x'=4,'h'=4,'y'=4,'l'=4,'c'=2] {'l','c'}, dimensions={1}, use_global_device_ids=true | all-gather | bytes 294912 | tf_op jit(solution)/shard_map/all_gather | solution.py:196
  54.6 4.3 all-to-all-start.1
  60.7 12.2 %all-to-all-done.1.chunks.refs_3_ = bf16[16,24,1024]{2,1,0:T(8,128)(2,1)} async-done(((bf16[16,24,1024]{2,1,0:T(8,128)(2,1)}), bf16[16,24,1024]{2,1,0:T(8,128)(2,1)}, u32[]{:S(2)}, u32[]{:S(2)}) %all-to-all-start.1) | async-done | bytes 786464 | tf_op jit(solution)/shard_map/all_to_all | solution.py:140
  72.9 4.4 all-to-all-start.2
  80.6 8.7 %collective-permute-start.24 = (bf16[6,24,1024]{2,1,0:T(8,128)(2,1)S(1)}, bf16[6,24,1024]{2,1,0:T(8,128)(2,1)S(1)}, u32[]{:S(2)}, u32[]{:S(2)}) collective-permute-start(bf16[6,24,1024]{2,1,0:T(8,128)(2,1)S(1)} %get-tuple-element.296), channel_id=1, source_target_pairs={{0,96},{32,0},{64,32},{96,64},{1,97},{33,1},{65,33},{97,65},{2,98}... | collective-permute-start | bytes 884744 | tf_op jit(solution)/shard_map/ppermute | solution.py:135
  91.2 10.3 %collective-permute-start.26 = (bf16[6,24,1024]{2,1,0:T(8,128)(2,1)S(1)}, bf16[6,24,1024]{2,1,0:T(8,128)(2,1)S(1)}, u32[]{:S(2)}, u32[]{:S(2)}) collective-permute-start(bf16[6,24,1024]{2,1,0:T(8,128)(2,1)S(1)} %get-tuple-element.298), channel_id=1, source_target_pairs={{0,64},{32,96},{64,0},{96,32},{1,65},{33,97},{65,1},{97,33},{2,66}... | collective-permute-start | bytes 884744 | tf_op jit(solution)/shard_map/ppermute | solution.py:133
  105.1 27.2 %collective-permute-done.24.refs_0_ = bf16[6,24,1024]{2,1,0:T(8,128)(2,1)S(1)} collective-permute-done((bf16[6,24,1024]{2,1,0:T(8,128)(2,1)S(1)}, bf16[6,24,1024]{2,1,0:T(8,128)(2,1)S(1)}, u32[]{:S(2)}, u32[]{:S(2)}) %collective-permute-start.24) | collective-permute-done | bytes 294944 | tf_op jit(solution)/shard_map/ppermute | solution.py:135
  134.4 6.1 all-to-all-start.3
  144.1 7.2 %all-to-all-done.3.chunks.refs_3_ = bf16[16,64,384]{2,1,0:T(8,128)(2,1)S(1)} async-done(((bf16[16,64,384]{2,1,0:T(8,128)(2,1)}), bf16[16,64,384]{2,1,0:T(8,128)(2,1)S(1)}, u32[]{:S(2)}, u32[]{:S(2)}) %all-to-all-start.3) | async-done | bytes 786464 | tf_op jit(solution)/shard_map/all_to_all | solution.py:140
  152.2 4.3 all-to-all-start.6
  156.5 18.1 %collective-permute-start.18 = (bf16[6,64,384]{2,1,0:T(8,128)(2,1)S(1)}, bf16[6,64,384]{2,1,0:T(8,128)(2,1)S(1)}, u32[]{:S(2)}, u32[]{:S(2)}) collective-permute-start(bf16[6,64,384]{2,1,0:T(8,128)(2,1)S(1)} %get-tuple-element.284), channel_id=1, source_target_pairs={{0,96},{32,0},{64,32},{96,64},{1,97},{33,1},{65,33},{97,65},{2,98}... | collective-permute-start | bytes 884744 | tf_op jit(solution)/shard_map/ppermute | solution.py:135
  174.6 7.1 %collective-permute-start.19 = (bf16[6,64,384]{2,1,0:T(8,128)(2,1)S(1)}, bf16[6,64,384]{2,1,0:T(8,128)(2,1)S(1)}, u32[]{:S(2)}, u32[]{:S(2)}) collective-permute-start(bf16[6,64,384]{2,1,0:T(8,128)(2,1)S(1)} %get-tuple-element.285), channel_id=1, source_target_pairs={{0,32},{32,64},{64,96},{96,0},{1,33},{33,65},{65,97},{97,1},{2,34}... | collective-permute-start | bytes 884744 | tf_op jit(solution)/shard_map/ppermute | solution.py:134
  181.7 7.0 %collective-permute-start.20 = (bf16[6,64,384]{2,1,0:T(8,128)(2,1)S(1)}, bf16[6,64,384]{2,1,0:T(8,128)(2,1)S(1)}, u32[]{:S(2)}, u32[]{:S(2)}) collective-permute-start(bf16[6,64,384]{2,1,0:T(8,128)(2,1)S(1)} %get-tuple-element.286), channel_id=1, source_target_pairs={{0,64},{32,96},{64,0},{96,32},{1,65},{33,97},{65,1},{97,33},{2,66}... | collective-permute-start | bytes 884744 | tf_op jit(solution)/shard_map/ppermute | solution.py:133
  190.1 7.3 %collective-permute-start.21 = (bf16[6,64,384]{2,1,0:T(8,128)(2,1)S(1)}, bf16[6,64,384]{2,1,0:T(8,128)(2,1)S(1)}, u32[]{:S(2)}, u32[]{:S(2)}) collective-permute-start(bf16[6,64,384]{2,1,0:T(8,128)(2,1)S(1)} %get-tuple-element.289), channel_id=1, source_target_pairs={{0,96},{32,0},{64,32},{96,64},{1,97},{33,1},{65,33},{97,65},{2,98}... | collective-permute-start | bytes 884744 | tf_op jit(solution)/shard_map/ppermute | solution.py:135
  199.3 33.8 %collective-permute-done.18.refs_0_ = bf16[6,64,384]{2,1,0:T(8,128)(2,1)S(1)} collective-permute-done((bf16[6,64,384]{2,1,0:T(8,128)(2,1)S(1)}, bf16[6,64,384]{2,1,0:T(8,128)(2,1)S(1)}, u32[]{:S(2)}, u32[]{:S(2)}) %collective-permute-start.18) | collective-permute-done | bytes 294944 | tf_op jit(solution)/shard_map/ppermute | solution.py:135
  233.1 6.7 collective-permute-start.23
  239.8 8.4 %collective-permute-done.20.refs_2_ = bf16[6,64,384]{2,1,0:T(8,128)(2,1)S(1)} collective-permute-done((bf16[6,64,384]{2,1,0:T(8,128)(2,1)S(1)}, bf16[6,64,384]{2,1,0:T(8,128)(2,1)S(1)}, u32[]{:S(2)}, u32[]{:S(2)}) %collective-permute-start.20) | collective-permute-done | bytes 294944 | tf_op jit(solution)/shard_map/ppermute | solution.py:133
  251.7 16.4 %collective-permute-done.23.refs_2_ = bf16[6,64,384]{2,1,0:T(8,128)(2,1)S(1)} collective-permute-done((bf16[6,64,384]{2,1,0:T(8,128)(2,1)S(1)}, bf16[6,64,384]{2,1,0:T(8,128)(2,1)S(1)}, u32[]{:S(2)}, u32[]{:S(2)}) %collective-permute-start.23) | collective-permute-done | bytes 294944 | tf_op jit(solution)/shard_map/ppermute | solution.py:133
  271.0 6.7 all-to-all-start.4
  278.4 12.0 %all-to-all-done.4 = bf16[16,64,384]{2,1,0:T(8,128)(2,1)S(1)} async-done(((bf16[16,64,384]{2,1,0:T(8,128)(2,1)}), bf16[16,64,384]{2,1,0:T(8,128)(2,1)S(1)}, u32[]{:S(2)}, u32[]{:S(2)}) %all-to-all-start.4) | async-done | bytes 786464 | tf_op jit(solution)/shard_map/all_to_all | solution.py:140
  290.4 4.6 all-to-all-start.5
  300.5 5.0 all-to-all-done.5
  308.9 24.9 %all_to_all.70 = bf16[8,128,128]{2,1,0:T(8,128)(2,1)S(1)} all-to-all(bf16[8,128,128]{2,1,0:T(8,128)(2,1)S(1)} %bitcast.161), channel_id=1, replica_groups=mesh['x'=4,'h'=4,'y'=4,'l'=4,'c'=2] {'l','c'}, dimensions={0} | all-to-all | bytes 524288 | tf_op jit(solution)/shard_map/all_to_all | solution.py:191
  333.9 14.0 %all_gather.11 = bf16[128,1024]{1,0:T(8,128)(2,1)S(1)} all-gather(bf16[128,128]{1,0:T(8,128)(2,1)S(1)} %fusion.45), channel_id=1, replica_groups=mesh['x'=4,'h'=4,'y'=4,'l'=4,'c'=2] {'l','c'}, dimensions={1}, use_global_device_ids=true | all-gather | bytes 294912 | tf_op jit(solution)/shard_map/all_gather | solution.py:196
  347.8 3.4 subtract_convert_fusion.1
  351.2 4.4 all-to-all-start.8
  356.9 3.3 subtract_convert_fusion.2
  360.2 9.4 %all-to-all-done.8.chunks.refs_3_ = bf16[16,24,1024]{2,1,0:T(8,128)(2,1)} async-done(((bf16[16,24,1024]{2,1,0:T(8,128)(2,1)}), bf16[16,24,1024]{2,1,0:T(8,128)(2,1)}, u32[]{:S(2)}, u32[]{:S(2)}) %all-to-all-start.8) | async-done | bytes 786464 | tf_op jit(solution)/shard_map/all_to_all | solution.py:140
  369.6 4.4 all-to-all-start.9
  375.5 11.7 %collective-permute-start.33 = (bf16[6,24,1024]{2,1,0:T(8,128)(2,1)S(1)}, bf16[6,24,1024]{2,1,0:T(8,128)(2,1)S(1)}, u32[]{:S(2)}, u32[]{:S(2)}) collective-permute-start(bf16[6,24,1024]{2,1,0:T(8,128)(2,1)S(1)} %get-tuple-element.316), channel_id=1, source_target_pairs={{0,96},{32,0},{64,32},{96,64},{1,97},{33,1},{65,33},{97,65},{2,98}... | collective-permute-start | bytes 884744 | tf_op jit(solution)/shard_map/ppermute | solution.py:135
  387.2 3.1 collective-permute-start.34
  390.3 7.0 %collective-permute-start.35 = (bf16[6,24,1024]{2,1,0:T(8,128)(2,1)S(1)}, bf16[6,24,1024]{2,1,0:T(8,128)(2,1)S(1)}, u32[]{:S(2)}, u32[]{:S(2)}) collective-permute-start(bf16[6,24,1024]{2,1,0:T(8,128)(2,1)S(1)} %get-tuple-element.318), channel_id=1, source_target_pairs={{0,64},{32,96},{64,0},{96,32},{1,65},{33,97},{65,1},{97,33},{2,66}... | collective-permute-start | bytes 884744 | tf_op jit(solution)/shard_map/ppermute | solution.py:133
  397.4 3.7 subtract_convert_fusion
  402.5 18.9 %collective-permute-done.33.refs_0_ = bf16[6,24,1024]{2,1,0:T(8,128)(2,1)S(1)} collective-permute-done((bf16[6,24,1024]{2,1,0:T(8,128)(2,1)S(1)}, bf16[6,24,1024]{2,1,0:T(8,128)(2,1)S(1)}, u32[]{:S(2)}, u32[]{:S(2)}) %collective-permute-start.33) | collective-permute-done | bytes 294944 | tf_op jit(solution)/shard_map/ppermute | solution.py:135
  421.4 7.2 %collective-permute-done.35.refs_2_ = bf16[6,24,1024]{2,1,0:T(8,128)(2,1)S(1)} collective-permute-done((bf16[6,24,1024]{2,1,0:T(8,128)(2,1)S(1)}, bf16[6,24,1024]{2,1,0:T(8,128)(2,1)S(1)}, u32[]{:S(2)}, u32[]{:S(2)}) %collective-permute-start.35) | collective-permute-done | bytes 294944 | tf_op jit(solution)/shard_map/ppermute | solution.py:133
  428.6 6.7 all-to-all-start.10
  438.2 34.7 %while.71 = (s32[]{:T(128)}, bf16[16,24,1024]{2,1,0:T(8,128)(2,1)}, s32[]{:T(128)}, s32[3,20]{1,0:T(4,128)S(1)}, bf16[16,24,1024]{2,1,0:T(8,128)(2,1)}, /*index=...) while((s32[]{:T(128)}, bf16[16,24,1024]{2,1,0:T(8,128)(2,1)}, ...), condition=%wide.region_18.19_spmd.clone, body=%wide.region_17.18_spmd.sunk.clone.sunk | while | flops 3735571 | bytes 9634703 | solution.py:157
  440.2 13.3 %collective-permute-start.15 = (bf16[2,24,1024]{2,1,0:T(8,128)(2,1)S(1)}, bf16[2,24,1024]{2,1,0:T(8,128)(2,1)S(1)}, u32[]{:S(2)}, u32[]{:S(2)}) collective-permute-start(bf16[2,24,1024]{2,1,0:T(8,128)(2,1)S(1)} %get-tuple-element.936), channel_id=1, source_target_pairs={{0,96},{32,0},{64,32},{96,64},{1,97},{33,1},{65,33},{97,65},{2,98}... | collective-permute-start | bytes 294920 | tf_op jit(solution)/shard_map/while/body/ppermute | solution.py:135
  455.5 7.0 %collective-permute-start.17 = (bf16[2,24,1024]{2,1,0:T(8,128)(2,1)S(1)}, bf16[2,24,1024]{2,1,0:T(8,128)(2,1)S(1)}, u32[]{:S(2)}, u32[]{:S(2)}) collective-permute-start(bf16[2,24,1024]{2,1,0:T(8,128)(2,1)S(1)} %get-tuple-element.938), channel_id=1, source_target_pairs={{0,64},{32,96},{64,0},{96,32},{1,65},{33,97},{65,1},{97,33},{2,66}... | collective-permute-start | bytes 294920 | tf_op jit(solution)/shard_map/while/body/ppermute | solution.py:133
  463.9 5.7 collective-permute-done.17.refs_2_
  473.8 6.7 all-to-all-start.13
  480.5 14.3 %collective-permute-start.27 = (bf16[6,64,384]{2,1,0:T(8,128)(2,1)S(1)}, bf16[6,64,384]{2,1,0:T(8,128)(2,1)S(1)}, u32[]{:S(2)}, u32[]{:S(2)}) collective-permute-start(bf16[6,64,384]{2,1,0:T(8,128)(2,1)S(1)} %get-tuple-element.304), channel_id=1, source_target_pairs={{0,96},{32,0},{64,32},{96,64},{1,97},{33,1},{65,33},{97,65},{2,98}... | collective-permute-start | bytes 884744 | tf_op jit(solution)/shard_map/ppermute | solution.py:135
  496.7 7.0 %collective-permute-start.29 = (bf16[6,64,384]{2,1,0:T(8,128)(2,1)S(1)}, bf16[6,64,384]{2,1,0:T(8,128)(2,1)S(1)}, u32[]{:S(2)}, u32[]{:S(2)}) collective-permute-start(bf16[6,64,384]{2,1,0:T(8,128)(2,1)S(1)} %get-tuple-element.306), channel_id=1, source_target_pairs={{0,64},{32,96},{64,0},{96,32},{1,65},{33,97},{65,1},{97,33},{2,66}... | collective-permute-start | bytes 884744 | tf_op jit(solution)/shard_map/ppermute | solution.py:133
  505.1 6.1 collective-permute-start.30
  514.3 7.0 %collective-permute-start.32 = (bf16[6,64,384]{2,1,0:T(8,128)(2,1)S(1)}, bf16[6,64,384]{2,1,0:T(8,128)(2,1)S(1)}, u32[]{:S(2)}, u32[]{:S(2)}) collective-permute-start(bf16[6,64,384]{2,1,0:T(8,128)(2,1)S(1)} %get-tuple-element.310), channel_id=1, source_target_pairs={{0,64},{32,96},{64,0},{96,32},{1,65},{33,97},{65,1},{97,33},{2,66}... | collective-permute-start | bytes 884744 | tf_op jit(solution)/shard_map/ppermute | solution.py:133
  521.4 4.0 collective-permute-done.28.refs_1_
  525.4 24.7 %collective-permute-done.29.refs_2_ = bf16[6,64,384]{2,1,0:T(8,128)(2,1)S(1)} collective-permute-done((bf16[6,64,384]{2,1,0:T(8,128)(2,1)S(1)}, bf16[6,64,384]{2,1,0:T(8,128)(2,1)S(1)}, u32[]{:S(2)}, u32[]{:S(2)}) %collective-permute-start.29) | collective-permute-done | bytes 294944 | tf_op jit(solution)/shard_map/ppermute | solution.py:133
  552.9 45.3 %collective-permute-done.30.refs_0_ = bf16[6,64,384]{2,1,0:T(8,128)(2,1)S(1)} collective-permute-done((bf16[6,64,384]{2,1,0:T(8,128)(2,1)S(1)}, bf16[6,64,384]{2,1,0:T(8,128)(2,1)S(1)}, u32[]{:S(2)}, u32[]{:S(2)}) %collective-permute-start.30) | collective-permute-done | bytes 294944 | tf_op jit(solution)/shard_map/ppermute | solution.py:135
  600.4 31.3 %while.69 = (s32[]{:T(128)}, bf16[16,64,384]{2,1,0:T(8,128)(2,1)}, s32[]{:T(128)}, s32[3,20]{1,0:T(4,128)S(1)}, bf16[16,64,384]{2,1,0:T(8,128)(2,1)}, /*index=5*...) while((s32[]{:T(128)}, bf16[16,64,384]{2,1,0:T(8,128)(2,1)}, ...), condition=%wide.region_14.15_spmd.clone, body=%wide.region_13.14_spmd.sunk.clone.sunk | while | flops 3735571 | bytes 6488947 | solution.py:157
  602.4 7.9 %collective-permute-start.10 = (bf16[2,64,384]{2,1,0:T(8,128)(2,1)S(1)}, bf16[2,64,384]{2,1,0:T(8,128)(2,1)S(1)}, u32[]{:S(2)}, u32[]{:S(2)}) collective-permute-start(bf16[2,64,384]{2,1,0:T(8,128)(2,1)S(1)} %get-tuple-element.909), channel_id=1, source_target_pairs={{0,32},{32,64},{64,96},{96,0},{1,33},{33,65},{65,97},{97,1},{2,34}... | collective-permute-start | bytes 294920 | tf_op jit(solution)/shard_map/while/body/ppermute | solution.py:134
  610.3 7.5 %collective-permute-start.11 = (bf16[2,64,384]{2,1,0:T(8,128)(2,1)S(1)}, bf16[2,64,384]{2,1,0:T(8,128)(2,1)S(1)}, u32[]{:S(2)}, u32[]{:S(2)}) collective-permute-start(bf16[2,64,384]{2,1,0:T(8,128)(2,1)S(1)} %get-tuple-element.910), channel_id=1, source_target_pairs={{0,64},{32,96},{64,0},{96,32},{1,65},{33,97},{65,1},{97,33},{2,66}... | collective-permute-start | bytes 294920 | tf_op jit(solution)/shard_map/while/body/ppermute | solution.py:133
  620.8 7.6 %collective-permute-done.11.refs_2_ = bf16[2,64,384]{2,1,0:T(8,128)(2,1)S(1)} collective-permute-done((bf16[2,64,384]{2,1,0:T(8,128)(2,1)S(1)}, bf16[2,64,384]{2,1,0:T(8,128)(2,1)S(1)}, u32[]{:S(2)}, u32[]{:S(2)}) %collective-permute-start.11) | collective-permute-done | bytes 98336 | tf_op jit(solution)/shard_map/while/body/ppermute | solution.py:133
  631.7 6.7 all-to-all-start.11
  638.4 29.3 %while.70 = (s32[]{:T(128)}, bf16[16,64,384]{2,1,0:T(8,128)(2,1)}, s32[]{:T(128)}, s32[3,20]{1,0:T(4,128)S(1)}, bf16[16,64,384]{2,1,0:T(8,128)(2,1)S(1)}, /*inde...) while((s32[]{:T(128)}, bf16[16,64,384]{2,1,0:T(8,128)(2,1)}, ...), condition=%wide.region_16.17_spmd.clone, body=%wide.region_15.16_spmd.sunk.clone.sunk | while | flops 3735571 | bytes 6488947 | solution.py:157
  641.7 7.3 %collective-permute-start.13 = (bf16[2,64,384]{2,1,0:T(8,128)(2,1)S(1)}, bf16[2,64,384]{2,1,0:T(8,128)(2,1)S(1)}, u32[]{:S(2)}, u32[]{:S(2)}) collective-permute-start(bf16[2,64,384]{2,1,0:T(8,128)(2,1)S(1)} %get-tuple-element.923), channel_id=1, source_target_pairs={{0,32},{32,64},{64,96},{96,0},{1,33},{33,65},{65,97},{97,1},{2,34}... | collective-permute-start | bytes 294920 | tf_op jit(solution)/shard_map/while/body/ppermute | solution.py:134
  649.0 7.1 %collective-permute-start.14 = (bf16[2,64,384]{2,1,0:T(8,128)(2,1)S(1)}, bf16[2,64,384]{2,1,0:T(8,128)(2,1)S(1)}, u32[]{:S(2)}, u32[]{:S(2)}) collective-permute-start(bf16[2,64,384]{2,1,0:T(8,128)(2,1)S(1)} %get-tuple-element.924), channel_id=1, source_target_pairs={{0,64},{32,96},{64,0},{96,32},{1,65},{33,97},{65,1},{97,33},{2,66}... | collective-permute-start | bytes 294920 | tf_op jit(solution)/shard_map/while/body/ppermute | solution.py:133
  657.3 7.8 %collective-permute-done.14.refs_2_ = bf16[2,64,384]{2,1,0:T(8,128)(2,1)S(1)} collective-permute-done((bf16[2,64,384]{2,1,0:T(8,128)(2,1)S(1)}, bf16[2,64,384]{2,1,0:T(8,128)(2,1)S(1)}, u32[]{:S(2)}, u32[]{:S(2)}) %collective-permute-start.14) | collective-permute-done | bytes 98336 | tf_op jit(solution)/shard_map/while/body/ppermute | solution.py:133
  667.7 6.8 all-to-all-start.12
  674.7 4.0 fusion.35
  681.8 3.3 all-to-all-done.12
  685.1 3.7 fusion.34
  (203 shorter events, 86.5 us)
Async XLA Ops:
  3.4 21.1 %copy-start.14 = (bf16[1,1024,384]{2,1,0:T(8,128)(2,1)S(1)}, bf16[1,1024,384]{2,1,0:T(8,128)(2,1)}, u32[]{:S(2)}) copy-start(bf16[1,1024,384]{2,1,0:T(8,128)(2,1)} %param.25) | copy-start | bytes 2359300
  3.6 35.8 %copy-start.34 = (bf16[2,2,128,128]{3,2,1,0:T(8,128)(2,1)}, bf16[2,2,128,128]{3,2,1,0:T(8,128)(2,1)S(1)}, u32[]{:S(2)}) copy-start(bf16[2,2,128,128]{3,2,1,0:T(8,128)(2,1)S(1)} %broadcast_select_fusion) | copy-start | bytes 393220
  3.6 21.2 %copy-start.26 = (bf16[1,1024,384]{2,1,0:T(8,128)(2,1)S(1)}, bf16[1,1024,384]{2,1,0:T(8,128)(2,1)}, u32[]{:S(2)}) copy-start(bf16[1,1024,384]{2,1,0:T(8,128)(2,1)} %param.26) | copy-start | bytes 2359300
  24.5 77.0 %copy-start.30 = (bf16[2,1,128,1024]{3,2,1,0:T(8,128)(2,1)}, bf16[2,1,128,1024]{3,2,1,0:T(8,128)(2,1)S(1)}, u32[]{:S(2)}) copy-start(bf16[2,1,128,1024]{3,2,1,0:T(8,128)(2,1)S(1)} %all-gather) | copy-start | bytes 1572868
  24.8 34.6 %copy-start.37 = (f32[128,384]{1,0:T(8,128)}, f32[128,384]{1,0:T(8,128)S(1)}, u32[]{:S(2)}) copy-start(f32[128,384]{1,0:T(8,128)S(1)} %convolution_multiply_fusion.7) | copy-start | bytes 589828
  27.1 12.2 %all-to-all-start = ((bf16[8,128,128]{2,1,0:T(8,128)(2,1)}), bf16[8,128,128]{2,1,0:T(8,128)(2,1)S(1)}, u32[]{:S(2)}, u32[]{:S(2)}) async-start(bf16[8,128,128]{2,1,0:T(8,128)(2,1)} %bitcast.158), calls=%async_computation | async-start | bytes 524288 | tf_op jit(solution)/shard_map/all_to_all | solution.py:191
  54.6 18.3 %all-to-all-start.1 = ((bf16[16,24,1024]{2,1,0:T(8,128)(2,1)}), bf16[16,24,1024]{2,1,0:T(8,128)(2,1)}, u32[]{:S(2)}, u32[]{:S(2)}) async-start(bf16[16,24,1024]{2,1,0:T(8,128)(2,1)} %bitcast.16), calls=%async_computation.1 | async-start | bytes 1572864 | tf_op jit(solution)/shard_map/all_to_all | solution.py:140
  72.9 28.6 %copy-start.38 = (f32[128,384]{1,0:T(8,128)S(1)}, f32[128,384]{1,0:T(8,128)}, u32[]{:S(2)}) copy-start(f32[128,384]{1,0:T(8,128)} %copy-done.37) | copy-start | bytes 589828
  72.9 30.8 %all-to-all-start.2 = ((bf16[16,64,384]{2,1,0:T(8,128)(2,1)}), bf16[16,64,384]{2,1,0:T(8,128)(2,1)}, u32[]{:S(2)}, u32[]{:S(2)}) async-start(bf16[16,64,384]{2,1,0:T(8,128)(2,1)} %bitcast.15), calls=%async_computation.2 | async-start | bytes 1572864 | tf_op jit(solution)/shard_map/all_to_all | solution.py:140
  77.3 24.2 %copy-start.27 = (bf16[1,1024,384]{2,1,0:T(8,128)(2,1)S(1)}, bf16[1,1024,384]{2,1,0:T(8,128)(2,1)}, u32[]{:S(2)}) copy-start(bf16[1,1024,384]{2,1,0:T(8,128)(2,1)} %param.26) | copy-start | bytes 2359300
  80.6 51.7 %collective-permute-start.24 = (bf16[6,24,1024]{2,1,0:T(8,128)(2,1)S(1)}, bf16[6,24,1024]{2,1,0:T(8,128)(2,1)S(1)}, u32[]{:S(2)}, u32[]{:S(2)}) collective-permute-start(bf16[6,24,1024]{2,1,0:T(8,128)(2,1)S(1)} %get-tuple-element.296), channel_id=1, source_target_pairs={{0,96},{32,0},{64,32},{96,64},{1,97},{33,1},{65,33},{97,65},{2,98}... | collective-permute-start | bytes 884744 | tf_op jit(solution)/shard_map/ppermute | solution.py:135
  89.3 43.0 %collective-permute-start.25 = (bf16[6,24,1024]{2,1,0:T(8,128)(2,1)S(1)}, bf16[6,24,1024]{2,1,0:T(8,128)(2,1)S(1)}, u32[]{:S(2)}, u32[]{:S(2)}) collective-permute-start(bf16[6,24,1024]{2,1,0:T(8,128)(2,1)S(1)} %get-tuple-element.297), channel_id=1, source_target_pairs={{0,32},{32,64},{64,96},{96,0},{1,33},{33,65},{65,97},{97,1},{2,34}... | collective-permute-start | bytes 884744 | tf_op jit(solution)/shard_map/ppermute | solution.py:134
  91.2 43.2 %collective-permute-start.26 = (bf16[6,24,1024]{2,1,0:T(8,128)(2,1)S(1)}, bf16[6,24,1024]{2,1,0:T(8,128)(2,1)S(1)}, u32[]{:S(2)}, u32[]{:S(2)}) collective-permute-start(bf16[6,24,1024]{2,1,0:T(8,128)(2,1)S(1)} %get-tuple-element.298), channel_id=1, source_target_pairs={{0,64},{32,96},{64,0},{96,32},{1,65},{33,97},{65,1},{97,33},{2,66}... | collective-permute-start | bytes 884744 | tf_op jit(solution)/shard_map/ppermute | solution.py:133
  134.4 16.8 %all-to-all-start.3 = ((bf16[16,64,384]{2,1,0:T(8,128)(2,1)}), bf16[16,64,384]{2,1,0:T(8,128)(2,1)S(1)}, u32[]{:S(2)}, u32[]{:S(2)}) async-start(bf16[16,64,384]{2,1,0:T(8,128)(2,1)} %bitcast.160), calls=%async_computation.3 | async-start | bytes 1572864 | tf_op jit(solution)/shard_map/all_to_all | solution.py:140
  152.2 118.1 %all-to-all-start.6 = ((bf16[16,24,1024]{2,1,0:T(8,128)(2,1)}), bf16[16,24,1024]{2,1,0:T(8,128)(2,1)}, u32[]{:S(2)}, u32[]{:S(2)}) async-start(bf16[16,24,1024]{2,1,0:T(8,128)(2,1)} %get-tuple-element.302), calls=%async_computation.6 | async-start | bytes 1572864 | tf_op jit(solution)/shard_map/all_to_all | solution.py:140
  156.5 76.6 %collective-permute-start.18 = (bf16[6,64,384]{2,1,0:T(8,128)(2,1)S(1)}, bf16[6,64,384]{2,1,0:T(8,128)(2,1)S(1)}, u32[]{:S(2)}, u32[]{:S(2)}) collective-permute-start(bf16[6,64,384]{2,1,0:T(8,128)(2,1)S(1)} %get-tuple-element.284), channel_id=1, source_target_pairs={{0,96},{32,0},{64,32},{96,64},{1,97},{33,1},{65,33},{97,65},{2,98}... | collective-permute-start | bytes 884744 | tf_op jit(solution)/shard_map/ppermute | solution.py:135
  174.6 65.2 %collective-permute-start.19 = (bf16[6,64,384]{2,1,0:T(8,128)(2,1)S(1)}, bf16[6,64,384]{2,1,0:T(8,128)(2,1)S(1)}, u32[]{:S(2)}, u32[]{:S(2)}) collective-permute-start(bf16[6,64,384]{2,1,0:T(8,128)(2,1)S(1)} %get-tuple-element.285), channel_id=1, source_target_pairs={{0,32},{32,64},{64,96},{96,0},{1,33},{33,65},{65,97},{97,1},{2,34}... | collective-permute-start | bytes 884744 | tf_op jit(solution)/shard_map/ppermute | solution.py:134
  181.7 66.5 %collective-permute-start.20 = (bf16[6,64,384]{2,1,0:T(8,128)(2,1)S(1)}, bf16[6,64,384]{2,1,0:T(8,128)(2,1)S(1)}, u32[]{:S(2)}, u32[]{:S(2)}) collective-permute-start(bf16[6,64,384]{2,1,0:T(8,128)(2,1)S(1)} %get-tuple-element.286), channel_id=1, source_target_pairs={{0,64},{32,96},{64,0},{96,32},{1,65},{33,97},{65,1},{97,33},{2,66}... | collective-permute-start | bytes 884744 | tf_op jit(solution)/shard_map/ppermute | solution.py:133
  190.1 60.9 %collective-permute-start.21 = (bf16[6,64,384]{2,1,0:T(8,128)(2,1)S(1)}, bf16[6,64,384]{2,1,0:T(8,128)(2,1)S(1)}, u32[]{:S(2)}, u32[]{:S(2)}) collective-permute-start(bf16[6,64,384]{2,1,0:T(8,128)(2,1)S(1)} %get-tuple-element.289), channel_id=1, source_target_pairs={{0,96},{32,0},{64,32},{96,64},{1,97},{33,1},{65,33},{97,65},{2,98}... | collective-permute-start | bytes 884744 | tf_op jit(solution)/shard_map/ppermute | solution.py:135
  197.4 54.3 %collective-permute-start.22 = (bf16[6,64,384]{2,1,0:T(8,128)(2,1)S(1)}, bf16[6,64,384]{2,1,0:T(8,128)(2,1)S(1)}, u32[]{:S(2)}, u32[]{:S(2)}) collective-permute-start(bf16[6,64,384]{2,1,0:T(8,128)(2,1)S(1)} %get-tuple-element.288), channel_id=1, source_target_pairs={{0,32},{32,64},{64,96},{96,0},{1,33},{33,65},{65,97},{97,1},{2,34}... | collective-permute-start | bytes 884744 | tf_op jit(solution)/shard_map/ppermute | solution.py:134
  233.1 35.0 %collective-permute-start.23 = (bf16[6,64,384]{2,1,0:T(8,128)(2,1)S(1)}, bf16[6,64,384]{2,1,0:T(8,128)(2,1)S(1)}, u32[]{:S(2)}, u32[]{:S(2)}) collective-permute-start(bf16[6,64,384]{2,1,0:T(8,128)(2,1)S(1)} %get-tuple-element.290), channel_id=1, source_target_pairs={{0,64},{32,96},{64,0},{96,32},{1,65},{33,97},{65,1},{97,33},{2,66}... | collective-permute-start | bytes 884744 | tf_op jit(solution)/shard_map/ppermute | solution.py:133
  239.8 28.3 %copy-start.5 = (bf16[16,64,384]{2,1,0:T(8,128)(2,1)S(1)}, bf16[16,64,384]{2,1,0:T(8,128)(2,1)}, u32[]{:S(2)}) copy-start(bf16[16,64,384]{2,1,0:T(8,128)(2,1)} %copy-done.4) | copy-start | bytes 2359300
  271.0 6.7 copy-start.6
  271.0 19.4 %all-to-all-start.4 = ((bf16[16,64,384]{2,1,0:T(8,128)(2,1)}), bf16[16,64,384]{2,1,0:T(8,128)(2,1)S(1)}, u32[]{:S(2)}, u32[]{:S(2)}) async-start(bf16[16,64,384]{2,1,0:T(8,128)(2,1)} %get-tuple-element.294), calls=%async_computation.4 | async-start | bytes 1572864 | tf_op jit(solution)/shard_map/all_to_all | solution.py:140
  290.4 6.7 copy-start.20
  290.4 15.1 %all-to-all-start.5 = ((bf16[16,64,384]{2,1,0:T(8,128)(2,1)}), bf16[16,64,384]{2,1,0:T(8,128)(2,1)}, u32[]{:S(2)}, u32[]{:S(2)}) async-start(bf16[16,64,384]{2,1,0:T(8,128)(2,1)} %get-tuple-element.295), calls=%async_computation.5 | async-start | bytes 1572864 | tf_op jit(solution)/shard_map/all_to_all | solution.py:140
  297.2 58.5 %copy-start.12 = (bf16[384,1024]{1,0:T(8,128)(2,1)}, bf16[384,1024]{1,0:T(8,128)(2,1)S(1)}, u32[]{:S(2)}) copy-start(bf16[384,1024]{1,0:T(8,128)(2,1)S(1)} %fusion.18) | copy-start | bytes 2359300
  300.5 7.1 %copy-start.39 = (f32[128,384]{1,0:T(8,128)}, f32[128,384]{1,0:T(8,128)S(1)}, u32[]{:S(2)}) copy-start(f32[128,384]{1,0:T(8,128)S(1)} %convolution_multiply_fusion.4) | copy-start | bytes 589828
  308.9 25.0 %copy-start.35 = (bf16[2,2,128,128]{3,2,1,0:T(8,128)(2,1)S(1)}, bf16[2,2,128,128]{3,2,1,0:T(8,128)(2,1)}, u32[]{:S(2)}) copy-start(bf16[2,2,128,128]{3,2,1,0:T(8,128)(2,1)} %copy-done.34) | copy-start | bytes 393220
  351.2 5.5 copy-start.24
  351.2 5.5 copy-start.33
  351.2 18.4 %all-to-all-start.8 = ((bf16[16,24,1024]{2,1,0:T(8,128)(2,1)}), bf16[16,24,1024]{2,1,0:T(8,128)(2,1)}, u32[]{:S(2)}, u32[]{:S(2)}) async-start(bf16[16,24,1024]{2,1,0:T(8,128)(2,1)} %bitcast.163), calls=%async_computation.8 | async-start | bytes 1572864 | tf_op jit(solution)/shard_map/all_to_all | solution.py:140
  369.6 27.7 %copy-start.41 = (f32[128,384]{1,0:T(8,128)S(1)}, f32[128,384]{1,0:T(8,128)}, u32[]{:S(2)}) copy-start(f32[128,384]{1,0:T(8,128)} %copy-done.39) | copy-start | bytes 589828
  369.6 31.5 %all-to-all-start.9 = ((bf16[16,64,384]{2,1,0:T(8,128)(2,1)}), bf16[16,64,384]{2,1,0:T(8,128)(2,1)}, u32[]{:S(2)}, u32[]{:S(2)}) async-start(bf16[16,64,384]{2,1,0:T(8,128)(2,1)} %bitcast.27), calls=%async_computation.9 | async-start | bytes 1572864 | tf_op jit(solution)/shard_map/all_to_all | solution.py:140
  374.1 23.3 %copy-start.18 = (bf16[1024,384]{1,0:T(8,128)(2,1)S(1)}, bf16[1024,384]{1,0:T(8,128)(2,1)}, u32[]{:S(2)}) copy-start(bf16[1024,384]{1,0:T(8,128)(2,1)} %fusion.19) | copy-start | bytes 2359300
  375.5 45.9 %collective-permute-start.33 = (bf16[6,24,1024]{2,1,0:T(8,128)(2,1)S(1)}, bf16[6,24,1024]{2,1,0:T(8,128)(2,1)S(1)}, u32[]{:S(2)}, u32[]{:S(2)}) collective-permute-start(bf16[6,24,1024]{2,1,0:T(8,128)(2,1)S(1)} %get-tuple-element.316), channel_id=1, source_target_pairs={{0,96},{32,0},{64,32},{96,64},{1,97},{33,1},{65,33},{97,65},{2,98}... | collective-permute-start | bytes 884744 | tf_op jit(solution)/shard_map/ppermute | solution.py:135
  387.2 34.2 %collective-permute-start.34 = (bf16[6,24,1024]{2,1,0:T(8,128)(2,1)S(1)}, bf16[6,24,1024]{2,1,0:T(8,128)(2,1)S(1)}, u32[]{:S(2)}, u32[]{:S(2)}) collective-permute-start(bf16[6,24,1024]{2,1,0:T(8,128)(2,1)S(1)} %get-tuple-element.317), channel_id=1, source_target_pairs={{0,32},{32,64},{64,96},{96,0},{1,33},{33,65},{65,97},{97,1},{2,34}... | collective-permute-start | bytes 884744 | tf_op jit(solution)/shard_map/ppermute | solution.py:134
  390.3 38.3 %collective-permute-start.35 = (bf16[6,24,1024]{2,1,0:T(8,128)(2,1)S(1)}, bf16[6,24,1024]{2,1,0:T(8,128)(2,1)S(1)}, u32[]{:S(2)}, u32[]{:S(2)}) collective-permute-start(bf16[6,24,1024]{2,1,0:T(8,128)(2,1)S(1)} %get-tuple-element.318), channel_id=1, source_target_pairs={{0,64},{32,96},{64,0},{96,32},{1,65},{33,97},{65,1},{97,33},{2,66}... | collective-permute-start | bytes 884744 | tf_op jit(solution)/shard_map/ppermute | solution.py:133
  428.6 44.3 %all-to-all-start.10 = ((bf16[16,64,384]{2,1,0:T(8,128)(2,1)}), bf16[16,64,384]{2,1,0:T(8,128)(2,1)S(1)}, u32[]{:S(2)}, u32[]{:S(2)}) async-start(bf16[16,64,384]{2,1,0:T(8,128)(2,1)} %bitcast.162), calls=%async_computation.10 | async-start | bytes 1572864 | tf_op jit(solution)/shard_map/all_to_all | solution.py:140
  438.8 23.7 %copy-start.7 = (bf16[16,24,1024]{2,1,0:T(8,128)(2,1)S(1)}, bf16[16,24,1024]{2,1,0:T(8,128)(2,1)}, u32[]{:S(2)}) copy-start(bf16[16,24,1024]{2,1,0:T(8,128)(2,1)} %get-tuple-element.1116) | copy-start | bytes 2359300 | tf_op jit(solution)/shard_map/while
  440.2 22.4 %collective-permute-start.15 = (bf16[2,24,1024]{2,1,0:T(8,128)(2,1)S(1)}, bf16[2,24,1024]{2,1,0:T(8,128)(2,1)S(1)}, u32[]{:S(2)}, u32[]{:S(2)}) collective-permute-start(bf16[2,24,1024]{2,1,0:T(8,128)(2,1)S(1)} %get-tuple-element.936), channel_id=1, source_target_pairs={{0,96},{32,0},{64,32},{96,64},{1,97},{33,1},{65,33},{97,65},{2,98}... | collective-permute-start | bytes 294920 | tf_op jit(solution)/shard_map/while/body/ppermute | solution.py:135
  453.6 10.3 %collective-permute-start.16 = (bf16[2,24,1024]{2,1,0:T(8,128)(2,1)S(1)}, bf16[2,24,1024]{2,1,0:T(8,128)(2,1)S(1)}, u32[]{:S(2)}, u32[]{:S(2)}) collective-permute-start(bf16[2,24,1024]{2,1,0:T(8,128)(2,1)S(1)} %get-tuple-element.937), channel_id=1, source_target_pairs={{0,32},{32,64},{64,96},{96,0},{1,33},{33,65},{65,97},{97,1},{2,34}... | collective-permute-start | bytes 294920 | tf_op jit(solution)/shard_map/while/body/ppermute | solution.py:134
  455.5 14.1 %collective-permute-start.17 = (bf16[2,24,1024]{2,1,0:T(8,128)(2,1)S(1)}, bf16[2,24,1024]{2,1,0:T(8,128)(2,1)S(1)}, u32[]{:S(2)}, u32[]{:S(2)}) collective-permute-start(bf16[2,24,1024]{2,1,0:T(8,128)(2,1)S(1)} %get-tuple-element.938), channel_id=1, source_target_pairs={{0,64},{32,96},{64,0},{96,32},{1,65},{33,97},{65,1},{97,33},{2,66}... | collective-permute-start | bytes 294920 | tf_op jit(solution)/shard_map/while/body/ppermute | solution.py:133
  473.8 126.6 %all-to-all-start.13 = ((bf16[16,24,1024]{2,1,0:T(8,128)(2,1)}), bf16[16,24,1024]{2,1,0:T(8,128)(2,1)}, u32[]{:S(2)}, u32[]{:S(2)}) async-start(bf16[16,24,1024]{2,1,0:T(8,128)(2,1)} %get-tuple-element.322), calls=%async_computation.13 | async-start | bytes 1572864 | tf_op jit(solution)/shard_map/all_to_all | solution.py:140
  480.5 33.8 %collective-permute-start.27 = (bf16[6,64,384]{2,1,0:T(8,128)(2,1)S(1)}, bf16[6,64,384]{2,1,0:T(8,128)(2,1)S(1)}, u32[]{:S(2)}, u32[]{:S(2)}) collective-permute-start(bf16[6,64,384]{2,1,0:T(8,128)(2,1)S(1)} %get-tuple-element.304), channel_id=1, source_target_pairs={{0,96},{32,0},{64,32},{96,64},{1,97},{33,1},{65,33},{97,65},{2,98}... | collective-permute-start | bytes 884744 | tf_op jit(solution)/shard_map/ppermute | solution.py:135
  494.8 30.6 %collective-permute-start.28 = (bf16[6,64,384]{2,1,0:T(8,128)(2,1)S(1)}, bf16[6,64,384]{2,1,0:T(8,128)(2,1)S(1)}, u32[]{:S(2)}, u32[]{:S(2)}) collective-permute-start(bf16[6,64,384]{2,1,0:T(8,128)(2,1)S(1)} %get-tuple-element.305), channel_id=1, source_target_pairs={{0,32},{32,64},{64,96},{96,0},{1,33},{33,65},{65,97},{97,1},{2,34}... | collective-permute-start | bytes 884744 | tf_op jit(solution)/shard_map/ppermute | solution.py:134
  496.7 53.3 %collective-permute-start.29 = (bf16[6,64,384]{2,1,0:T(8,128)(2,1)S(1)}, bf16[6,64,384]{2,1,0:T(8,128)(2,1)S(1)}, u32[]{:S(2)}, u32[]{:S(2)}) collective-permute-start(bf16[6,64,384]{2,1,0:T(8,128)(2,1)S(1)} %get-tuple-element.306), channel_id=1, source_target_pairs={{0,64},{32,96},{64,0},{96,32},{1,65},{33,97},{65,1},{97,33},{2,66}... | collective-permute-start | bytes 884744 | tf_op jit(solution)/shard_map/ppermute | solution.py:133
  505.1 93.0 %collective-permute-start.30 = (bf16[6,64,384]{2,1,0:T(8,128)(2,1)S(1)}, bf16[6,64,384]{2,1,0:T(8,128)(2,1)S(1)}, u32[]{:S(2)}, u32[]{:S(2)}) collective-permute-start(bf16[6,64,384]{2,1,0:T(8,128)(2,1)S(1)} %get-tuple-element.309), channel_id=1, source_target_pairs={{0,96},{32,0},{64,32},{96,64},{1,97},{33,1},{65,33},{97,65},{2,98}... | collective-permute-start | bytes 884744 | tf_op jit(solution)/shard_map/ppermute | solution.py:135
  511.3 86.9 %collective-permute-start.31 = (bf16[6,64,384]{2,1,0:T(8,128)(2,1)S(1)}, bf16[6,64,384]{2,1,0:T(8,128)(2,1)S(1)}, u32[]{:S(2)}, u32[]{:S(2)}) collective-permute-start(bf16[6,64,384]{2,1,0:T(8,128)(2,1)S(1)} %get-tuple-element.308), channel_id=1, source_target_pairs={{0,32},{32,64},{64,96},{96,0},{1,33},{33,65},{65,97},{97,1},{2,34}... | collective-permute-start | bytes 884744 | tf_op jit(solution)/shard_map/ppermute | solution.py:134
  514.3 83.8 %collective-permute-start.32 = (bf16[6,64,384]{2,1,0:T(8,128)(2,1)S(1)}, bf16[6,64,384]{2,1,0:T(8,128)(2,1)S(1)}, u32[]{:S(2)}, u32[]{:S(2)}) collective-permute-start(bf16[6,64,384]{2,1,0:T(8,128)(2,1)S(1)} %get-tuple-element.310), channel_id=1, source_target_pairs={{0,64},{32,96},{64,0},{96,32},{1,65},{33,97},{65,1},{97,33},{2,66}... | collective-permute-start | bytes 884744 | tf_op jit(solution)/shard_map/ppermute | solution.py:133
  521.4 76.8 %copy-start.2 = (bf16[16,64,384]{2,1,0:T(8,128)(2,1)S(1)}, bf16[16,64,384]{2,1,0:T(8,128)(2,1)}, u32[]{:S(2)}) copy-start(bf16[16,64,384]{2,1,0:T(8,128)(2,1)} %copy-done.1) | copy-start | bytes 2359300
  602.4 18.5 %collective-permute-start.10 = (bf16[2,64,384]{2,1,0:T(8,128)(2,1)S(1)}, bf16[2,64,384]{2,1,0:T(8,128)(2,1)S(1)}, u32[]{:S(2)}, u32[]{:S(2)}) collective-permute-start(bf16[2,64,384]{2,1,0:T(8,128)(2,1)S(1)} %get-tuple-element.909), channel_id=1, source_target_pairs={{0,32},{32,64},{64,96},{96,0},{1,33},{33,65},{65,97},{97,1},{2,34}... | collective-permute-start | bytes 294920 | tf_op jit(solution)/shard_map/while/body/ppermute | solution.py:134
  610.3 18.2 %collective-permute-start.11 = (bf16[2,64,384]{2,1,0:T(8,128)(2,1)S(1)}, bf16[2,64,384]{2,1,0:T(8,128)(2,1)S(1)}, u32[]{:S(2)}, u32[]{:S(2)}) collective-permute-start(bf16[2,64,384]{2,1,0:T(8,128)(2,1)S(1)} %get-tuple-element.910), channel_id=1, source_target_pairs={{0,64},{32,96},{64,0},{96,32},{1,65},{33,97},{65,1},{97,33},{2,66}... | collective-permute-start | bytes 294920 | tf_op jit(solution)/shard_map/while/body/ppermute | solution.py:133
  617.8 10.7 %collective-permute-start.9 = (bf16[2,64,384]{2,1,0:T(8,128)(2,1)S(1)}, bf16[2,64,384]{2,1,0:T(8,128)(2,1)S(1)}, u32[]{:S(2)}, u32[]{:S(2)}) collective-permute-start(bf16[2,64,384]{2,1,0:T(8,128)(2,1)S(1)} %get-tuple-element.908), channel_id=1, source_target_pairs={{0,96},{32,0},{64,32},{96,64},{1,97},{33,1},{65,33},{97,65},{2,98}... | collective-permute-start | bytes 294920 | tf_op jit(solution)/shard_map/while/body/ppermute | solution.py:135
  631.7 6.7 copy-start.3
  631.7 36.0 %all-to-all-start.11 = ((bf16[16,64,384]{2,1,0:T(8,128)(2,1)}), bf16[16,64,384]{2,1,0:T(8,128)(2,1)S(1)}, u32[]{:S(2)}, u32[]{:S(2)}) async-start(bf16[16,64,384]{2,1,0:T(8,128)(2,1)} %get-tuple-element.314), calls=%async_computation.11 | async-start | bytes 1572864 | tf_op jit(solution)/shard_map/all_to_all | solution.py:140
  639.8 17.5 %collective-permute-start.12 = (bf16[2,64,384]{2,1,0:T(8,128)(2,1)S(1)}, bf16[2,64,384]{2,1,0:T(8,128)(2,1)S(1)}, u32[]{:S(2)}, u32[]{:S(2)}) collective-permute-start(bf16[2,64,384]{2,1,0:T(8,128)(2,1)S(1)} %get-tuple-element.922), channel_id=1, source_target_pairs={{0,96},{32,0},{64,32},{96,64},{1,97},{33,1},{65,33},{97,65},{2,98}... | collective-permute-start | bytes 294920 | tf_op jit(solution)/shard_map/while/body/ppermute | solution.py:135
  641.7 15.5 %collective-permute-start.13 = (bf16[2,64,384]{2,1,0:T(8,128)(2,1)S(1)}, bf16[2,64,384]{2,1,0:T(8,128)(2,1)S(1)}, u32[]{:S(2)}, u32[]{:S(2)}) collective-permute-start(bf16[2,64,384]{2,1,0:T(8,128)(2,1)S(1)} %get-tuple-element.923), channel_id=1, source_target_pairs={{0,32},{32,64},{64,96},{96,0},{1,33},{33,65},{65,97},{97,1},{2,34}... | collective-permute-start | bytes 294920 | tf_op jit(solution)/shard_map/while/body/ppermute | solution.py:134
  649.0 16.0 %collective-permute-start.14 = (bf16[2,64,384]{2,1,0:T(8,128)(2,1)S(1)}, bf16[2,64,384]{2,1,0:T(8,128)(2,1)S(1)}, u32[]{:S(2)}, u32[]{:S(2)}) collective-permute-start(bf16[2,64,384]{2,1,0:T(8,128)(2,1)S(1)} %get-tuple-element.924), channel_id=1, source_target_pairs={{0,64},{32,96},{64,0},{96,32},{1,65},{33,97},{65,1},{97,33},{2,66}... | collective-permute-start | bytes 294920 | tf_op jit(solution)/shard_map/while/body/ppermute | solution.py:133
  667.7 6.9 copy-start.11
  667.7 6.9 copy-start.13
  667.7 17.3 %all-to-all-start.12 = ((bf16[16,64,384]{2,1,0:T(8,128)(2,1)}), bf16[16,64,384]{2,1,0:T(8,128)(2,1)}, u32[]{:S(2)}, u32[]{:S(2)}) async-start(bf16[16,64,384]{2,1,0:T(8,128)(2,1)} %get-tuple-element.315), calls=%async_computation.12 | async-start | bytes 1572864 | tf_op jit(solution)/shard_map/all_to_all | solution.py:140
  678.7 6.4 copy-start.19
  678.7 6.4 copy-start.28
  (22 other events, 54.4 us)

commit v4 on v3

v4 whole, which is shorter than its diff:
```python
import functools

import jax
import jax.numpy as jnp
from jax import lax
from jax.experimental import pallas as pl
from jax.experimental.pallas import tpu as pltpu
from jax.sharding import Mesh, PartitionSpec as P

D = 1024
FF = 3072
HID = 384
REPLICAS = 64
N_TENSOR = 8
COLS = D // N_TENSOR
PLANE = 16
PLANES = 4
ROUNDS = 2
IN_SCALE = D**-0.5
HID_SCALE = FF**-0.5

inner_rate = 1.0
outer_rate = 0.5
momentum_rate = 0.9

REPLICA = ("x", "h", "y")
FLAT = ("x", "y")
TENSOR = ("l", "c")

NEXT = 5
FAR = 4
VMEM = 48 << 20


def routes(partners):
    me = lax.axis_index("h")
    ids = jnp.arange(REPLICAS, dtype=jnp.int32)
    plane = (ids // 4) % PLANES
    flat = (ids // PLANE) * 4 + ids % 4
    to_plane = (partners // 4) % PLANES
    off = (to_plane - plane + PLANES) % PLANES
    same = (plane[:, None] == plane[None, :]) & (flat[None, :] < flat[:, None])
    rank = jnp.sum((same & (off[:, :, None] == off[:, None, :])).astype(jnp.int32), axis=2)
    places = jnp.arange(PLANE, dtype=jnp.int32)
    slots = places
    offs = jnp.array([1, 3, 2], jnp.int32)
    here = (plane == me)[None, None, None, :]
    sends = here & (off[:, None, None, :] == offs[None, :, None, None])
    sends = sends & (rank[:, None, None, :] == slots[None, None, :, None])
    send_index = jnp.sum(jnp.where(sends, flat, 0), axis=3)
    home = (places // 4) * PLANE + me * 4 + places % 4
    wanted = partners[:, None, :] == home[None, :, None]
    come_from = (plane[None, :] - me + PLANES) % PLANES
    kind = jnp.sum(jnp.where(wanted, come_from[:, None, :], 0), axis=2)
    place = jnp.where(off == 0, flat[None, :], rank)
    slot = jnp.sum(jnp.where(wanted, place[:, None, :], 0), axis=2)
    where = jnp.stack([kind, slot], axis=1)
    next_trips = jnp.max(jnp.where(off % 2 == 1, rank + 1 - NEXT, 0), axis=1)
    far_trips = jnp.max(jnp.where(off == 2, rank + 1 - FAR, 0), axis=1)
    return [(send_index[r], where[r], next_trips[r], far_trips[r]) for r in range(ROUNDS)]


def kernel_call(kernel, out_shape, index_args, args, name):
    scalars = [pl.BlockSpec(memory_space=pltpu.SMEM)] * len(index_args)
    whole = pl.BlockSpec(memory_space=pltpu.VMEM)
    size = sum(a.size * a.dtype.itemsize for a in (*args, *out_shape))
    return pl.pallas_call(
        kernel,
        out_shape=out_shape,
        in_specs=scalars + [whole] * len(args),
        out_specs=(whole,) * len(out_shape),
        compiler_params=pltpu.CompilerParams(vmem_limit_bytes=VMEM),
        cost_estimate=pl.CostEstimate(flops=size, bytes_accessed=size, transcendentals=0),
        name=name,
    )(*index_args, *args)


def pick_kernel(index, chunks, *outs):
    for o, out in enumerate(outs):

        @pl.loop(0, out.shape[0])
        def _(k, o=o, out=out):
            out[k] = chunks[index[o, k]]


def pick(index, chunks, counts):
    out_shape = tuple(jax.ShapeDtypeStruct((n, *chunks.shape[1:]), chunks.dtype) for n in counts)
    return kernel_call(pick_kernel, out_shape, (index,), (chunks,), "pick")


def merge_kernel(kinds, where, low, before, *refs):
    sources, out = refs[:-1], refs[-1]

    @pl.loop(0, PLANE)
    def _(d):
        kind, slot = where[0, d], where[1, d]
        out[d] = before[d]
        for i, (number, source) in enumerate(zip(kinds, sources)):
            at = slot - low[i]

            @pl.when((kind == number) & (at >= 0) & (at < source.shape[0]))
            def _(source=source, at=at):
                out[d] = source[at]


def merge(where, low, before, sources):
    kernel = functools.partial(merge_kernel, tuple(sources))
    out_shape = (jax.ShapeDtypeStruct(before.shape, before.dtype),)
    low = jnp.stack([jnp.int32(0) + low] * len(sources))
    return kernel_call(kernel, out_shape, (where, low), (before, *sources.values()), "merge")[0]


def step_by(n):
    return [(i, (i + n) % PLANES) for i in range(PLANES)]


def hop(sends):
    steps = {3: 1, 1: -1, 2: 2}
    return {k: lax.ppermute(s, "h", step_by(steps[k])) for k, s in sends.items()}


def depart(index, share):
    return dict(zip((3, 1, 2), pick(index, share, (NEXT, NEXT, FAR))))


def late(route, share, after):
    send_index, where, next_trips, far_trips = route
    start, _ = lax.optimization_barrier((jnp.int32(0), after))

    def next_one(state):
        i, placed = state
        at = NEXT + i
        index = lax.dynamic_slice(send_index, (0, at), (2, 1))
        came = hop(dict(zip((3, 1), pick(index, share, (1, 1)))))
        return i + 1, merge(where, at, placed, came)

    def far_one(state):
        i, placed = state
        at = FAR + i
        index = lax.dynamic_slice(send_index, (2, at), (1, 1))
        came = hop(dict(zip((2,), pick(index, share, (1,)))))
        return i + 1, merge(where, at, placed, came)

    _, placed = lax.while_loop(lambda s: s[0] < next_trips, next_one, (start, share))
    _, placed = lax.while_loop(lambda s: s[0] < far_trips, far_one, (start, placed))
    return placed


def over_plane(chunks):
    return lax.all_to_all(chunks, FLAT, 0, 0, tiled=True)


def swap(route, arrays):
    tie = lax.optimization_barrier
    shares, sent, came, done = [], [], [], []
    for a in arrays:
        a = a.reshape(PLANE, a.shape[0] // PLANE, a.shape[1])
        if shares:
            a, _ = tie((a, shares[-1]))
        shares.append(over_plane(a))
        sent.append(depart(route[0], shares[-1]))
        came.append(hop(sent[-1]))
    for i, share in enumerate(shares):
        placed = late(route, share, (sent[i], sent[min(i + 1, len(sent) - 1)]))
        parts, placed, _ = tie((came[i], placed, done))
        parts = {0: share, **parts}
        done = done + [over_plane(merge(route[1], 0, placed, parts))]
    return [d.reshape(a.shape) for d, a in zip(done, arrays)]


rows = (((0,), (0,)), ((), ()))


def grad(a, b):
    return lax.dot_general(a, b, rows, preferred_element_type=jnp.float32)


def local_step(weights, inputs, in_cols, out_cols):
    both, down = weights
    pre = jnp.dot(inputs, both, preferred_element_type=jnp.float32) * IN_SCALE
    gate_pre, up_value = pre[:, :HID], pre[:, HID:]
    sigmoid_gate = jax.nn.sigmoid(gate_pre)
    active = gate_pre * sigmoid_gate
    hidden = (active * up_value).astype(jnp.bfloat16)
    term = (
        lax.dot_general(hidden, down, (((1,), (1,)), ((), ())), preferred_element_type=jnp.float32)
        * HID_SCALE
    )
    blocks = term.astype(jnp.bfloat16).reshape(-1, N_TENSOR, COLS).transpose(1, 0, 2)
    terms = lax.all_to_all(blocks, TENSOR, 0, 0, tiled=True)
    branch = jnp.sum(terms.astype(jnp.float32), axis=0)
    error_cols = (in_cols.astype(jnp.float32) + branch - out_cols.astype(jnp.float32)).astype(
        jnp.bfloat16
    )
    errors = lax.all_gather(error_cols, TENSOR, axis=1, tiled=True)
    back = jnp.dot(errors, down, preferred_element_type=jnp.float32) * HID_SCALE
    delta_gate = back * up_value * sigmoid_gate * (1.0 + gate_pre * (1.0 - sigmoid_gate))
    delta_up = back * active
    deltas = jnp.concatenate([delta_gate, delta_up], axis=1).astype(jnp.bfloat16)
    gradients = (grad(inputs, deltas) * IN_SCALE, grad(errors, hidden) * HID_SCALE)
    return tuple(
        (w.astype(jnp.float32) - inner_rate * g).astype(jnp.bfloat16)
        for w, g in zip(weights, gradients)
    )


def partner_copy(route, arrays):
    return swap(route, arrays[::-1])[::-1]


def outer_update(weight, stepped, partner_step):
    weight = weight.astype(jnp.float32)
    pair_mean = 0.5 * (stepped.astype(jnp.float32) + partner_step.astype(jnp.float32))
    outer_grad = weight - pair_mean
    moment_new = outer_grad
    updated = weight - outer_rate * (momentum_rate * moment_new + outer_grad)
    return updated.astype(jnp.bfloat16), moment_new.astype(jnp.bfloat16)


def make_share(stepped, moment):
    return (0.475 * stepped.astype(jnp.float32) - 0.2025 * moment.astype(jnp.float32)).astype(
        jnp.bfloat16
    )


def final_update(weight, stepped, moment, partner_share):
    updated = (
        0.05 * weight.astype(jnp.float32)
        + 0.475 * stepped.astype(jnp.float32)
        - 0.2025 * moment.astype(jnp.float32)
        + partner_share.astype(jnp.float32)
    )
    return updated.astype(jnp.bfloat16)


def body(w_gate, w_up, w_down, pool, rows_index, partners):
    weights = (jnp.concatenate([w_gate[0], w_up[0]], axis=1), w_down[0].T)
    first, last = routes(partners)
    picked = jnp.take(pool[0], rows_index[0].reshape(-1), axis=0)
    picked = picked.reshape(ROUNDS, 2, -1, COLS)
    in_cols, out_cols = picked[:, 0], picked[:, 1]
    inputs = lax.all_gather(in_cols, TENSOR, axis=2, tiled=True)

    stepped = local_step(weights, inputs[0], in_cols[0], out_cols[0])
    theirs = partner_copy(first, stepped)
    results = [outer_update(*each) for each in zip(weights, stepped, theirs)]
    weights = tuple(r[0] for r in results)
    moments = tuple(r[1] for r in results)

    stepped = local_step(weights, inputs[1], in_cols[1], out_cols[1])
    shares = tuple(make_share(s, m) for s, m in zip(stepped, moments))
    theirs = partner_copy(last, shares)
    new = [final_update(*each) for each in zip(weights, stepped, moments, theirs)]
    both, down = new
    return both[None, :, :HID], both[None, :, HID:], down.T[None]


def solution(mesh):
    grid = Mesh(mesh.devices.reshape(4, 4, 4, 4, 2), ("x", "h", "y", "l", "c"))
    return jax.shard_map(
        body,
        mesh=grid,
        in_specs=(
            P(REPLICA, None, TENSOR),
            P(REPLICA, None, TENSOR),
            P(REPLICA, TENSOR, None),
            P(REPLICA, None, TENSOR),
            P(REPLICA, None, None, None),
            P(),
        ),
        out_specs=(
            P(REPLICA, None, TENSOR),
            P(REPLICA, None, TENSOR),
            P(REPLICA, TENSOR, None),
        ),
        check_vma=False,
    )
```

time: 700 us -> 676 us (0.966)
  the two profiles are of different devices: /device:TPU:1 before, /device:TPU:32 now
where the time goes in v4:
time: 676 us; the launch traced here: 673 us
  waiting for transfers between devices  247 us (37%)
  starting transfers between devices  240 us (36%)
  Pallas kernels  57.1 us (8%)
  blocking collectives  52.1 us (8%)
  local copies, waits for them, and re-layouts  28 us (4%)
  other arithmetic  19.4 us (3%)
  matrix products  16.7 us (2%)
  loops' own time  12 us (2%)
    ppermute x30, starting transfers between devices, hop(): lax.ppermute(s, 'h', step_by(steps[k]))  187 us
    ppermute x30, waiting for transfers between devices, hop(): lax.ppermute(s, 'h', step_by(steps[k]))  186 us
    pallas_call x28, Pallas kernels, kernel_call(): pl.pallas_call(kernel, out_shape=out_shape, in_specs=scalars + [whole] *...  57.1 us
    all_to_all x8, waiting for transfers between devices, over_plane(): return lax.all_to_all(chunks, FLAT, 0, 0, tiled=True)  54.3 us
    all_to_all x8, starting transfers between devices, over_plane(): return lax.all_to_all(chunks, FLAT, 0, 0, tiled=True)  46 us
    all_gather x2, blocking collectives, local_step(): errors = lax.all_gather(error_cols, TENSOR, axis=1, tiled=True)  24.8 us
    all_gather x1, blocking collectives, body(): inputs = lax.all_gather(in_cols, TENSOR, axis=2, tiled=True)  16.4 us
    unnamed x72, local copies, waits for them, and re-layouts  15.2 us
  transfers between devices with their start and end apart: 39, of which 21 were waited for; matrix products, arithmetic and copies ran while one was open for 6% of the time, Pallas kernels for 7%

profile of v4, /device:TPU:32, one launch (start us, length us, event | category | flops | bytes accessed | tf_op | source)
XLA Modules:
  0.0 673.2 jit_solution(18021965561352929932)
XLA Ops:
  3.7 16.4 %all-gather = bf16[2,1,128,1024]{3,2,1,0:T(8,128)(2,1)S(1)} all-gather(bf16[2,1,128,128]{3,2,1,0:T(8,128)(2,1)S(1)} %slice.97), channel_id=2, replica_groups=mesh['x'=4,'h'=4,'y'=4,'l'=4,'c'=2] {'l','c'}, dimensions={3}, use_global_device_ids=true | all-gather | bytes 589824 | tf_op jit(solution)/shard_map/all_gather | solution.py:242
  22.5 6.4 all-to-all-start
  30.6 6.2 all-to-all-done
  37.7 12.4 %all_gather.10 = bf16[128,1024]{1,0:T(8,128)(2,1)S(1)} all-gather(bf16[128,128]{1,0:T(8,128)(2,1)S(1)} %fusion.38), channel_id=1, replica_groups=mesh['x'=4,'h'=4,'y'=4,'l'=4,'c'=2] {'l','c'}, dimensions={1}, use_global_device_ids=true | all-gather | bytes 294912 | tf_op jit(solution)/shard_map/all_gather | solution.py:195
  52.2 4.3 all-to-all-start.1
  59.9 12.0 %all-to-all-done.1.chunks.refs_0_ = bf16[16,64,384]{2,1,0:T(8,128)(2,1)} async-done(((bf16[16,64,384]{2,1,0:T(8,128)(2,1)}), bf16[16,64,384]{2,1,0:T(8,128)(2,1)}, u32[]{:S(2)}, u32[]{:S(2)}) %all-to-all-start.1) | async-done | bytes 786464 | tf_op jit(solution)/shard_map/all_to_all | solution.py:150
  72.0 4.5 all-to-all-start.2
  78.6 9.8 %collective-permute-start.15 = (bf16[5,64,384]{2,1,0:T(8,128)(2,1)S(1)}, bf16[5,64,384]{2,1,0:T(8,128)(2,1)S(1)}, u32[]{:S(2)}, u32[]{:S(2)}) collective-permute-start(bf16[5,64,384]{2,1,0:T(8,128)(2,1)S(1)} %get-tuple-element.660), channel_id=1, source_target_pairs={{0,96},{32,0},{64,32},{96,64},{1,97},{33,1},{65,33},{97,65},{2,98}... | collective-permute-start | bytes 737288 | tf_op jit(solution)/shard_map/ppermute | solution.py:119
  90.9 10.8 %collective-permute-start.16 = (bf16[4,64,384]{2,1,0:T(8,128)(2,1)S(1)}, bf16[4,64,384]{2,1,0:T(8,128)(2,1)S(1)}, u32[]{:S(2)}, u32[]{:S(2)}) collective-permute-start(bf16[4,64,384]{2,1,0:T(8,128)(2,1)S(1)} %get-tuple-element.661), channel_id=1, source_target_pairs={{0,64},{32,96},{64,0},{96,32},{1,65},{33,97},{65,1},{97,33},{2,66}... | collective-permute-start | bytes 589832 | tf_op jit(solution)/shard_map/ppermute | solution.py:119
  107.1 3.8 collective-permute-start.12
  110.9 5.9 collective-permute-start.14
  116.9 9.4 %collective-permute-start.13 = (bf16[4,64,768]{2,1,0:T(8,128)(2,1)}, bf16[4,64,768]{2,1,0:T(8,128)(2,1)S(1)}, u32[]{:S(2)}, u32[]{:S(2)}) collective-permute-start(bf16[4,64,768]{2,1,0:T(8,128)(2,1)} %get-tuple-element.655), channel_id=1, source_target_pairs={{0,64},{32,96},{64,0},{96,32},{1,65},{33,97},{65,1},{97,33},{2,66}... | collective-permute-start | bytes 1179656 | tf_op jit(solution)/shard_map/ppermute | solution.py:119
  126.4 90.6 %while.98 = (s32[]{:T(128)}, bf16[16,64,384]{2,1,0:T(8,128)(2,1)}, s32[]{:T(128)}, s32[3,16]{1,0:T(4,128)S(1)}, bf16[16,64,384]{2,1,0:T(8,128)(2,1)}, /*index=5*...) while((s32[]{:T(128)}, bf16[16,64,384]{2,1,0:T(8,128)(2,1)}, s32[]{:T(128)}, ...), condition=%wide.region_12.13_spmd, body=%wide.region_11.12_spmd.sunk | while | flops 2555912 | bytes 4522243 | solution.py:144
  130.2 7.8 %collective-permute-start.4 = (bf16[1,64,384]{2,1,0:T(8,128)(2,1)S(1)}, bf16[1,64,384]{2,1,0:T(8,128)(2,1)S(1)}, u32[]{:S(2)}, u32[]{:S(2)}) collective-permute-start(bf16[1,64,384]{2,1,0:T(8,128)(2,1)S(1)} %get-tuple-element.1110), channel_id=1, source_target_pairs={{0,96},{32,0},{64,32},{96,64},{1,97},{33,1},{65,33},{97,65},{2,98}... | collective-permute-start | bytes 147464 | tf_op jit(solution)/shard_map/while/body/ppermute | solution.py:119
  139.2 75.2 %collective-permute-done.3.refs_0_ = bf16[1,64,384]{2,1,0:T(8,128)(2,1)S(1)} collective-permute-done((bf16[1,64,384]{2,1,0:T(8,128)(2,1)S(1)}, bf16[1,64,384]{2,1,0:T(8,128)(2,1)S(1)}, u32[]{:S(2)}, u32[]{:S(2)}) %collective-permute-start.3) | collective-permute-done | bytes 49184 | tf_op jit(solution)/shard_map/while/body/ppermute | solution.py:119
  217.0 20.7 %while.99 = (s32[]{:T(128)}, bf16[16,64,384]{2,1,0:T(8,128)(2,1)}, s32[]{:T(128)}, s32[3,16]{1,0:T(4,128)S(1)}, bf16[16,64,384]{2,1,0:T(8,128)(2,1)}, /*index=5*...) while((s32[]{:T(128)}, bf16[16,64,384]{2,1,0:T(8,128)(2,1)}, s32[]{:T(128)}, ...), condition=%wide.region_14.15_spmd, body=%wide.region_13.14_spmd.sunk | while | flops 2457606 | bytes 4227271 | solution.py:145
  220.1 5.8 collective-permute-start.5
  227.1 8.1 %collective-permute-done.5.refs_0_ = bf16[1,64,384]{2,1,0:T(8,128)(2,1)S(1)} collective-permute-done((bf16[1,64,384]{2,1,0:T(8,128)(2,1)S(1)}, bf16[1,64,384]{2,1,0:T(8,128)(2,1)S(1)}, u32[]{:S(2)}, u32[]{:S(2)}) %collective-permute-start.5) | collective-permute-done | bytes 49184 | tf_op jit(solution)/shard_map/while/body/ppermute | solution.py:119
  240.8 7.3 %all-to-all-start.3 = ((bf16[16,64,384]{2,1,0:T(8,128)(2,1)}), bf16[16,64,384]{2,1,0:T(8,128)(2,1)}, u32[]{:S(2)}, u32[]{:S(2)}) async-start(bf16[16,64,384]{2,1,0:T(8,128)(2,1)} %merge.36), calls=%async_computation.3 | async-start | bytes 1572864 | tf_op jit(solution)/shard_map/all_to_all | solution.py:150
  250.9 20.4 %while.96 = (s32[]{:T(128)}, bf16[16,64,768]{2,1,0:T(8,128)(2,1)}, s32[]{:T(128)}, s32[3,16]{1,0:T(4,128)S(1)}, bf16[16,64,768]{2,1,0:T(8,128)(2,1)}, /*index=5*...) while((s32[]{:T(128)}, bf16[16,64,768]{2,1,0:T(8,128)(2,1)}, s32[]{:T(128)}, ...), condition=%wide.region_7.8_spmd, body=%wide.region_6.7_spmd.sunk | while | flops 5111816 | bytes 15335711 | solution.py:144
  255.4 7.5 %collective-permute-start.1 = (bf16[1,64,768]{2,1,0:T(8,128)(2,1)S(1)}, bf16[1,64,768]{2,1,0:T(8,128)(2,1)S(1)}, u32[]{:S(2)}, u32[]{:S(2)}) collective-permute-start(bf16[1,64,768]{2,1,0:T(8,128)(2,1)S(1)} %get-tuple-element.1096), channel_id=1, source_target_pairs={{0,96},{32,0},{64,32},{96,64},{1,97},{33,1},{65,33},{97,65},{2,98}... | collective-permute-start | bytes 294920 | tf_op jit(solution)/shard_map/while/body/ppermute | solution.py:119
  264.5 3.9 collective-permute-done.1.refs_1_
  271.3 23.9 %while.97 = (s32[]{:T(128)}, bf16[16,64,768]{2,1,0:T(8,128)(2,1)}, s32[]{:T(128)}, s32[3,16]{1,0:T(4,128)S(1)}, bf16[16,64,768]{2,1,0:T(8,128)(2,1)}, /*index=5*...) while((s32[]{:T(128)}, bf16[16,64,768]{2,1,0:T(8,128)(2,1)}, s32[]{:T(128)}, ...), condition=%wide.region_10.11_spmd, body=%wide.region_9.10_spmd.sunk | while | flops 4915206 | bytes 14745827 | solution.py:145
  274.7 8.8 %collective-permute-start.2 = (bf16[1,64,768]{2,1,0:T(8,128)(2,1)S(1)}, bf16[1,64,768]{2,1,0:T(8,128)(2,1)S(1)}, u32[]{:S(2)}, u32[]{:S(2)}) collective-permute-start(bf16[1,64,768]{2,1,0:T(8,128)(2,1)S(1)} %pick.41), channel_id=1, source_target_pairs={{0,64},{32,96},{64,0},{96,32},{1,65},{33,97},{65,1},{97,33},{2,66}... | collective-permute-start | bytes 294920 | tf_op jit(solution)/shard_map/while/body/ppermute | solution.py:119
  283.6 8.8 %collective-permute-done.2.refs_0_ = bf16[1,64,768]{2,1,0:T(8,128)(2,1)S(1)} collective-permute-done((bf16[1,64,768]{2,1,0:T(8,128)(2,1)S(1)}, bf16[1,64,768]{2,1,0:T(8,128)(2,1)S(1)}, u32[]{:S(2)}, u32[]{:S(2)}) %collective-permute-start.2) | collective-permute-done | bytes 98336 | tf_op jit(solution)/shard_map/while/body/ppermute | solution.py:119
  295.2 4.0 merge.37
  299.2 6.1 all-to-all-start.4
  308.2 16.1 %all-to-all-done.4 = bf16[16,64,768]{2,1,0:T(8,128)(2,1)S(1)} async-done(((bf16[16,64,768]{2,1,0:T(8,128)(2,1)}), bf16[16,64,768]{2,1,0:T(8,128)(2,1)S(1)}, u32[]{:S(2)}, u32[]{:S(2)}) %all-to-all-start.4) | async-done | bytes 1572896 | tf_op jit(solution)/shard_map/all_to_all | solution.py:150
  324.4 3.6 fusion.6
  330.1 11.0 %all_to_all.50 = bf16[8,128,128]{2,1,0:T(8,128)(2,1)S(1)} all-to-all(bf16[8,128,128]{2,1,0:T(8,128)(2,1)S(1)} %bitcast.177), channel_id=1, replica_groups=mesh['x'=4,'h'=4,'y'=4,'l'=4,'c'=2] {'l','c'}, dimensions={0} | all-to-all | bytes 524288 | tf_op jit(solution)/shard_map/all_to_all | solution.py:190
  341.2 12.4 %all_gather.11 = bf16[128,1024]{1,0:T(8,128)(2,1)S(1)} all-gather(bf16[128,128]{1,0:T(8,128)(2,1)S(1)} %fusion.37), channel_id=1, replica_groups=mesh['x'=4,'h'=4,'y'=4,'l'=4,'c'=2] {'l','c'}, dimensions={1}, use_global_device_ids=true | all-gather | bytes 294912 | tf_op jit(solution)/shard_map/all_gather | solution.py:195
  353.6 3.4 subtract_convert_fusion.1
  357.0 4.5 all-to-all-start.6
  363.4 4.8 subtract_convert_fusion
  368.2 8.5 %all-to-all-done.6.chunks.refs_0_ = bf16[16,64,384]{2,1,0:T(8,128)(2,1)} async-done(((bf16[16,64,384]{2,1,0:T(8,128)(2,1)}), bf16[16,64,384]{2,1,0:T(8,128)(2,1)}, u32[]{:S(2)}, u32[]{:S(2)}) %all-to-all-start.6) | async-done | bytes 786464 | tf_op jit(solution)/shard_map/all_to_all | solution.py:150
  376.7 4.4 all-to-all-start.7
  382.4 8.0 %collective-permute-start.21 = (bf16[5,64,384]{2,1,0:T(8,128)(2,1)S(1)}, bf16[5,64,384]{2,1,0:T(8,128)(2,1)S(1)}, u32[]{:S(2)}, u32[]{:S(2)}) collective-permute-start(bf16[5,64,384]{2,1,0:T(8,128)(2,1)S(1)} %get-tuple-element.681), channel_id=1, source_target_pairs={{0,96},{32,0},{64,32},{96,64},{1,97},{33,1},{65,33},{97,65},{2,98}... | collective-permute-start | bytes 737288 | tf_op jit(solution)/shard_map/ppermute | solution.py:119
  392.3 13.0 %collective-permute-start.22 = (bf16[4,64,384]{2,1,0:T(8,128)(2,1)S(1)}, bf16[4,64,384]{2,1,0:T(8,128)(2,1)S(1)}, u32[]{:S(2)}, u32[]{:S(2)}) collective-permute-start(bf16[4,64,384]{2,1,0:T(8,128)(2,1)S(1)} %get-tuple-element.682), channel_id=1, source_target_pairs={{0,64},{32,96},{64,0},{96,32},{1,65},{33,97},{65,1},{97,33},{2,66}... | collective-permute-start | bytes 589832 | tf_op jit(solution)/shard_map/ppermute | solution.py:119
  410.1 4.8 collective-permute-start.18
  414.9 5.0 collective-permute-start.20
  422.7 7.6 %collective-permute-start.19 = (bf16[4,64,768]{2,1,0:T(8,128)(2,1)}, bf16[4,64,768]{2,1,0:T(8,128)(2,1)S(1)}, u32[]{:S(2)}, u32[]{:S(2)}) collective-permute-start(bf16[4,64,768]{2,1,0:T(8,128)(2,1)} %get-tuple-element.676), channel_id=1, source_target_pairs={{0,64},{32,96},{64,0},{96,32},{1,65},{33,97},{65,1},{97,33},{2,66}... | collective-permute-start | bytes 1179656 | tf_op jit(solution)/shard_map/ppermute | solution.py:119
  430.4 126.7 %while.102 = (s32[]{:T(128)}, bf16[16,64,384]{2,1,0:T(8,128)(2,1)}, s32[]{:T(128)}, s32[3,16]{1,0:T(4,128)S(1)}, bf16[16,64,384]{2,1,0:T(8,128)(2,1)}, /*index=5...) while((s32[]{:T(128)}, bf16[16,64,384]{2,1,0:T(8,128)(2,1)}, s32[]{:T(128)}, ...), condition=%wide.region_21.22_spmd, body=%wide.region_20.21_spmd.sunk | while | flops 2555912 | bytes 4522243 | solution.py:144
  432.2 5.7 collective-permute-start.10
  437.9 4.1 collective-permute-start.9
  443.2 12.7 %collective-permute-done.10.refs_1_ = bf16[1,64,384]{2,1,0:T(8,128)(2,1)S(1)} collective-permute-done((bf16[1,64,384]{2,1,0:T(8,128)(2,1)S(1)}, bf16[1,64,384]{2,1,0:T(8,128)(2,1)S(1)}, u32[]{:S(2)}, u32[]{:S(2)}) %collective-permute-start.10) | collective-permute-done | bytes 49184 | tf_op jit(solution)/shard_map/while/body/ppermute | solution.py:119
  456.0 46.1 %collective-permute-done.9.refs_0_ = bf16[1,64,384]{2,1,0:T(8,128)(2,1)S(1)} collective-permute-done((bf16[1,64,384]{2,1,0:T(8,128)(2,1)S(1)}, bf16[1,64,384]{2,1,0:T(8,128)(2,1)S(1)}, u32[]{:S(2)}, u32[]{:S(2)}) %collective-permute-start.9) | collective-permute-done | bytes 49184 | tf_op jit(solution)/shard_map/while/body/ppermute | solution.py:119
  505.8 20.4 %collective-permute-start.10 = (bf16[1,64,384]{2,1,0:T(8,128)(2,1)S(1)}, bf16[1,64,384]{2,1,0:T(8,128)(2,1)S(1)}, u32[]{:S(2)}, u32[]{:S(2)}) collective-permute-start(bf16[1,64,384]{2,1,0:T(8,128)(2,1)S(1)} %get-tuple-element.1138), channel_id=1, source_target_pairs={{0,96},{32,0},{64,32},{96,64},{1,97},{33,1},{65,33},{97,65},{2,98}... | collective-permute-start | bytes 147464 | tf_op jit(solution)/shard_map/while/body/ppermute | solution.py:119
  529.4 7.5 %collective-permute-done.9.refs_0_ = bf16[1,64,384]{2,1,0:T(8,128)(2,1)S(1)} collective-permute-done((bf16[1,64,384]{2,1,0:T(8,128)(2,1)S(1)}, bf16[1,64,384]{2,1,0:T(8,128)(2,1)S(1)}, u32[]{:S(2)}, u32[]{:S(2)}) %collective-permute-start.9) | collective-permute-done | bytes 49184 | tf_op jit(solution)/shard_map/while/body/ppermute | solution.py:119
  540.7 3.5 collective-permute-start.10
  544.2 6.3 collective-permute-start.9
  557.6 3.1 merge.38
  560.8 6.6 all-to-all-start.8
  570.0 61.0 %while.100 = (s32[]{:T(128)}, bf16[16,64,768]{2,1,0:T(8,128)(2,1)}, s32[]{:T(128)}, s32[3,16]{1,0:T(4,128)S(1)}, bf16[16,64,768]{2,1,0:T(8,128)(2,1)}, /*index=5...) while((s32[]{:T(128)}, bf16[16,64,768]{2,1,0:T(8,128)(2,1)}, s32[]{:T(128)}, ...), condition=%wide.region_17.18_spmd, body=%wide.region_16.17_spmd.sunk | while | flops 5111816 | bytes 15335711 | solution.py:144
  572.3 5.0 collective-permute-start.6
  577.2 4.8 collective-permute-start.7
  585.4 3.6 collective-permute-done.7.refs_1_
  596.4 6.8 %collective-permute-start.7 = (bf16[1,64,768]{2,1,0:T(8,128)(2,1)S(1)}, bf16[1,64,768]{2,1,0:T(8,128)(2,1)S(1)}, u32[]{:S(2)}, u32[]{:S(2)}) collective-permute-start(bf16[1,64,768]{2,1,0:T(8,128)(2,1)S(1)} %get-tuple-element.1124), channel_id=1, source_target_pairs={{0,96},{32,0},{64,32},{96,64},{1,97},{33,1},{65,33},{97,65},{2,98}... | collective-permute-start | bytes 294920 | tf_op jit(solution)/shard_map/while/body/ppermute | solution.py:119
  605.7 4.4 collective-permute-done.7.refs_1_
  616.9 7.3 %collective-permute-start.7 = (bf16[1,64,768]{2,1,0:T(8,128)(2,1)S(1)}, bf16[1,64,768]{2,1,0:T(8,128)(2,1)S(1)}, u32[]{:S(2)}, u32[]{:S(2)}) collective-permute-start(bf16[1,64,768]{2,1,0:T(8,128)(2,1)S(1)} %get-tuple-element.1124), channel_id=1, source_target_pairs={{0,96},{32,0},{64,32},{96,64},{1,97},{33,1},{65,33},{97,65},{2,98}... | collective-permute-start | bytes 294920 | tf_op jit(solution)/shard_map/while/body/ppermute | solution.py:119
  631.6 3.9 merge.39
  635.5 8.2 %all-to-all-start.9 = ((bf16[16,64,768]{2,1,0:T(8,128)(2,1)}), bf16[16,64,768]{2,1,0:T(8,128)(2,1)}, u32[]{:S(2)}, u32[]{:S(2)}) async-start(bf16[16,64,768]{2,1,0:T(8,128)(2,1)} %merge.39), calls=%async_computation.9 | async-start | bytes 3145728 | tf_op jit(solution)/shard_map/all_to_all | solution.py:150
  643.8 3.7 fusion.26
  649.9 17.6 %all-to-all-done.9 = bf16[16,64,768]{2,1,0:T(8,128)(2,1)} async-done(((bf16[16,64,768]{2,1,0:T(8,128)(2,1)}), bf16[16,64,768]{2,1,0:T(8,128)(2,1)}, u32[]{:S(2)}, u32[]{:S(2)}) %all-to-all-start.9) | async-done | bytes 1572896 | tf_op jit(solution)/shard_map/all_to_all | solution.py:150
  667.5 4.4 fusion.3
  (210 shorter events, 122.9 us)
Async XLA Ops:
  0.6 19.5 %copy-start.18 = (bf16[1,1024,384]{2,1,0:T(8,128)(2,1)S(1)}, bf16[1,1024,384]{2,1,0:T(8,128)(2,1)}, u32[]{:S(2)}) copy-start(bf16[1,1024,384]{2,1,0:T(8,128)(2,1)} %param.23) | copy-start | bytes 2359300
  0.7 19.5 %copy-start.16 = (bf16[1,1024,384]{2,1,0:T(8,128)(2,1)S(1)}, bf16[1,1024,384]{2,1,0:T(8,128)(2,1)}, u32[]{:S(2)}) copy-start(bf16[1,1024,384]{2,1,0:T(8,128)(2,1)} %param.24) | copy-start | bytes 2359300
  3.7 16.4 %copy-start.26 = (bf16[2,2,128,128]{3,2,1,0:T(8,128)(2,1)}, bf16[2,2,128,128]{3,2,1,0:T(8,128)(2,1)S(1)}, u32[]{:S(2)}) copy-start(bf16[2,2,128,128]{3,2,1,0:T(8,128)(2,1)S(1)} %broadcast_select_fusion) | copy-start | bytes 393220
  21.8 8.2 %copy-start.30 = (s32[2,64]{1,0:T(2,128)S(1)}, s32[2,64]{1,0:T(2,128)}, u32[]{:S(2)}) copy-start(s32[2,64]{1,0:T(2,128)} %param.28) | copy-start | bytes 1540
  22.5 14.3 %all-to-all-start = ((bf16[8,128,128]{2,1,0:T(8,128)(2,1)}), bf16[8,128,128]{2,1,0:T(8,128)(2,1)S(1)}, u32[]{:S(2)}, u32[]{:S(2)}) async-start(bf16[8,128,128]{2,1,0:T(8,128)(2,1)} %bitcast.148), calls=%async_computation | async-start | bytes 524288 | tf_op jit(solution)/shard_map/all_to_all | solution.py:190
  29.3 22.9 %copy-start.9 = (bf16[1,384,1024]{1,2,0:T(8,128)(2,1)}, bf16[1,384,1024]{1,2,0:T(8,128)(2,1)S(1)}, u32[]{:S(2)}) copy-start(bf16[1,384,1024]{1,2,0:T(8,128)(2,1)S(1)} %copy.16) | copy-start | bytes 2359300
  52.2 19.7 %all-to-all-start.1 = ((bf16[16,64,384]{2,1,0:T(8,128)(2,1)}), bf16[16,64,384]{2,1,0:T(8,128)(2,1)}, u32[]{:S(2)}, u32[]{:S(2)}) async-start(bf16[16,64,384]{2,1,0:T(8,128)(2,1)} %bitcast.26), calls=%async_computation.1 | async-start | bytes 1572864 | tf_op jit(solution)/shard_map/all_to_all | solution.py:150
  71.9 4.6 copy-start.35
  71.9 4.6 copy-start.36
  71.9 4.7 copy-start.34
  72.0 4.9 copy-start.32
  72.0 32.4 %all-to-all-start.2 = ((bf16[16,64,768]{2,1,0:T(8,128)(2,1)}), bf16[16,64,768]{2,1,0:T(8,128)(2,1)}, u32[]{:S(2)}, u32[]{:S(2)}) async-start(bf16[16,64,768]{2,1,0:T(8,128)(2,1)} %bitcast.24), calls=%async_computation.2 | async-start | bytes 3145728 | tf_op jit(solution)/shard_map/all_to_all | solution.py:150
  78.6 47.8 %collective-permute-start.15 = (bf16[5,64,384]{2,1,0:T(8,128)(2,1)S(1)}, bf16[5,64,384]{2,1,0:T(8,128)(2,1)S(1)}, u32[]{:S(2)}, u32[]{:S(2)}) collective-permute-start(bf16[5,64,384]{2,1,0:T(8,128)(2,1)S(1)} %get-tuple-element.660), channel_id=1, source_target_pairs={{0,96},{32,0},{64,32},{96,64},{1,97},{33,1},{65,33},{97,65},{2,98}... | collective-permute-start | bytes 737288 | tf_op jit(solution)/shard_map/ppermute | solution.py:119
  88.4 38.0 %collective-permute-start.17 = (bf16[5,64,384]{2,1,0:T(8,128)(2,1)S(1)}, bf16[5,64,384]{2,1,0:T(8,128)(2,1)S(1)}, u32[]{:S(2)}, u32[]{:S(2)}) collective-permute-start(bf16[5,64,384]{2,1,0:T(8,128)(2,1)S(1)} %get-tuple-element.662), channel_id=1, source_target_pairs={{0,32},{32,64},{64,96},{96,0},{1,33},{33,65},{65,97},{97,1},{2,34}... | collective-permute-start | bytes 737288 | tf_op jit(solution)/shard_map/ppermute | solution.py:119
  90.9 26.0 %collective-permute-start.16 = (bf16[4,64,384]{2,1,0:T(8,128)(2,1)S(1)}, bf16[4,64,384]{2,1,0:T(8,128)(2,1)S(1)}, u32[]{:S(2)}, u32[]{:S(2)}) collective-permute-start(bf16[4,64,384]{2,1,0:T(8,128)(2,1)S(1)} %get-tuple-element.661), channel_id=1, source_target_pairs={{0,64},{32,96},{64,0},{96,32},{1,65},{33,97},{65,1},{97,33},{2,66}... | collective-permute-start | bytes 589832 | tf_op jit(solution)/shard_map/ppermute | solution.py:119
  107.1 188.1 %collective-permute-start.12 = (bf16[5,64,768]{2,1,0:T(8,128)(2,1)}, bf16[5,64,768]{2,1,0:T(8,128)(2,1)S(1)}, u32[]{:S(2)}, u32[]{:S(2)}) collective-permute-start(bf16[5,64,768]{2,1,0:T(8,128)(2,1)} %get-tuple-element.654), channel_id=1, source_target_pairs={{0,96},{32,0},{64,32},{96,64},{1,97},{33,1},{65,33},{97,65},{2,98}... | collective-permute-start | bytes 1474568 | tf_op jit(solution)/shard_map/ppermute | solution.py:119
  110.9 184.3 %collective-permute-start.14 = (bf16[5,64,768]{2,1,0:T(8,128)(2,1)}, bf16[5,64,768]{2,1,0:T(8,128)(2,1)S(1)}, u32[]{:S(2)}, u32[]{:S(2)}) collective-permute-start(bf16[5,64,768]{2,1,0:T(8,128)(2,1)} %get-tuple-element.656), channel_id=1, source_target_pairs={{0,32},{32,64},{64,96},{96,0},{1,33},{33,65},{65,97},{97,1},{2,34}... | collective-permute-start | bytes 1474568 | tf_op jit(solution)/shard_map/ppermute | solution.py:119
  116.9 178.3 %collective-permute-start.13 = (bf16[4,64,768]{2,1,0:T(8,128)(2,1)}, bf16[4,64,768]{2,1,0:T(8,128)(2,1)S(1)}, u32[]{:S(2)}, u32[]{:S(2)}) collective-permute-start(bf16[4,64,768]{2,1,0:T(8,128)(2,1)} %get-tuple-element.655), channel_id=1, source_target_pairs={{0,64},{32,96},{64,0},{96,32},{1,65},{33,97},{65,1},{97,33},{2,66}... | collective-permute-start | bytes 1179656 | tf_op jit(solution)/shard_map/ppermute | solution.py:119
  128.2 86.2 %collective-permute-start.3 = (bf16[1,64,384]{2,1,0:T(8,128)(2,1)S(1)}, bf16[1,64,384]{2,1,0:T(8,128)(2,1)S(1)}, u32[]{:S(2)}, u32[]{:S(2)}) collective-permute-start(bf16[1,64,384]{2,1,0:T(8,128)(2,1)S(1)} %get-tuple-element.1109), channel_id=1, source_target_pairs={{0,32},{32,64},{64,96},{96,0},{1,33},{33,65},{65,97},{97,1},{2,34}... | collective-permute-start | bytes 147464 | tf_op jit(solution)/shard_map/while/body/ppermute | solution.py:119
  130.2 84.3 %collective-permute-start.4 = (bf16[1,64,384]{2,1,0:T(8,128)(2,1)S(1)}, bf16[1,64,384]{2,1,0:T(8,128)(2,1)S(1)}, u32[]{:S(2)}, u32[]{:S(2)}) collective-permute-start(bf16[1,64,384]{2,1,0:T(8,128)(2,1)S(1)} %get-tuple-element.1110), channel_id=1, source_target_pairs={{0,96},{32,0},{64,32},{96,64},{1,97},{33,1},{65,33},{97,65},{2,98}... | collective-permute-start | bytes 147464 | tf_op jit(solution)/shard_map/while/body/ppermute | solution.py:119
  220.1 15.1 %collective-permute-start.5 = (bf16[1,64,384]{2,1,0:T(8,128)(2,1)S(1)}, bf16[1,64,384]{2,1,0:T(8,128)(2,1)S(1)}, u32[]{:S(2)}, u32[]{:S(2)}) collective-permute-start(bf16[1,64,384]{2,1,0:T(8,128)(2,1)S(1)} %pick.43), channel_id=1, source_target_pairs={{0,64},{32,96},{64,0},{96,32},{1,65},{33,97},{65,1},{97,33},{2,66}... | collective-permute-start | bytes 147464 | tf_op jit(solution)/shard_map/while/body/ppermute | solution.py:119
  240.8 54.4 %all-to-all-start.3 = ((bf16[16,64,384]{2,1,0:T(8,128)(2,1)}), bf16[16,64,384]{2,1,0:T(8,128)(2,1)}, u32[]{:S(2)}, u32[]{:S(2)}) async-start(bf16[16,64,384]{2,1,0:T(8,128)(2,1)} %merge.36), calls=%async_computation.3 | async-start | bytes 1572864 | tf_op jit(solution)/shard_map/all_to_all | solution.py:150
  251.5 11.4 %copy-start.1 = (bf16[16,64,768]{2,1,0:T(8,128)(2,1)S(1)}, bf16[16,64,768]{2,1,0:T(8,128)(2,1)}, u32[]{:S(2)}) copy-start(bf16[16,64,768]{2,1,0:T(8,128)(2,1)} %get-tuple-element.1156) | copy-start | bytes 4718596 | tf_op jit(solution)/shard_map/while
  253.2 11.3 %collective-permute-start = (bf16[1,64,768]{2,1,0:T(8,128)(2,1)S(1)}, bf16[1,64,768]{2,1,0:T(8,128)(2,1)S(1)}, u32[]{:S(2)}, u32[]{:S(2)}) collective-permute-start(bf16[1,64,768]{2,1,0:T(8,128)(2,1)S(1)} %get-tuple-element.1095), channel_id=1, source_target_pairs={{0,32},{32,64},{64,96},{96,0},{1,33},{33,65},{65,97},{97,1},{2,34}... | collective-permute-start | bytes 294920 | tf_op jit(solution)/shard_map/while/body/ppermute | solution.py:119
  255.4 13.0 %collective-permute-start.1 = (bf16[1,64,768]{2,1,0:T(8,128)(2,1)S(1)}, bf16[1,64,768]{2,1,0:T(8,128)(2,1)S(1)}, u32[]{:S(2)}, u32[]{:S(2)}) collective-permute-start(bf16[1,64,768]{2,1,0:T(8,128)(2,1)S(1)} %get-tuple-element.1096), channel_id=1, source_target_pairs={{0,96},{32,0},{64,32},{96,64},{1,97},{33,1},{65,33},{97,65},{2,98}... | collective-permute-start | bytes 294920 | tf_op jit(solution)/shard_map/while/body/ppermute | solution.py:119
  272.0 11.5 %copy-start.2 = (bf16[16,64,768]{2,1,0:T(8,128)(2,1)S(1)}, bf16[16,64,768]{2,1,0:T(8,128)(2,1)}, u32[]{:S(2)}) copy-start(bf16[16,64,768]{2,1,0:T(8,128)(2,1)} %get-tuple-element.1186) | copy-start | bytes 4718596 | tf_op jit(solution)/shard_map/while
  274.7 17.8 %collective-permute-start.2 = (bf16[1,64,768]{2,1,0:T(8,128)(2,1)S(1)}, bf16[1,64,768]{2,1,0:T(8,128)(2,1)S(1)}, u32[]{:S(2)}, u32[]{:S(2)}) collective-permute-start(bf16[1,64,768]{2,1,0:T(8,128)(2,1)S(1)} %pick.41), channel_id=1, source_target_pairs={{0,64},{32,96},{64,0},{96,32},{1,65},{33,97},{65,1},{97,33},{2,66}... | collective-permute-start | bytes 294920 | tf_op jit(solution)/shard_map/while/body/ppermute | solution.py:119
  299.2 6.1 copy-start.10
  299.2 25.1 %all-to-all-start.4 = ((bf16[16,64,768]{2,1,0:T(8,128)(2,1)}), bf16[16,64,768]{2,1,0:T(8,128)(2,1)S(1)}, u32[]{:S(2)}, u32[]{:S(2)}) async-start(bf16[16,64,768]{2,1,0:T(8,128)(2,1)} %merge.37), calls=%async_computation.4 | async-start | bytes 3145728 | tf_op jit(solution)/shard_map/all_to_all | solution.py:150
  324.4 38.9 %copy-start.5 = (bf16[16,64,768]{2,1,0:T(8,128)(2,1)}, bf16[16,64,768]{2,1,0:T(8,128)(2,1)S(1)}, u32[]{:S(2)}) copy-start(bf16[16,64,768]{2,1,0:T(8,128)(2,1)S(1)} %all-to-all-done.4) | copy-start | bytes 4718596
  324.4 3.6 copy-start.23
  327.9 35.3 %copy-start.7 = (bf16[1024,768]{1,0:T(8,128)(2,1)}, bf16[1024,768]{1,0:T(8,128)(2,1)S(1)}, u32[]{:S(2)}) copy-start(bf16[1024,768]{1,0:T(8,128)(2,1)S(1)} %fusion.6) | copy-start | bytes 4718596
  329.1 12.0 %copy-start.27 = (bf16[2,2,128,128]{3,2,1,0:T(8,128)(2,1)S(1)}, bf16[2,2,128,128]{3,2,1,0:T(8,128)(2,1)}, u32[]{:S(2)}) copy-start(bf16[2,2,128,128]{3,2,1,0:T(8,128)(2,1)} %copy-done.26) | copy-start | bytes 393220
  329.7 23.9 %copy-start.11 = (bf16[1,384,1024]{1,2,0:T(8,128)(2,1)S(1)}, bf16[1,384,1024]{1,2,0:T(8,128)(2,1)}, u32[]{:S(2)}) copy-start(bf16[1,384,1024]{1,2,0:T(8,128)(2,1)} %copy-done.9) | copy-start | bytes 2359300
  353.5 3.4 copy-start.29
  357.0 19.7 %all-to-all-start.6 = ((bf16[16,64,384]{2,1,0:T(8,128)(2,1)}), bf16[16,64,384]{2,1,0:T(8,128)(2,1)}, u32[]{:S(2)}, u32[]{:S(2)}) async-start(bf16[16,64,384]{2,1,0:T(8,128)(2,1)} %bitcast.178), calls=%async_computation.6 | async-start | bytes 1572864 | tf_op jit(solution)/shard_map/all_to_all | solution.py:150
  376.7 30.7 %all-to-all-start.7 = ((bf16[16,64,768]{2,1,0:T(8,128)(2,1)}), bf16[16,64,768]{2,1,0:T(8,128)(2,1)}, u32[]{:S(2)}, u32[]{:S(2)}) async-start(bf16[16,64,768]{2,1,0:T(8,128)(2,1)} %bitcast.176), calls=%async_computation.7 | async-start | bytes 3145728 | tf_op jit(solution)/shard_map/all_to_all | solution.py:150
  382.4 47.9 %collective-permute-start.21 = (bf16[5,64,384]{2,1,0:T(8,128)(2,1)S(1)}, bf16[5,64,384]{2,1,0:T(8,128)(2,1)S(1)}, u32[]{:S(2)}, u32[]{:S(2)}) collective-permute-start(bf16[5,64,384]{2,1,0:T(8,128)(2,1)S(1)} %get-tuple-element.681), channel_id=1, source_target_pairs={{0,96},{32,0},{64,32},{96,64},{1,97},{33,1},{65,33},{97,65},{2,98}... | collective-permute-start | bytes 737288 | tf_op jit(solution)/shard_map/ppermute | solution.py:119
  390.4 39.9 %collective-permute-start.23 = (bf16[5,64,384]{2,1,0:T(8,128)(2,1)S(1)}, bf16[5,64,384]{2,1,0:T(8,128)(2,1)S(1)}, u32[]{:S(2)}, u32[]{:S(2)}) collective-permute-start(bf16[5,64,384]{2,1,0:T(8,128)(2,1)S(1)} %get-tuple-element.683), channel_id=1, source_target_pairs={{0,32},{32,64},{64,96},{96,0},{1,33},{33,65},{65,97},{97,1},{2,34}... | collective-permute-start | bytes 737288 | tf_op jit(solution)/shard_map/ppermute | solution.py:119
  392.3 30.4 %collective-permute-start.22 = (bf16[4,64,384]{2,1,0:T(8,128)(2,1)S(1)}, bf16[4,64,384]{2,1,0:T(8,128)(2,1)S(1)}, u32[]{:S(2)}, u32[]{:S(2)}) collective-permute-start(bf16[4,64,384]{2,1,0:T(8,128)(2,1)S(1)} %get-tuple-element.682), channel_id=1, source_target_pairs={{0,64},{32,96},{64,0},{96,32},{1,65},{33,97},{65,1},{97,33},{2,66}... | collective-permute-start | bytes 589832 | tf_op jit(solution)/shard_map/ppermute | solution.py:119
  410.1 221.5 %collective-permute-start.18 = (bf16[5,64,768]{2,1,0:T(8,128)(2,1)}, bf16[5,64,768]{2,1,0:T(8,128)(2,1)S(1)}, u32[]{:S(2)}, u32[]{:S(2)}) collective-permute-start(bf16[5,64,768]{2,1,0:T(8,128)(2,1)} %get-tuple-element.675), channel_id=1, source_target_pairs={{0,96},{32,0},{64,32},{96,64},{1,97},{33,1},{65,33},{97,65},{2,98}... | collective-permute-start | bytes 1474568 | tf_op jit(solution)/shard_map/ppermute | solution.py:119
  414.9 216.7 %collective-permute-start.20 = (bf16[5,64,768]{2,1,0:T(8,128)(2,1)}, bf16[5,64,768]{2,1,0:T(8,128)(2,1)S(1)}, u32[]{:S(2)}, u32[]{:S(2)}) collective-permute-start(bf16[5,64,768]{2,1,0:T(8,128)(2,1)} %get-tuple-element.677), channel_id=1, source_target_pairs={{0,32},{32,64},{64,96},{96,0},{1,33},{33,65},{65,97},{97,1},{2,34}... | collective-permute-start | bytes 1474568 | tf_op jit(solution)/shard_map/ppermute | solution.py:119
  422.7 208.9 %collective-permute-start.19 = (bf16[4,64,768]{2,1,0:T(8,128)(2,1)}, bf16[4,64,768]{2,1,0:T(8,128)(2,1)S(1)}, u32[]{:S(2)}, u32[]{:S(2)}) collective-permute-start(bf16[4,64,768]{2,1,0:T(8,128)(2,1)} %get-tuple-element.676), channel_id=1, source_target_pairs={{0,64},{32,96},{64,0},{96,32},{1,65},{33,97},{65,1},{97,33},{2,66}... | collective-permute-start | bytes 1179656 | tf_op jit(solution)/shard_map/ppermute | solution.py:119
  432.2 23.7 %collective-permute-start.10 = (bf16[1,64,384]{2,1,0:T(8,128)(2,1)S(1)}, bf16[1,64,384]{2,1,0:T(8,128)(2,1)S(1)}, u32[]{:S(2)}, u32[]{:S(2)}) collective-permute-start(bf16[1,64,384]{2,1,0:T(8,128)(2,1)S(1)} %get-tuple-element.1138), channel_id=1, source_target_pairs={{0,96},{32,0},{64,32},{96,64},{1,97},{33,1},{65,33},{97,65},{2,98}... | collective-permute-start | bytes 147464 | tf_op jit(solution)/shard_map/while/body/ppermute | solution.py:119
  437.9 64.1 %collective-permute-start.9 = (bf16[1,64,384]{2,1,0:T(8,128)(2,1)S(1)}, bf16[1,64,384]{2,1,0:T(8,128)(2,1)S(1)}, u32[]{:S(2)}, u32[]{:S(2)}) collective-permute-start(bf16[1,64,384]{2,1,0:T(8,128)(2,1)S(1)} %get-tuple-element.1137), channel_id=1, source_target_pairs={{0,32},{32,64},{64,96},{96,0},{1,33},{33,65},{65,97},{97,1},{2,34}... | collective-permute-start | bytes 147464 | tf_op jit(solution)/shard_map/while/body/ppermute | solution.py:119
  505.8 23.6 %collective-permute-start.10 = (bf16[1,64,384]{2,1,0:T(8,128)(2,1)S(1)}, bf16[1,64,384]{2,1,0:T(8,128)(2,1)S(1)}, u32[]{:S(2)}, u32[]{:S(2)}) collective-permute-start(bf16[1,64,384]{2,1,0:T(8,128)(2,1)S(1)} %get-tuple-element.1138), channel_id=1, source_target_pairs={{0,96},{32,0},{64,32},{96,64},{1,97},{33,1},{65,33},{97,65},{2,98}... | collective-permute-start | bytes 147464 | tf_op jit(solution)/shard_map/while/body/ppermute | solution.py:119
  526.3 10.6 %collective-permute-start.9 = (bf16[1,64,384]{2,1,0:T(8,128)(2,1)S(1)}, bf16[1,64,384]{2,1,0:T(8,128)(2,1)S(1)}, u32[]{:S(2)}, u32[]{:S(2)}) collective-permute-start(bf16[1,64,384]{2,1,0:T(8,128)(2,1)S(1)} %get-tuple-element.1137), channel_id=1, source_target_pairs={{0,32},{32,64},{64,96},{96,0},{1,33},{33,65},{65,97},{97,1},{2,34}... | collective-permute-start | bytes 147464 | tf_op jit(solution)/shard_map/while/body/ppermute | solution.py:119
  540.7 11.0 %collective-permute-start.10 = (bf16[1,64,384]{2,1,0:T(8,128)(2,1)S(1)}, bf16[1,64,384]{2,1,0:T(8,128)(2,1)S(1)}, u32[]{:S(2)}, u32[]{:S(2)}) collective-permute-start(bf16[1,64,384]{2,1,0:T(8,128)(2,1)S(1)} %get-tuple-element.1138), channel_id=1, source_target_pairs={{0,96},{32,0},{64,32},{96,64},{1,97},{33,1},{65,33},{97,65},{2,98}... | collective-permute-start | bytes 147464 | tf_op jit(solution)/shard_map/while/body/ppermute | solution.py:119
  544.2 10.3 %collective-permute-start.9 = (bf16[1,64,384]{2,1,0:T(8,128)(2,1)S(1)}, bf16[1,64,384]{2,1,0:T(8,128)(2,1)S(1)}, u32[]{:S(2)}, u32[]{:S(2)}) collective-permute-start(bf16[1,64,384]{2,1,0:T(8,128)(2,1)S(1)} %get-tuple-element.1137), channel_id=1, source_target_pairs={{0,32},{32,64},{64,96},{96,0},{1,33},{33,65},{65,97},{97,1},{2,34}... | collective-permute-start | bytes 147464 | tf_op jit(solution)/shard_map/while/body/ppermute | solution.py:119
  560.8 70.8 %all-to-all-start.8 = ((bf16[16,64,384]{2,1,0:T(8,128)(2,1)}), bf16[16,64,384]{2,1,0:T(8,128)(2,1)}, u32[]{:S(2)}, u32[]{:S(2)}) async-start(bf16[16,64,384]{2,1,0:T(8,128)(2,1)} %merge.38), calls=%async_computation.8 | async-start | bytes 1572864 | tf_op jit(solution)/shard_map/all_to_all | solution.py:150
  570.6 11.4 %copy-start.3 = (bf16[16,64,768]{2,1,0:T(8,128)(2,1)S(1)}, bf16[16,64,768]{2,1,0:T(8,128)(2,1)}, u32[]{:S(2)}) copy-start(bf16[16,64,768]{2,1,0:T(8,128)(2,1)} %get-tuple-element.1276) | copy-start | bytes 4718596 | tf_op jit(solution)/shard_map/while
  572.3 13.1 %collective-permute-start.6 = (bf16[1,64,768]{2,1,0:T(8,128)(2,1)S(1)}, bf16[1,64,768]{2,1,0:T(8,128)(2,1)S(1)}, u32[]{:S(2)}, u32[]{:S(2)}) collective-permute-start(bf16[1,64,768]{2,1,0:T(8,128)(2,1)S(1)} %get-tuple-element.1123), channel_id=1, source_target_pairs={{0,32},{32,64},{64,96},{96,0},{1,33},{33,65},{65,97},{97,1},{2,34}... | collective-permute-start | bytes 294920 | tf_op jit(solution)/shard_map/while/body/ppermute | solution.py:119
  577.2 11.7 %collective-permute-start.7 = (bf16[1,64,768]{2,1,0:T(8,128)(2,1)S(1)}, bf16[1,64,768]{2,1,0:T(8,128)(2,1)S(1)}, u32[]{:S(2)}, u32[]{:S(2)}) collective-permute-start(bf16[1,64,768]{2,1,0:T(8,128)(2,1)S(1)} %get-tuple-element.1124), channel_id=1, source_target_pairs={{0,96},{32,0},{64,32},{96,64},{1,97},{33,1},{65,33},{97,65},{2,98}... | collective-permute-start | bytes 294920 | tf_op jit(solution)/shard_map/while/body/ppermute | solution.py:119
  591.8 11.4 %copy-start.3 = (bf16[16,64,768]{2,1,0:T(8,128)(2,1)S(1)}, bf16[16,64,768]{2,1,0:T(8,128)(2,1)}, u32[]{:S(2)}) copy-start(bf16[16,64,768]{2,1,0:T(8,128)(2,1)} %get-tuple-element.1276) | copy-start | bytes 4718596 | tf_op jit(solution)/shard_map/while
  593.4 12.3 %collective-permute-start.6 = (bf16[1,64,768]{2,1,0:T(8,128)(2,1)S(1)}, bf16[1,64,768]{2,1,0:T(8,128)(2,1)S(1)}, u32[]{:S(2)}, u32[]{:S(2)}) collective-permute-start(bf16[1,64,768]{2,1,0:T(8,128)(2,1)S(1)} %get-tuple-element.1123), channel_id=1, source_target_pairs={{0,32},{32,64},{64,96},{96,0},{1,33},{33,65},{65,97},{97,1},{2,34}... | collective-permute-start | bytes 294920 | tf_op jit(solution)/shard_map/while/body/ppermute | solution.py:119
  596.4 13.7 %collective-permute-start.7 = (bf16[1,64,768]{2,1,0:T(8,128)(2,1)S(1)}, bf16[1,64,768]{2,1,0:T(8,128)(2,1)S(1)}, u32[]{:S(2)}, u32[]{:S(2)}) collective-permute-start(bf16[1,64,768]{2,1,0:T(8,128)(2,1)S(1)} %get-tuple-element.1124), channel_id=1, source_target_pairs={{0,96},{32,0},{64,32},{96,64},{1,97},{33,1},{65,33},{97,65},{2,98}... | collective-permute-start | bytes 294920 | tf_op jit(solution)/shard_map/while/body/ppermute | solution.py:119
  612.9 11.4 %copy-start.3 = (bf16[16,64,768]{2,1,0:T(8,128)(2,1)S(1)}, bf16[16,64,768]{2,1,0:T(8,128)(2,1)}, u32[]{:S(2)}) copy-start(bf16[16,64,768]{2,1,0:T(8,128)(2,1)} %get-tuple-element.1276) | copy-start | bytes 4718596 | tf_op jit(solution)/shard_map/while
  614.5 11.6 %collective-permute-start.6 = (bf16[1,64,768]{2,1,0:T(8,128)(2,1)S(1)}, bf16[1,64,768]{2,1,0:T(8,128)(2,1)S(1)}, u32[]{:S(2)}, u32[]{:S(2)}) collective-permute-start(bf16[1,64,768]{2,1,0:T(8,128)(2,1)S(1)} %get-tuple-element.1123), channel_id=1, source_target_pairs={{0,32},{32,64},{64,96},{96,0},{1,33},{33,65},{65,97},{97,1},{2,34}... | collective-permute-start | bytes 294920 | tf_op jit(solution)/shard_map/while/body/ppermute | solution.py:119
  616.9 11.2 %collective-permute-start.7 = (bf16[1,64,768]{2,1,0:T(8,128)(2,1)S(1)}, bf16[1,64,768]{2,1,0:T(8,128)(2,1)S(1)}, u32[]{:S(2)}, u32[]{:S(2)}) collective-permute-start(bf16[1,64,768]{2,1,0:T(8,128)(2,1)S(1)} %get-tuple-element.1124), channel_id=1, source_target_pairs={{0,96},{32,0},{64,32},{96,64},{1,97},{33,1},{65,33},{97,65},{2,98}... | collective-permute-start | bytes 294920 | tf_op jit(solution)/shard_map/while/body/ppermute | solution.py:119
  635.5 8.3 %copy-start.12 = (bf16[1,384,1024]{1,2,0:T(8,128)(2,1)S(1)}, bf16[1,384,1024]{1,2,0:T(8,128)(2,1)}, u32[]{:S(2)}) copy-start(bf16[1,384,1024]{1,2,0:T(8,128)(2,1)} %copy-done.9) | copy-start | bytes 2359300
  635.5 8.3 %copy-start.14 = (bf16[1024,384]{1,0:T(8,128)(2,1)S(1)}, bf16[1024,384]{1,0:T(8,128)(2,1)}, u32[]{:S(2)}) copy-start(bf16[1024,384]{1,0:T(8,128)(2,1)} %fusion.17) | copy-start | bytes 2359300
  635.5 32.0 %all-to-all-start.9 = ((bf16[16,64,768]{2,1,0:T(8,128)(2,1)}), bf16[16,64,768]{2,1,0:T(8,128)(2,1)}, u32[]{:S(2)}, u32[]{:S(2)}) async-start(bf16[16,64,768]{2,1,0:T(8,128)(2,1)} %merge.39), calls=%async_computation.9 | async-start | bytes 3145728 | tf_op jit(solution)/shard_map/all_to_all | solution.py:150
  643.8 23.7 %copy-start.8 = (bf16[1024,768]{1,0:T(8,128)(2,1)S(1)}, bf16[1024,768]{1,0:T(8,128)(2,1)}, u32[]{:S(2)}) copy-start(bf16[1024,768]{1,0:T(8,128)(2,1)} %copy-done.7) | copy-start | bytes 4718596
  647.5 20.0 %copy-start.6 = (bf16[16,64,768]{2,1,0:T(8,128)(2,1)S(1)}, bf16[16,64,768]{2,1,0:T(8,128)(2,1)}, u32[]{:S(2)}) copy-start(bf16[16,64,768]{2,1,0:T(8,128)(2,1)} %copy-done.5) | copy-start | bytes 4718596
  (13 other events, 17.2 us)

commit v5 on v4

--- a/solution.py
+++ b/solution.py
@@ -27,8 +27,8 @@
 FLAT = ("x", "y")
 TENSOR = ("l", "c")
 
-NEXT = 5
-FAR = 4
+NEXT = 6
+FAR = 5
 VMEM = 48 << 20
 
 
@@ -60,15 +60,17 @@
     return [(send_index[r], where[r], next_trips[r], far_trips[r]) for r in range(ROUNDS)]
 
 
-def kernel_call(kernel, out_shape, index_args, args, name):
+def kernel_call(kernel, out_shape, index_args, args, name, outside=0, scratch=()):
     scalars = [pl.BlockSpec(memory_space=pltpu.SMEM)] * len(index_args)
     whole = pl.BlockSpec(memory_space=pltpu.VMEM)
-    size = sum(a.size * a.dtype.itemsize for a in (*args, *out_shape))
+    inside = [whole] * (len(args) - outside)
+    size = sum(a.size * a.dtype.itemsize for a in (*args[: len(inside)], *out_shape))
     return pl.pallas_call(
         kernel,
         out_shape=out_shape,
-        in_specs=scalars + [whole] * len(args),
+        in_specs=scalars + inside + [pl.BlockSpec(memory_space=pl.ANY)] * outside,
         out_specs=(whole,) * len(out_shape),
+        scratch_shapes=list(scratch),
         compiler_params=pltpu.CompilerParams(vmem_limit_bytes=VMEM),
         cost_estimate=pl.CostEstimate(flops=size, bytes_accessed=size, transcendentals=0),
         name=name,
@@ -88,26 +90,39 @@
     return kernel_call(pick_kernel, out_shape, (index,), (chunks,), "pick")
 
 
-def merge_kernel(kinds, where, low, before, *refs):
-    sources, out = refs[:-1], refs[-1]
+def merge_kernel(kinds, column, where, *refs):
+    n = len(kinds)
+    sources, spare, out, sem = refs[:n], refs[n:-2], refs[-2], refs[-1]
 
     @pl.loop(0, PLANE)
     def _(d):
         kind, slot = where[0, d], where[1, d]
-        out[d] = before[d]
         for i, (number, source) in enumerate(zip(kinds, sources)):
-            at = slot - low[i]
-
-            @pl.when((kind == number) & (at >= 0) & (at < source.shape[0]))
-            def _(source=source, at=at):
-                out[d] = source[at]
-
-
-def merge(where, low, before, sources):
-    kernel = functools.partial(merge_kernel, tuple(sources))
-    out_shape = (jax.ShapeDtypeStruct(before.shape, before.dtype),)
-    low = jnp.stack([jnp.int32(0) + low] * len(sources))
-    return kernel_call(kernel, out_shape, (where, low), (before, *sources.values()), "merge")[0]
+            count = source.shape[0]
+
+            @pl.when((kind == number) & (slot < count))
+            def _(source=source):
+                out[d] = source[slot]
+
+            if number:
+
+                @pl.when((kind == number) & (slot >= count))
+                def _(source=spare[i - 1], count=count):
+                    columns = pl.ds(column, out.shape[2])
+                    copy = pltpu.make_async_copy(
+                        source.at[slot - count, :, columns], out.at[d], sem
+                    )
+                    copy.start()
+                    copy.wait()
+
+
+def merge(where, sources, spare, column):
+    share = sources[0]
+    kernel = functools.partial(merge_kernel, tuple(sources), column)
+    out_shape = (jax.ShapeDtypeStruct(share.shape, share.dtype),)
+    args = (*sources.values(), *(spare[k] for k in sources if k))
+    scratch = [pltpu.SemaphoreType.DMA]
+    return kernel_call(kernel, out_shape, (where,), args, "merge", len(spare), scratch)[0]
 
 
 def step_by(n):
@@ -123,27 +138,49 @@
     return dict(zip((3, 1, 2), pick(index, share, (NEXT, NEXT, FAR))))
 
 
-def late(route, share, after):
-    send_index, where, next_trips, far_trips = route
+def pick_late_kernel(index, *refs):
+    outs = refs[-index.shape[0] :]
+    for o, out in enumerate(outs):
+        at = 0
+        for share in refs[: -len(outs)]:
+            width = share.shape[2]
+            out[0, :, at : at + width] = share[index[o, 0]]
+            at += width
+
+
+def late(route, shares, after):
+    send_index, _, next_trips, far_trips = route
     start, _ = lax.optimization_barrier((jnp.int32(0), after))
-
-    def next_one(state):
-        i, placed = state
-        at = NEXT + i
-        index = lax.dynamic_slice(send_index, (0, at), (2, 1))
-        came = hop(dict(zip((3, 1), pick(index, share, (1, 1)))))
-        return i + 1, merge(where, at, placed, came)
-
-    def far_one(state):
-        i, placed = state
-        at = FAR + i
-        index = lax.dynamic_slice(send_index, (2, at), (1, 1))
-        came = hop(dict(zip((2,), pick(index, share, (1,)))))
-        return i + 1, merge(where, at, placed, came)
-
-    _, placed = lax.while_loop(lambda s: s[0] < next_trips, next_one, (start, share))
-    _, placed = lax.while_loop(lambda s: s[0] < far_trips, far_one, (start, placed))
-    return placed
+    depth, width = shares[0].shape[1], sum(s.shape[2] for s in shares)
+
+    def room(n):
+        return jnp.zeros((PLANE - n, depth, width), shares[0].dtype)
+
+    def trip(first, steps, slots):
+        def one(state):
+            i, came = state
+            index = lax.dynamic_slice(send_index, (first, slots + i), (len(steps), 1))
+            one_chunk = jax.ShapeDtypeStruct((1, depth, width), shares[0].dtype)
+            sends = kernel_call(
+                pick_late_kernel, (one_chunk,) * len(steps), (index,), shares, "pick"
+            )
+            new = hop(dict(zip(steps, sends)))
+            return i + 1, {
+                k: lax.dynamic_update_slice(old, new[k], (i, 0, 0)) for k, old in came.items()
+            }
+
+        return one
+
+    _, near = lax.while_loop(
+        lambda s: s[0] < next_trips,
+        trip(0, (3, 1), NEXT),
+        (start, {1: room(NEXT), 3: room(NEXT)}),
+    )
+    start, _ = lax.optimization_barrier((start, near))
+    _, far = lax.while_loop(
+        lambda s: s[0] < far_trips, trip(2, (2,), FAR), (start, {2: room(FAR)})
+    )
+    return {**near, **far}
 
 
 def over_plane(chunks):
@@ -160,11 +197,13 @@
         shares.append(over_plane(a))
         sent.append(depart(route[0], shares[-1]))
         came.append(hop(sent[-1]))
-    for i, share in enumerate(shares):
-        placed = late(route, share, (sent[i], sent[min(i + 1, len(sent) - 1)]))
-        parts, placed, _ = tie((came[i], placed, done))
-        parts = {0: share, **parts}
-        done = done + [over_plane(merge(route[1], 0, placed, parts))]
+    spare, column, placed = late(route, shares, (sent, came[0])), 0, []
+    for share, parts in zip(shares, came):
+        parts, spare = tie((parts, spare))
+        placed.append(merge(route[1], {0: share, **parts}, spare, column))
+        column += share.shape[2]
+    placed[0], _ = tie((placed[0], came))
+    done = [over_plane(p) for p in placed]
     return [d.reshape(a.shape) for d, a in zip(done, arrays)]
 
 

time: 676 us -> 551 us (0.82)
  the two profiles are of different devices: /device:TPU:32 before, /device:TPU:1 now
where the time goes in v5:
time: 551 us; the launch traced here: 547 us
  waiting for transfers between devices  241 us (44%)
  starting transfers between devices  144 us (26%)
  blocking collectives  83 us (15%)
  Pallas kernels  20.8 us (4%)
  other arithmetic  19.1 us (3%)
  local copies, waits for them, and re-layouts  18.3 us (3%)
  matrix products  16.8 us (3%)
    ppermute x12, waiting for transfers between devices, hop(): lax.ppermute(s, 'h', step_by(steps[k]))  171 us
    ppermute x12, starting transfers between devices, hop(): lax.ppermute(s, 'h', step_by(steps[k]))  104 us
    all_to_all x8, waiting for transfers between devices, over_plane(): return lax.all_to_all(chunks, FLAT, 0, 0, tiled=True)  62.6 us
    all_to_all x8, starting transfers between devices, over_plane(): return lax.all_to_all(chunks, FLAT, 0, 0, tiled=True)  37 us
    all_to_all x1, blocking collectives, local_step(): terms = lax.all_to_all(blocks, TENSOR, 0, 0, tiled=True)  34.3 us
    all_gather x2, blocking collectives, local_step(): errors = lax.all_gather(error_cols, TENSOR, axis=1, tiled=True)  27.9 us
    pallas_call x8, Pallas kernels, kernel_call(): pl.pallas_call(kernel, out_shape=out_shape, in_specs=scalars + inside + [...  20.8 us
    all_gather x1, blocking collectives, body(): inputs = lax.all_gather(in_cols, TENSOR, axis=2, tiled=True)  20.7 us
  transfers between devices with their start and end apart: 21, of which 13 were waited for; matrix products, arithmetic and copies ran while one was open for 6% of the time, Pallas kernels for 4%

profile of v5, /device:TPU:1, one launch (start us, length us, event | category | flops | bytes accessed | tf_op | source)
XLA Modules:
  0.0 546.8 jit_solution(15346838119003080018)
XLA Ops:
  2.2 1.3 gather_fusion
  3.7 20.7 %all-gather = bf16[2,1,128,1024]{3,2,1,0:T(8,128)(2,1)S(1)} all-gather(bf16[2,1,128,128]{3,2,1,0:T(8,128)(2,1)S(1)} %slice.97), channel_id=2, replica_groups=mesh['x'=4,'h'=4,'y'=4,'l'=4,'c'=2] {'l','c'}, dimensions={3}, use_global_device_ids=true | all-gather | bytes 589824 | tf_op jit(solution)/shard_map/all_gather | solution.py:281
  26.9 3.5 all-to-all-start
  32.0 7.0 %all-to-all-done = bf16[8,128,128]{2,1,0:T(8,128)(2,1)S(1)} async-done(((bf16[8,128,128]{2,1,0:T(8,128)(2,1)}), bf16[8,128,128]{2,1,0:T(8,128)(2,1)S(1)}, u32[]{:S(2)}, u32[]{:S(2)}) %all-to-all-start) | async-done | bytes 262176 | tf_op jit(solution)/shard_map/all_to_all | solution.py:229
  39.9 14.0 %all_gather.10 = bf16[128,1024]{1,0:T(8,128)(2,1)S(1)} all-gather(bf16[128,128]{1,0:T(8,128)(2,1)S(1)} %fusion.38), channel_id=1, replica_groups=mesh['x'=4,'h'=4,'y'=4,'l'=4,'c'=2] {'l','c'}, dimensions={1}, use_global_device_ids=true | all-gather | bytes 294912 | tf_op jit(solution)/shard_map/all_gather | solution.py:234
  53.9 2.2 fusion.20
  56.1 3.6 all-to-all-start.1
  61.0 1.4 multiply_convert_fusion.4
  62.4 1.8 fusion.5
  64.2 9.4 %all-to-all-done.1.chunks.refs_0_ = bf16[16,64,384]{2,1,0:T(8,128)(2,1)S(1)} async-done(((bf16[16,64,384]{2,1,0:T(8,128)(2,1)}), bf16[16,64,384]{2,1,0:T(8,128)(2,1)S(1)}, u32[]{:S(2)}, u32[]{:S(2)}) %all-to-all-start.1) | async-done | bytes 786464 | tf_op jit(solution)/shard_map/all_to_all | solution.py:187
  73.6 4.5 all-to-all-start.2
  78.9 1.6 pick.21
  80.5 9.2 %collective-permute-start.9 = (bf16[6,64,384]{2,1,0:T(8,128)(2,1)}, bf16[6,64,384]{2,1,0:T(8,128)(2,1)S(1)}, u32[]{:S(2)}, u32[]{:S(2)}) collective-permute-start(bf16[6,64,384]{2,1,0:T(8,128)(2,1)} %get-tuple-element.393), channel_id=1, source_target_pairs={{0,96},{32,0},{64,32},{96,64},{1,97},{33,1},{65,33},{97,65},{2,98}... | collective-permute-start | bytes 884744 | tf_op jit(solution)/shard_map/ppermute | solution.py:134
  89.7 4.9 collective-permute-start.10
  94.6 7.3 %collective-permute-start.11 = (bf16[6,64,384]{2,1,0:T(8,128)(2,1)}, bf16[6,64,384]{2,1,0:T(8,128)(2,1)S(1)}, u32[]{:S(2)}, u32[]{:S(2)}) collective-permute-start(bf16[6,64,384]{2,1,0:T(8,128)(2,1)} %get-tuple-element.395), channel_id=1, source_target_pairs={{0,32},{32,64},{64,96},{96,0},{1,33},{33,65},{65,97},{97,1},{2,34}... | collective-permute-start | bytes 884744 | tf_op jit(solution)/shard_map/ppermute | solution.py:134
  103.1 2.6 pick.20
  105.8 4.4 collective-permute-start.6
  110.2 6.6 %collective-permute-start.7 = (bf16[5,64,768]{2,1,0:T(8,128)(2,1)}, bf16[5,64,768]{2,1,0:T(8,128)(2,1)S(1)}, u32[]{:S(2)}, u32[]{:S(2)}) collective-permute-start(bf16[5,64,768]{2,1,0:T(8,128)(2,1)} %get-tuple-element.391), channel_id=1, source_target_pairs={{0,64},{32,96},{64,0},{96,32},{1,65},{33,97},{65,1},{97,33},{2,66}... | collective-permute-start | bytes 1474568 | tf_op jit(solution)/shard_map/ppermute | solution.py:134
  116.8 5.6 %collective-permute-start.8 = (bf16[6,64,768]{2,1,0:T(8,128)(2,1)S(1)}, bf16[6,64,768]{2,1,0:T(8,128)(2,1)S(1)}, u32[]{:S(2)}, u32[]{:S(2)}) collective-permute-start(bf16[6,64,768]{2,1,0:T(8,128)(2,1)S(1)} %get-tuple-element.392), channel_id=1, source_target_pairs={{0,32},{32,64},{64,96},{96,0},{1,33},{33,65},{65,97},{97,1},{2,34}... | collective-permute-start | bytes 1769480 | tf_op jit(solution)/shard_map/ppermute | solution.py:134
  122.4 75.1 %collective-permute-done.9.refs_1_ = bf16[6,64,384]{2,1,0:T(8,128)(2,1)S(1)} collective-permute-done((bf16[6,64,384]{2,1,0:T(8,128)(2,1)}, bf16[6,64,384]{2,1,0:T(8,128)(2,1)S(1)}, u32[]{:S(2)}, u32[]{:S(2)}) %collective-permute-start.9) | collective-permute-done | bytes 294944 | tf_op jit(solution)/shard_map/ppermute | solution.py:134
  197.5 1.4 broadcast.595.clone
  198.9 1.3 broadcast.595.clone.1
  200.9 1.4 broadcast.596.clone
  203.0 2.8 merge.5
  205.7 16.3 %collective-permute-done.6.refs_1_ = bf16[6,64,768]{2,1,0:T(8,128)(2,1)S(1)} collective-permute-done((bf16[6,64,768]{2,1,0:T(8,128)(2,1)}, bf16[6,64,768]{2,1,0:T(8,128)(2,1)S(1)}, u32[]{:S(2)}, u32[]{:S(2)}) %collective-permute-start.6) | collective-permute-done | bytes 589856 | tf_op jit(solution)/shard_map/ppermute | solution.py:134
  222.1 6.1 %all-to-all-start.4 = ((bf16[16,64,384]{2,1,0:T(8,128)(2,1)}), bf16[16,64,384]{2,1,0:T(8,128)(2,1)}, u32[]{:S(2)}, u32[]{:S(2)}) async-start(bf16[16,64,384]{2,1,0:T(8,128)(2,1)} %merge.5), calls=%async_computation.4 | async-start | bytes 1572864 | tf_op jit(solution)/shard_map/all_to_all | solution.py:187
  228.1 3.4 merge.4
  231.5 7.1 %all-to-all-done.4 = bf16[16,64,384]{2,1,0:T(8,128)(2,1)} async-done(((bf16[16,64,384]{2,1,0:T(8,128)(2,1)}), bf16[16,64,384]{2,1,0:T(8,128)(2,1)}, u32[]{:S(2)}, u32[]{:S(2)}) %all-to-all-start.4) | async-done | bytes 786464 | tf_op jit(solution)/shard_map/all_to_all | solution.py:187
  238.7 3.7 all-to-all-start.3
  242.4 2.0 fusion.17
  244.4 15.9 %all-to-all-done.3 = bf16[16,64,768]{2,1,0:T(8,128)(2,1)S(1)} async-done(((bf16[16,64,768]{2,1,0:T(8,128)(2,1)}), bf16[16,64,768]{2,1,0:T(8,128)(2,1)S(1)}, u32[]{:S(2)}, u32[]{:S(2)}) %all-to-all-start.3) | async-done | bytes 1572896 | tf_op jit(solution)/shard_map/all_to_all | solution.py:187
  260.3 3.6 fusion.6
  265.7 34.3 %all_to_all.50 = bf16[8,128,128]{2,1,0:T(8,128)(2,1)S(1)} all-to-all(bf16[8,128,128]{2,1,0:T(8,128)(2,1)S(1)} %bitcast.157), channel_id=1, replica_groups=mesh['x'=4,'h'=4,'y'=4,'l'=4,'c'=2] {'l','c'}, dimensions={0} | all-to-all | bytes 524288 | tf_op jit(solution)/shard_map/all_to_all | solution.py:229
  300.1 14.0 %all_gather.11 = bf16[128,1024]{1,0:T(8,128)(2,1)S(1)} all-gather(bf16[128,128]{1,0:T(8,128)(2,1)S(1)} %fusion.37), channel_id=1, replica_groups=mesh['x'=4,'h'=4,'y'=4,'l'=4,'c'=2] {'l','c'}, dimensions={1}, use_global_device_ids=true | all-gather | bytes 294912 | tf_op jit(solution)/shard_map/all_gather | solution.py:234
  314.1 3.4 subtract_convert_fusion.1
  317.4 3.8 all-to-all-start.6
  321.3 1.5 multiply_convert_fusion.1
  323.0 5.2 subtract_convert_fusion
  328.1 6.8 %all-to-all-done.6.chunks.refs_0_ = bf16[16,64,384]{2,1,0:T(8,128)(2,1)S(1)} async-done(((bf16[16,64,384]{2,1,0:T(8,128)(2,1)}), bf16[16,64,384]{2,1,0:T(8,128)(2,1)S(1)}, u32[]{:S(2)}, u32[]{:S(2)}) %all-to-all-start.6) | async-done | bytes 786464 | tf_op jit(solution)/shard_map/all_to_all | solution.py:187
  335.0 4.4 all-to-all-start.7
  339.4 1.6 pick.23
  341.0 9.3 %collective-permute-start.15 = (bf16[6,64,384]{2,1,0:T(8,128)(2,1)}, bf16[6,64,384]{2,1,0:T(8,128)(2,1)S(1)}, u32[]{:S(2)}, u32[]{:S(2)}) collective-permute-start(bf16[6,64,384]{2,1,0:T(8,128)(2,1)} %get-tuple-element.418), channel_id=1, source_target_pairs={{0,96},{32,0},{64,32},{96,64},{1,97},{33,1},{65,33},{97,65},{2,98}... | collective-permute-start | bytes 884744 | tf_op jit(solution)/shard_map/ppermute | solution.py:134
  350.3 1.9 collective-permute-start.17
  352.2 9.5 %collective-permute-start.16 = (bf16[5,64,384]{2,1,0:T(8,128)(2,1)S(1)}, bf16[5,64,384]{2,1,0:T(8,128)(2,1)S(1)}, u32[]{:S(2)}, u32[]{:S(2)}) collective-permute-start(bf16[5,64,384]{2,1,0:T(8,128)(2,1)S(1)} %get-tuple-element.419), channel_id=1, source_target_pairs={{0,64},{32,96},{64,0},{96,32},{1,65},{33,97},{65,1},{97,33},{2,66}... | collective-permute-start | bytes 737288 | tf_op jit(solution)/shard_map/ppermute | solution.py:134
  361.8 2.6 pick.22
  364.4 7.6 %collective-permute-start.12 = (bf16[6,64,768]{2,1,0:T(8,128)(2,1)}, bf16[6,64,768]{2,1,0:T(8,128)(2,1)S(1)}, u32[]{:S(2)}, u32[]{:S(2)}) collective-permute-start(bf16[6,64,768]{2,1,0:T(8,128)(2,1)} %get-tuple-element.415), channel_id=1, source_target_pairs={{0,96},{32,0},{64,32},{96,64},{1,97},{33,1},{65,33},{97,65},{2,98}... | collective-permute-start | bytes 1769480 | tf_op jit(solution)/shard_map/ppermute | solution.py:134
  372.0 4.8 collective-permute-start.13
  376.8 13.8 %collective-permute-done.16.refs_2_ = bf16[5,64,384]{2,1,0:T(8,128)(2,1)S(1)} collective-permute-done((bf16[5,64,384]{2,1,0:T(8,128)(2,1)S(1)}, bf16[5,64,384]{2,1,0:T(8,128)(2,1)S(1)}, u32[]{:S(2)}, u32[]{:S(2)}) %collective-permute-start.16) | collective-permute-done | bytes 245792 | tf_op jit(solution)/shard_map/ppermute | solution.py:134
  390.6 33.0 %collective-permute-start.14 = (bf16[6,64,768]{2,1,0:T(8,128)(2,1)S(1)}, bf16[6,64,768]{2,1,0:T(8,128)(2,1)S(1)}, u32[]{:S(2)}, u32[]{:S(2)}) collective-permute-start(bf16[6,64,768]{2,1,0:T(8,128)(2,1)S(1)} %get-tuple-element.417), channel_id=1, source_target_pairs={{0,32},{32,64},{64,96},{96,0},{1,33},{33,65},{65,97},{97,1},{2,34}... | collective-permute-start | bytes 1769480 | tf_op jit(solution)/shard_map/ppermute | solution.py:134
  423.6 3.2 collective-permute-done.15.refs_1_
  426.7 1.4 broadcast.595
  430.0 1.4 broadcast.596
  432.0 2.8 merge.7
  434.8 9.0 %collective-permute-done.12.refs_1_ = bf16[6,64,768]{2,1,0:T(8,128)(2,1)S(1)} collective-permute-done((bf16[6,64,768]{2,1,0:T(8,128)(2,1)}, bf16[6,64,768]{2,1,0:T(8,128)(2,1)S(1)}, u32[]{:S(2)}, u32[]{:S(2)}) %collective-permute-start.12) | collective-permute-done | bytes 589856 | tf_op jit(solution)/shard_map/ppermute | solution.py:134
  443.8 53.6 %collective-permute-done.14.refs_3_ = bf16[6,64,768]{2,1,0:T(8,128)(2,1)S(1)} collective-permute-done((bf16[6,64,768]{2,1,0:T(8,128)(2,1)S(1)}, bf16[6,64,768]{2,1,0:T(8,128)(2,1)S(1)}, u32[]{:S(2)}, u32[]{:S(2)}) %collective-permute-start.14) | collective-permute-done | bytes 589856 | tf_op jit(solution)/shard_map/ppermute | solution.py:134
  497.4 6.5 %all-to-all-start.9 = ((bf16[16,64,384]{2,1,0:T(8,128)(2,1)}), bf16[16,64,384]{2,1,0:T(8,128)(2,1)}, u32[]{:S(2)}, u32[]{:S(2)}) async-start(bf16[16,64,384]{2,1,0:T(8,128)(2,1)} %merge.7), calls=%async_computation.9 | async-start | bytes 1572864 | tf_op jit(solution)/shard_map/all_to_all | solution.py:187
  503.9 3.4 merge.6
  507.3 9.4 %all-to-all-done.9 = bf16[16,64,384]{2,1,0:T(8,128)(2,1)} async-done(((bf16[16,64,384]{2,1,0:T(8,128)(2,1)}), bf16[16,64,384]{2,1,0:T(8,128)(2,1)}, u32[]{:S(2)}, u32[]{:S(2)}) %all-to-all-start.9) | async-done | bytes 786464 | tf_op jit(solution)/shard_map/all_to_all | solution.py:187
  516.7 4.4 all-to-all-start.8
  521.1 3.7 fusion.26
  524.8 2.4 copy.19
  527.2 13.9 %all-to-all-done.8 = bf16[16,64,768]{2,1,0:T(8,128)(2,1)} async-done(((bf16[16,64,768]{2,1,0:T(8,128)(2,1)}), bf16[16,64,768]{2,1,0:T(8,128)(2,1)}, u32[]{:S(2)}, u32[]{:S(2)}) %all-to-all-start.8) | async-done | bytes 1572896 | tf_op jit(solution)/shard_map/all_to_all | solution.py:187
  541.1 4.4 fusion.3
  545.5 1.3 slice_bitcast_fusion
  (115 shorter events, 15.7 us)
Async XLA Ops:
  0.6 1.5 copy-start
  0.6 23.8 %copy-start.14 = (bf16[1,1024,384]{2,1,0:T(8,128)(2,1)S(1)}, bf16[1,1024,384]{2,1,0:T(8,128)(2,1)}, u32[]{:S(2)}) copy-start(bf16[1,1024,384]{2,1,0:T(8,128)(2,1)} %param.16) | copy-start | bytes 2359300
  0.7 23.8 %copy-start.15 = (bf16[1,1024,384]{2,1,0:T(8,128)(2,1)S(1)}, bf16[1,1024,384]{2,1,0:T(8,128)(2,1)}, u32[]{:S(2)}) copy-start(bf16[1,1024,384]{2,1,0:T(8,128)(2,1)} %param.15) | copy-start | bytes 2359300
  3.7 20.8 %copy-start.22 = (bf16[2,2,128,128]{3,2,1,0:T(8,128)(2,1)}, bf16[2,2,128,128]{3,2,1,0:T(8,128)(2,1)S(1)}, u32[]{:S(2)}) copy-start(bf16[2,2,128,128]{3,2,1,0:T(8,128)(2,1)S(1)} %broadcast_select_fusion) | copy-start | bytes 393220
  24.4 0.8 copy-start.17
  24.5 1.3 copy-start.13
  25.2 1.6 copy-start.24
  25.8 1.1 copy-start.21
  26.1 5.3 copy-start.25
  26.9 12.2 %all-to-all-start = ((bf16[8,128,128]{2,1,0:T(8,128)(2,1)}), bf16[8,128,128]{2,1,0:T(8,128)(2,1)S(1)}, u32[]{:S(2)}, u32[]{:S(2)}) async-start(bf16[8,128,128]{2,1,0:T(8,128)(2,1)} %bitcast.140), calls=%async_computation | async-start | bytes 524288 | tf_op jit(solution)/shard_map/all_to_all | solution.py:229
  30.7 25.4 %copy-start.8 = (bf16[1,384,1024]{1,2,0:T(8,128)(2,1)}, bf16[1,384,1024]{1,2,0:T(8,128)(2,1)S(1)}, u32[]{:S(2)}) copy-start(bf16[1,384,1024]{1,2,0:T(8,128)(2,1)S(1)} %copy.16) | copy-start | bytes 2359300
  31.4 0.6 copy-start.27
  31.4 0.6 copy-start.29
  56.1 17.5 %all-to-all-start.1 = ((bf16[16,64,384]{2,1,0:T(8,128)(2,1)}), bf16[16,64,384]{2,1,0:T(8,128)(2,1)S(1)}, u32[]{:S(2)}, u32[]{:S(2)}) async-start(bf16[16,64,384]{2,1,0:T(8,128)(2,1)} %bitcast.17), calls=%async_computation.1 | async-start | bytes 1572864 | tf_op jit(solution)/shard_map/all_to_all | solution.py:187
  59.7 2.8 copy-start.18
  73.6 5.3 copy-start.1
  73.6 4.6 copy-start.32
  73.6 4.6 copy-start.33
  73.6 4.7 copy-start.26
  73.6 4.7 copy-start.30
  73.6 4.9 copy-start.28
  73.6 5.1 copy-start.31
  73.6 29.5 %all-to-all-start.2 = ((bf16[16,64,768]{2,1,0:T(8,128)(2,1)}), bf16[16,64,768]{2,1,0:T(8,128)(2,1)}, u32[]{:S(2)}, u32[]{:S(2)}) async-start(bf16[16,64,768]{2,1,0:T(8,128)(2,1)} %bitcast.15), calls=%async_computation.2 | async-start | bytes 3145728 | tf_op jit(solution)/shard_map/all_to_all | solution.py:187
  80.5 117.0 %collective-permute-start.9 = (bf16[6,64,384]{2,1,0:T(8,128)(2,1)}, bf16[6,64,384]{2,1,0:T(8,128)(2,1)S(1)}, u32[]{:S(2)}, u32[]{:S(2)}) collective-permute-start(bf16[6,64,384]{2,1,0:T(8,128)(2,1)} %get-tuple-element.393), channel_id=1, source_target_pairs={{0,96},{32,0},{64,32},{96,64},{1,97},{33,1},{65,33},{97,65},{2,98}... | collective-permute-start | bytes 884744 | tf_op jit(solution)/shard_map/ppermute | solution.py:134
  89.7 27.1 %collective-permute-start.10 = (bf16[5,64,384]{2,1,0:T(8,128)(2,1)S(1)}, bf16[5,64,384]{2,1,0:T(8,128)(2,1)S(1)}, u32[]{:S(2)}, u32[]{:S(2)}) collective-permute-start(bf16[5,64,384]{2,1,0:T(8,128)(2,1)S(1)} %get-tuple-element.394), channel_id=1, source_target_pairs={{0,64},{32,96},{64,0},{96,32},{1,65},{33,97},{65,1},{97,33},{2,66}... | collective-permute-start | bytes 737288 | tf_op jit(solution)/shard_map/ppermute | solution.py:134
  94.6 102.9 %collective-permute-start.11 = (bf16[6,64,384]{2,1,0:T(8,128)(2,1)}, bf16[6,64,384]{2,1,0:T(8,128)(2,1)S(1)}, u32[]{:S(2)}, u32[]{:S(2)}) collective-permute-start(bf16[6,64,384]{2,1,0:T(8,128)(2,1)} %get-tuple-element.395), channel_id=1, source_target_pairs={{0,32},{32,64},{64,96},{96,0},{1,33},{33,65},{65,97},{97,1},{2,34}... | collective-permute-start | bytes 884744 | tf_op jit(solution)/shard_map/ppermute | solution.py:134
  105.8 116.3 %collective-permute-start.6 = (bf16[6,64,768]{2,1,0:T(8,128)(2,1)}, bf16[6,64,768]{2,1,0:T(8,128)(2,1)S(1)}, u32[]{:S(2)}, u32[]{:S(2)}) collective-permute-start(bf16[6,64,768]{2,1,0:T(8,128)(2,1)} %get-tuple-element.390), channel_id=1, source_target_pairs={{0,96},{32,0},{64,32},{96,64},{1,97},{33,1},{65,33},{97,65},{2,98}... | collective-permute-start | bytes 1769480 | tf_op jit(solution)/shard_map/ppermute | solution.py:134
  110.2 95.6 %collective-permute-start.7 = (bf16[5,64,768]{2,1,0:T(8,128)(2,1)}, bf16[5,64,768]{2,1,0:T(8,128)(2,1)S(1)}, u32[]{:S(2)}, u32[]{:S(2)}) collective-permute-start(bf16[5,64,768]{2,1,0:T(8,128)(2,1)} %get-tuple-element.391), channel_id=1, source_target_pairs={{0,64},{32,96},{64,0},{96,32},{1,65},{33,97},{65,1},{97,33},{2,66}... | collective-permute-start | bytes 1474568 | tf_op jit(solution)/shard_map/ppermute | solution.py:134
  116.8 105.3 %collective-permute-start.8 = (bf16[6,64,768]{2,1,0:T(8,128)(2,1)S(1)}, bf16[6,64,768]{2,1,0:T(8,128)(2,1)S(1)}, u32[]{:S(2)}, u32[]{:S(2)}) collective-permute-start(bf16[6,64,768]{2,1,0:T(8,128)(2,1)S(1)} %get-tuple-element.392), channel_id=1, source_target_pairs={{0,32},{32,64},{64,96},{96,0},{1,33},{33,65},{65,97},{97,1},{2,34}... | collective-permute-start | bytes 1769480 | tf_op jit(solution)/shard_map/ppermute | solution.py:134
  222.1 16.6 %all-to-all-start.4 = ((bf16[16,64,384]{2,1,0:T(8,128)(2,1)}), bf16[16,64,384]{2,1,0:T(8,128)(2,1)}, u32[]{:S(2)}, u32[]{:S(2)}) async-start(bf16[16,64,384]{2,1,0:T(8,128)(2,1)} %merge.5), calls=%async_computation.4 | async-start | bytes 1572864 | tf_op jit(solution)/shard_map/all_to_all | solution.py:187
  231.5 10.8 %copy-start.9 = (bf16[1,384,1024]{1,2,0:T(8,128)(2,1)S(1)}, bf16[1,384,1024]{1,2,0:T(8,128)(2,1)}, u32[]{:S(2)}) copy-start(bf16[1,384,1024]{1,2,0:T(8,128)(2,1)} %copy-done.8) | copy-start | bytes 2359300
  238.7 21.6 %all-to-all-start.3 = ((bf16[16,64,768]{2,1,0:T(8,128)(2,1)}), bf16[16,64,768]{2,1,0:T(8,128)(2,1)S(1)}, u32[]{:S(2)}, u32[]{:S(2)}) async-start(bf16[16,64,768]{2,1,0:T(8,128)(2,1)} %merge.4), calls=%async_computation.3 | async-start | bytes 3145728 | tf_op jit(solution)/shard_map/all_to_all | solution.py:187
  244.4 76.9 %copy-start.11 = (bf16[1024,384]{1,0:T(8,128)(2,1)}, bf16[1024,384]{1,0:T(8,128)(2,1)S(1)}, u32[]{:S(2)}) copy-start(bf16[1024,384]{1,0:T(8,128)(2,1)S(1)} %fusion.17) | copy-start | bytes 2359300
  260.3 62.5 %copy-start.3 = (bf16[16,64,768]{2,1,0:T(8,128)(2,1)}, bf16[16,64,768]{2,1,0:T(8,128)(2,1)S(1)}, u32[]{:S(2)}) copy-start(bf16[16,64,768]{2,1,0:T(8,128)(2,1)S(1)} %all-to-all-done.3) | copy-start | bytes 4718596
  260.3 3.6 copy-start.19
  263.9 1.8 copy-start.5
  264.3 0.9 copy-start.16
  265.2 34.9 %copy-start.23 = (bf16[2,2,128,128]{3,2,1,0:T(8,128)(2,1)S(1)}, bf16[2,2,128,128]{3,2,1,0:T(8,128)(2,1)}, u32[]{:S(2)}) copy-start(bf16[2,2,128,128]{3,2,1,0:T(8,128)(2,1)} %copy-done.22) | copy-start | bytes 393220
  317.4 17.5 %all-to-all-start.6 = ((bf16[16,64,384]{2,1,0:T(8,128)(2,1)}), bf16[16,64,384]{2,1,0:T(8,128)(2,1)S(1)}, u32[]{:S(2)}, u32[]{:S(2)}) async-start(bf16[16,64,384]{2,1,0:T(8,128)(2,1)} %bitcast.158), calls=%async_computation.6 | async-start | bytes 1572864 | tf_op jit(solution)/shard_map/all_to_all | solution.py:187
  321.3 1.6 copy-start.6
  321.3 1.7 copy-start.20
  335.0 4.4 copy-start.2
  335.0 26.8 %all-to-all-start.7 = ((bf16[16,64,768]{2,1,0:T(8,128)(2,1)}), bf16[16,64,768]{2,1,0:T(8,128)(2,1)}, u32[]{:S(2)}, u32[]{:S(2)}) async-start(bf16[16,64,768]{2,1,0:T(8,128)(2,1)} %bitcast.156), calls=%async_computation.7 | async-start | bytes 3145728 | tf_op jit(solution)/shard_map/all_to_all | solution.py:187
  341.0 85.7 %collective-permute-start.15 = (bf16[6,64,384]{2,1,0:T(8,128)(2,1)}, bf16[6,64,384]{2,1,0:T(8,128)(2,1)S(1)}, u32[]{:S(2)}, u32[]{:S(2)}) collective-permute-start(bf16[6,64,384]{2,1,0:T(8,128)(2,1)} %get-tuple-element.418), channel_id=1, source_target_pairs={{0,96},{32,0},{64,32},{96,64},{1,97},{33,1},{65,33},{97,65},{2,98}... | collective-permute-start | bytes 884744 | tf_op jit(solution)/shard_map/ppermute | solution.py:134
  350.3 76.4 %collective-permute-start.17 = (bf16[6,64,384]{2,1,0:T(8,128)(2,1)}, bf16[6,64,384]{2,1,0:T(8,128)(2,1)S(1)}, u32[]{:S(2)}, u32[]{:S(2)}) collective-permute-start(bf16[6,64,384]{2,1,0:T(8,128)(2,1)} %get-tuple-element.420), channel_id=1, source_target_pairs={{0,32},{32,64},{64,96},{96,0},{1,33},{33,65},{65,97},{97,1},{2,34}... | collective-permute-start | bytes 884744 | tf_op jit(solution)/shard_map/ppermute | solution.py:134
  352.2 38.4 %collective-permute-start.16 = (bf16[5,64,384]{2,1,0:T(8,128)(2,1)S(1)}, bf16[5,64,384]{2,1,0:T(8,128)(2,1)S(1)}, u32[]{:S(2)}, u32[]{:S(2)}) collective-permute-start(bf16[5,64,384]{2,1,0:T(8,128)(2,1)S(1)} %get-tuple-element.419), channel_id=1, source_target_pairs={{0,64},{32,96},{64,0},{96,32},{1,65},{33,97},{65,1},{97,33},{2,66}... | collective-permute-start | bytes 737288 | tf_op jit(solution)/shard_map/ppermute | solution.py:134
  364.4 79.4 %collective-permute-start.12 = (bf16[6,64,768]{2,1,0:T(8,128)(2,1)}, bf16[6,64,768]{2,1,0:T(8,128)(2,1)S(1)}, u32[]{:S(2)}, u32[]{:S(2)}) collective-permute-start(bf16[6,64,768]{2,1,0:T(8,128)(2,1)} %get-tuple-element.415), channel_id=1, source_target_pairs={{0,96},{32,0},{64,32},{96,64},{1,97},{33,1},{65,33},{97,65},{2,98}... | collective-permute-start | bytes 1769480 | tf_op jit(solution)/shard_map/ppermute | solution.py:134
  372.0 62.8 %collective-permute-start.13 = (bf16[5,64,768]{2,1,0:T(8,128)(2,1)}, bf16[5,64,768]{2,1,0:T(8,128)(2,1)S(1)}, u32[]{:S(2)}, u32[]{:S(2)}) collective-permute-start(bf16[5,64,768]{2,1,0:T(8,128)(2,1)} %get-tuple-element.416), channel_id=1, source_target_pairs={{0,64},{32,96},{64,0},{96,32},{1,65},{33,97},{65,1},{97,33},{2,66}... | collective-permute-start | bytes 1474568 | tf_op jit(solution)/shard_map/ppermute | solution.py:134
  390.6 106.8 %collective-permute-start.14 = (bf16[6,64,768]{2,1,0:T(8,128)(2,1)S(1)}, bf16[6,64,768]{2,1,0:T(8,128)(2,1)S(1)}, u32[]{:S(2)}, u32[]{:S(2)}) collective-permute-start(bf16[6,64,768]{2,1,0:T(8,128)(2,1)S(1)} %get-tuple-element.417), channel_id=1, source_target_pairs={{0,32},{32,64},{64,96},{96,0},{1,33},{33,65},{65,97},{97,1},{2,34}... | collective-permute-start | bytes 1769480 | tf_op jit(solution)/shard_map/ppermute | solution.py:134
  497.4 19.3 %all-to-all-start.9 = ((bf16[16,64,384]{2,1,0:T(8,128)(2,1)}), bf16[16,64,384]{2,1,0:T(8,128)(2,1)}, u32[]{:S(2)}, u32[]{:S(2)}) async-start(bf16[16,64,384]{2,1,0:T(8,128)(2,1)} %merge.7), calls=%async_computation.9 | async-start | bytes 1572864 | tf_op jit(solution)/shard_map/all_to_all | solution.py:187
  507.2 13.9 %copy-start.10 = (bf16[1,384,1024]{1,2,0:T(8,128)(2,1)S(1)}, bf16[1,384,1024]{1,2,0:T(8,128)(2,1)}, u32[]{:S(2)}) copy-start(bf16[1,384,1024]{1,2,0:T(8,128)(2,1)} %copy-done.8) | copy-start | bytes 2359300
  507.2 13.9 %copy-start.12 = (bf16[1024,384]{1,0:T(8,128)(2,1)S(1)}, bf16[1024,384]{1,0:T(8,128)(2,1)}, u32[]{:S(2)}) copy-start(bf16[1024,384]{1,0:T(8,128)(2,1)} %copy-done.11) | copy-start | bytes 2359300
  516.7 24.4 %all-to-all-start.8 = ((bf16[16,64,768]{2,1,0:T(8,128)(2,1)}), bf16[16,64,768]{2,1,0:T(8,128)(2,1)}, u32[]{:S(2)}, u32[]{:S(2)}) async-start(bf16[16,64,768]{2,1,0:T(8,128)(2,1)} %merge.6), calls=%async_computation.8 | async-start | bytes 3145728 | tf_op jit(solution)/shard_map/all_to_all | solution.py:187
  521.1 20.0 %copy-start.7 = (bf16[1024,768]{1,0:T(8,128)(2,1)S(1)}, bf16[1024,768]{1,0:T(8,128)(2,1)}, u32[]{:S(2)}) copy-start(bf16[1024,768]{1,0:T(8,128)(2,1)} %copy-done.5) | copy-start | bytes 4718596
  524.8 16.3 %copy-start.4 = (bf16[16,64,768]{2,1,0:T(8,128)(2,1)S(1)}, bf16[16,64,768]{2,1,0:T(8,128)(2,1)}, u32[]{:S(2)}) copy-start(bf16[16,64,768]{2,1,0:T(8,128)(2,1)} %copy-done.3) | copy-start | bytes 4718596

commit v6 on v5

--- a/solution.py
+++ b/solution.py
@@ -77,52 +77,67 @@
     )(*index_args, *args)
 
 
-def pick_kernel(index, chunks, *outs):
+def pick_kernel(index, *refs):
+    outs = refs[-index.shape[0] :]
     for o, out in enumerate(outs):
 
         @pl.loop(0, out.shape[0])
         def _(k, o=o, out=out):
-            out[k] = chunks[index[o, k]]
-
-
-def pick(index, chunks, counts):
-    out_shape = tuple(jax.ShapeDtypeStruct((n, *chunks.shape[1:]), chunks.dtype) for n in counts)
-    return kernel_call(pick_kernel, out_shape, (index,), (chunks,), "pick")
-
-
-def merge_kernel(kinds, column, where, *refs):
-    n = len(kinds)
-    sources, spare, out, sem = refs[:n], refs[n:-2], refs[-2], refs[-1]
+            at = 0
+            for share in refs[: -len(outs)]:
+                width = share.shape[2]
+                out[k, :, at : at + width] = share[index[o, k]]
+                at += width
+
+
+def pick(index, shares, counts):
+    depth, width = shares[0].shape[1], sum(s.shape[2] for s in shares)
+    out_shape = tuple(jax.ShapeDtypeStruct((n, depth, width), shares[0].dtype) for n in counts)
+    return kernel_call(pick_kernel, out_shape, (index,), shares, "pick")
+
+
+def merge_kernel(layout, where, *refs):
+    out, sem = refs[-2:]
+    spare = dict(zip((1, 3, 2), refs[-5:-2]))
 
     @pl.loop(0, PLANE)
     def _(d):
         kind, slot = where[0, d], where[1, d]
-        for i, (number, source) in enumerate(zip(kinds, sources)):
-            count = source.shape[0]
+        for (number, column), source in zip(layout, refs):
+            count, _, width = source.shape
 
             @pl.when((kind == number) & (slot < count))
-            def _(source=source):
-                out[d] = source[slot]
-
-            if number:
-
-                @pl.when((kind == number) & (slot >= count))
-                def _(source=spare[i - 1], count=count):
-                    columns = pl.ds(column, out.shape[2])
-                    copy = pltpu.make_async_copy(
-                        source.at[slot - count, :, columns], out.at[d], sem
-                    )
-                    copy.start()
-                    copy.wait()
-
-
-def merge(where, sources, spare, column):
-    share = sources[0]
-    kernel = functools.partial(merge_kernel, tuple(sources), column)
-    out_shape = (jax.ShapeDtypeStruct(share.shape, share.dtype),)
-    args = (*sources.values(), *(spare[k] for k in sources if k))
+            def _(source=source, column=column, width=width):
+                out[d, :, column : column + width] = source[slot]
+
+        for number, source in spare.items():
+            count = PLANE - source.shape[0]
+
+            @pl.when((kind == number) & (slot >= count))
+            def _(source=source, count=count):
+                copy = pltpu.make_async_copy(source.at[slot - count], out.at[d], sem)
+                copy.start()
+                copy.wait()
+
+
+def merge(where, sources, spare):
+    layout = tuple((number, column) for number, column, _ in sources)
+    chunks = [c for _, _, c in sources]
+    _, depth, width = spare[1].shape
+    out_shape = (jax.ShapeDtypeStruct((PLANE, depth, width), chunks[0].dtype),)
+    args = (*chunks, spare[1], spare[3], spare[2])
     scratch = [pltpu.SemaphoreType.DMA]
+    kernel = functools.partial(merge_kernel, layout)
     return kernel_call(kernel, out_shape, (where,), args, "merge", len(spare), scratch)[0]
+
+
+def room(n, like):
+    return pl.pallas_call(
+        lambda out: None,
+        out_shape=jax.ShapeDtypeStruct((PLANE - n, *like), jnp.bfloat16),
+        out_specs=pl.BlockSpec(memory_space=pl.ANY),
+        name="room",
+    )()
 
 
 def step_by(n):
@@ -134,37 +149,16 @@
     return {k: lax.ppermute(s, "h", step_by(steps[k])) for k, s in sends.items()}
 
 
-def depart(index, share):
-    return dict(zip((3, 1, 2), pick(index, share, (NEXT, NEXT, FAR))))
-
-
-def pick_late_kernel(index, *refs):
-    outs = refs[-index.shape[0] :]
-    for o, out in enumerate(outs):
-        at = 0
-        for share in refs[: -len(outs)]:
-            width = share.shape[2]
-            out[0, :, at : at + width] = share[index[o, 0]]
-            at += width
-
-
 def late(route, shares, after):
     send_index, _, next_trips, far_trips = route
     start, _ = lax.optimization_barrier((jnp.int32(0), after))
-    depth, width = shares[0].shape[1], sum(s.shape[2] for s in shares)
-
-    def room(n):
-        return jnp.zeros((PLANE - n, depth, width), shares[0].dtype)
+    like = (shares[0].shape[1], sum(s.shape[2] for s in shares))
 
     def trip(first, steps, slots):
         def one(state):
             i, came = state
             index = lax.dynamic_slice(send_index, (first, slots + i), (len(steps), 1))
-            one_chunk = jax.ShapeDtypeStruct((1, depth, width), shares[0].dtype)
-            sends = kernel_call(
-                pick_late_kernel, (one_chunk,) * len(steps), (index,), shares, "pick"
-            )
-            new = hop(dict(zip(steps, sends)))
+            new = hop(dict(zip(steps, pick(index, shares, (1,) * len(steps)))))
             return i + 1, {
                 k: lax.dynamic_update_slice(old, new[k], (i, 0, 0)) for k, old in came.items()
             }
@@ -174,11 +168,11 @@
     _, near = lax.while_loop(
         lambda s: s[0] < next_trips,
         trip(0, (3, 1), NEXT),
-        (start, {1: room(NEXT), 3: room(NEXT)}),
+        (start, {1: room(NEXT, like), 3: room(NEXT, like)}),
     )
     start, _ = lax.optimization_barrier((start, near))
     _, far = lax.while_loop(
-        lambda s: s[0] < far_trips, trip(2, (2,), FAR), (start, {2: room(FAR)})
+        lambda s: s[0] < far_trips, trip(2, (2,), FAR), (start, {2: room(FAR, like)})
     )
     return {**near, **far}
 
@@ -189,22 +183,25 @@
 
 def swap(route, arrays):
     tie = lax.optimization_barrier
-    shares, sent, came, done = [], [], [], []
+    send_index, where = route[:2]
+    shares, sources, sent, column = [], [], [], 0
     for a in arrays:
         a = a.reshape(PLANE, a.shape[0] // PLANE, a.shape[1])
         if shares:
             a, _ = tie((a, shares[-1]))
-        shares.append(over_plane(a))
-        sent.append(depart(route[0], shares[-1]))
-        came.append(hop(sent[-1]))
-    spare, column, placed = late(route, shares, (sent, came[0])), 0, []
-    for share, parts in zip(shares, came):
-        parts, spare = tie((parts, spare))
-        placed.append(merge(route[1], {0: share, **parts}, spare, column))
+        share = over_plane(a)
+        sent.append(pick(send_index[:2], (share,), (NEXT, NEXT)))
+        came = hop(dict(zip((3, 1), sent[-1])))
+        shares.append(share)
+        sources += [(number, column, chunks) for number, chunks in {0: share, **came}.items()]
         column += share.shape[2]
-    placed[0], _ = tie((placed[0], came))
-    done = [over_plane(p) for p in placed]
-    return [d.reshape(a.shape) for d, a in zip(done, arrays)]
+    sent.append(pick(send_index[2:], shares, (FAR,)))
+    far = hop({2: sent[-1][0]})
+    spare = late(route, shares, (sent, [chunks for _, _, chunks in sources[:3]]))
+    sources.append((2, 0, far[2]))
+    placed = over_plane(merge(where, sources, spare)).reshape(-1, column)
+    at = [sum(a.shape[1] for a in arrays[:i]) for i in range(len(arrays))]
+    return [placed[:, i : i + a.shape[1]] for i, a in zip(at, arrays)]
 
 
 rows = (((0,), (0,)), ((), ()))

time: 551 us -> 604 us (1.096)
  the two profiles are of different devices: /device:TPU:1 before, /device:TPU:96 now
where the time goes in v6:
time: 604 us; the launch traced here: 602 us
  waiting for transfers between devices  283 us (47%)
  blocking collectives  139 us (23%)
  starting transfers between devices  102 us (17%)
  Pallas kernels  23.9 us (4%)
  local copies, waits for them, and re-layouts  18 us (3%)
  other arithmetic  15.3 us (3%)
  matrix products  15.2 us (3%)
    ppermute x13, waiting for transfers between devices, hop(): lax.ppermute(s, 'h', step_by(steps[k]))  238 us
    all_to_all x2, blocking collectives, over_plane(): return lax.all_to_all(chunks, FLAT, 0, 0, tiled=True)  89.3 us
    ppermute x13, starting transfers between devices, hop(): lax.ppermute(s, 'h', step_by(steps[k]))  76.9 us
    all_to_all x4, waiting for transfers between devices, over_plane(): return lax.all_to_all(chunks, FLAT, 0, 0, tiled=True)  39 us
    pallas_call x11, Pallas kernels, kernel_call(): pl.pallas_call(kernel, out_shape=out_shape, in_specs=scalars + inside + [...  23.9 us
    all_gather x2, blocking collectives, local_step(): errors = lax.all_gather(error_cols, TENSOR, axis=1, tiled=True)  23.8 us
    all_to_all x4, starting transfers between devices, over_plane(): return lax.all_to_all(chunks, FLAT, 0, 0, tiled=True)  16.4 us
    all_gather x1, blocking collectives, body(): inputs = lax.all_gather(in_cols, TENSOR, axis=2, tiled=True)  14.3 us
  transfers between devices with their start and end apart: 18, of which 10 were waited for; matrix products, arithmetic and copies ran while one was open for 3% of the time, Pallas kernels for 3%

profile of v6, /device:TPU:96, one launch (start us, length us, event | category | flops | bytes accessed | tf_op | source)
XLA Modules:
  0.0 602.3 jit_solution(6552735090393592365)
XLA Ops:
  0.7 0.8 compare_and_fusion.2
  2.2 1.3 gather_fusion
  3.7 14.3 %all-gather = bf16[2,1,128,1024]{3,2,1,0:T(8,128)(2,1)S(1)} all-gather(bf16[2,1,128,128]{3,2,1,0:T(8,128)(2,1)S(1)} %slice.151), channel_id=2, replica_groups=mesh['x'=4,'h'=4,'y'=4,'l'=4,'c'=2] {'l','c'}, dimensions={3}, use_global_device_ids=true | all-gather | bytes 589824 | tf_op jit(solution)/shard_map/all_gather | solution.py:278
  20.4 8.3 %all-to-all-start = ((bf16[8,128,128]{2,1,0:T(8,128)(2,1)}), bf16[8,128,128]{2,1,0:T(8,128)(2,1)}, u32[]{:S(2)}, u32[]{:S(2)}) async-start(bf16[8,128,128]{2,1,0:T(8,128)(2,1)} %bitcast.128), calls=%async_computation | async-start | bytes 524288 | tf_op jit(solution)/shard_map/all_to_all | solution.py:226
  30.2 5.7 all-to-all-done
  35.9 1.0 convert_reduce_fusion.1
  36.9 11.9 %all_gather.10 = bf16[128,1024]{1,0:T(8,128)(2,1)S(1)} all-gather(bf16[128,128]{1,0:T(8,128)(2,1)S(1)} %fusion.35), channel_id=1, replica_groups=mesh['x'=4,'h'=4,'y'=4,'l'=4,'c'=2] {'l','c'}, dimensions={1}, use_global_device_ids=true | all-gather | bytes 294912 | tf_op jit(solution)/shard_map/all_gather | solution.py:231
  49.5 1.3 fusion.17
  50.8 3.6 all-to-all-start.1
  55.1 1.5 multiply_convert_fusion.4
  56.6 1.8 fusion.5
  58.4 11.4 %all-to-all-done.1.refs_0_ = bf16[16,64,384]{2,1,0:T(8,128)(2,1)S(1)} async-done(((bf16[16,64,384]{2,1,0:T(8,128)(2,1)}), bf16[16,64,384]{2,1,0:T(8,128)(2,1)S(1)}, u32[]{:S(2)}, u32[]{:S(2)}) %all-to-all-start.1) | async-done | bytes 786464 | tf_op jit(solution)/shard_map/all_to_all | solution.py:181
  69.8 4.4 all-to-all-start.2
  75.4 1.5 pick.22
  76.9 7.8 %collective-permute-start.6 = (bf16[6,64,384]{2,1,0:T(8,128)(2,1)}, bf16[6,64,384]{2,1,0:T(8,128)(2,1)S(1)}, u32[]{:S(2)}, u32[]{:S(2)}) collective-permute-start(bf16[6,64,384]{2,1,0:T(8,128)(2,1)} %get-tuple-element.359), channel_id=1, source_target_pairs={{0,32},{32,64},{64,96},{96,0},{1,33},{33,65},{65,97},{97,1},{2,34}... | collective-permute-start | bytes 884744 | tf_op jit(solution)/shard_map/ppermute | solution.py:149
  84.8 4.5 collective-permute-start.7
  89.3 8.1 %all-to-all-done.2.refs_0_.refs_1_.refs_3_ = bf16[16,64,768]{2,1,0:T(8,128)(2,1)} async-done(((bf16[16,64,768]{2,1,0:T(8,128)(2,1)}), bf16[16,64,768]{2,1,0:T(8,128)(2,1)}, u32[]{:S(2)}, u32[]{:S(2)}) %all-to-all-start.2) | async-done | bytes 1572896 | tf_op jit(solution)/shard_map/all_to_all | solution.py:181
  97.4 2.7 pick.23
  100.0 6.6 %collective-permute-start.8 = (bf16[6,64,768]{2,1,0:T(8,128)(2,1)}, bf16[6,64,768]{2,1,0:T(8,128)(2,1)S(1)}, u32[]{:S(2)}, u32[]{:S(2)}) collective-permute-start(bf16[6,64,768]{2,1,0:T(8,128)(2,1)} %get-tuple-element.362), channel_id=1, source_target_pairs={{0,32},{32,64},{64,96},{96,0},{1,33},{33,65},{65,97},{97,1},{2,34}... | collective-permute-start | bytes 1769480 | tf_op jit(solution)/shard_map/ppermute | solution.py:149
  106.7 4.5 collective-permute-start.9
  111.1 1.5 pick.24
  112.6 10.8 %collective-permute-start.10 = (bf16[5,64,1152]{2,1,0:T(8,128)(2,1)S(1)}, bf16[5,64,1152]{2,1,0:T(8,128)(2,1)S(1)}, u32[]{:S(2)}, u32[]{:S(2)}) collective-permute-start(bf16[5,64,1152]{2,1,0:T(8,128)(2,1)S(1)} %pick.24), channel_id=1, source_target_pairs={{0,64},{32,96},{64,0},{96,32},{1,65},{33,97},{65,1},{97,33},{2,66}... | collective-permute-start | bytes 2211848 | tf_op jit(solution)/shard_map/ppermute | solution.py:149
  124.8 94.5 %collective-permute-done.8.refs_4_ = bf16[6,64,768]{2,1,0:T(8,128)(2,1)S(1)} collective-permute-done((bf16[6,64,768]{2,1,0:T(8,128)(2,1)}, bf16[6,64,768]{2,1,0:T(8,128)(2,1)S(1)}, u32[]{:S(2)}, u32[]{:S(2)}) %collective-permute-start.8) | collective-permute-done | bytes 589856 | tf_op jit(solution)/shard_map/ppermute | solution.py:149
  219.3 17.7 %collective-permute-done.10.refs_6_ = bf16[5,64,1152]{2,1,0:T(8,128)(2,1)S(1)} collective-permute-done((bf16[5,64,1152]{2,1,0:T(8,128)(2,1)S(1)}, bf16[5,64,1152]{2,1,0:T(8,128)(2,1)S(1)}, u32[]{:S(2)}, u32[]{:S(2)}) %collective-permute-start.10) | collective-permute-done | bytes 737312 | tf_op jit(solution)/shard_map/ppermute | solution.py:149
  237.0 2.7 merge.2
  239.7 38.0 %all_to_all.40 = bf16[16,64,1152]{2,1,0:T(8,128)(2,1)S(1)} all-to-all(bf16[16,64,1152]{2,1,0:T(8,128)(2,1)S(1)} %merge.2), channel_id=1, replica_groups=mesh['x'=4,'h'=4,'y'=4,'l'=4,'c'=2] {'x','y'}, dimensions={0} | all-to-all | bytes 4718592 | tf_op jit(solution)/shard_map/all_to_all | solution.py:181
  277.7 3.4 fusion.6
  281.1 2.3 fusion.16
  285.1 12.1 %all_to_all.41 = bf16[8,128,128]{2,1,0:T(8,128)(2,1)S(1)} all-to-all(bf16[8,128,128]{2,1,0:T(8,128)(2,1)S(1)} %bitcast.151), channel_id=1, replica_groups=mesh['x'=4,'h'=4,'y'=4,'l'=4,'c'=2] {'l','c'}, dimensions={0} | all-to-all | bytes 524288 | tf_op jit(solution)/shard_map/all_to_all | solution.py:226
  297.3 11.9 %all_gather.11 = bf16[128,1024]{1,0:T(8,128)(2,1)S(1)} all-gather(bf16[128,128]{1,0:T(8,128)(2,1)S(1)} %fusion.34), channel_id=1, replica_groups=mesh['x'=4,'h'=4,'y'=4,'l'=4,'c'=2] {'l','c'}, dimensions={1}, use_global_device_ids=true | all-gather | bytes 294912 | tf_op jit(solution)/shard_map/all_gather | solution.py:231
  309.2 3.2 subtract_convert_fusion.1
  312.4 3.8 all-to-all-start.5
  316.2 1.8 multiply_convert_fusion.1
  318.2 4.2 subtract_convert_fusion
  322.3 9.0 %all-to-all-done.5.refs_0_ = bf16[16,64,384]{2,1,0:T(8,128)(2,1)S(1)} async-done(((bf16[16,64,384]{2,1,0:T(8,128)(2,1)}), bf16[16,64,384]{2,1,0:T(8,128)(2,1)S(1)}, u32[]{:S(2)}, u32[]{:S(2)}) %all-to-all-start.5) | async-done | bytes 786464 | tf_op jit(solution)/shard_map/all_to_all | solution.py:181
  331.4 4.6 all-to-all-start.6
  336.0 1.5 pick.25
  337.5 2.0 collective-permute-start.11
  339.5 7.7 %collective-permute-start.12 = (bf16[6,64,384]{2,1,0:T(8,128)(2,1)}, bf16[6,64,384]{2,1,0:T(8,128)(2,1)S(1)}, u32[]{:S(2)}, u32[]{:S(2)}) collective-permute-start(bf16[6,64,384]{2,1,0:T(8,128)(2,1)} %get-tuple-element.370), channel_id=1, source_target_pairs={{0,96},{32,0},{64,32},{96,64},{1,97},{33,1},{65,33},{97,65},{2,98}... | collective-permute-start | bytes 884744 | tf_op jit(solution)/shard_map/ppermute | solution.py:149
  347.3 10.4 %all-to-all-done.6.refs_0_.refs_1_.refs_3_ = bf16[16,64,768]{2,1,0:T(8,128)(2,1)} async-done(((bf16[16,64,768]{2,1,0:T(8,128)(2,1)}), bf16[16,64,768]{2,1,0:T(8,128)(2,1)}, u32[]{:S(2)}, u32[]{:S(2)}) %all-to-all-start.6) | async-done | bytes 1572896 | tf_op jit(solution)/shard_map/all_to_all | solution.py:181
  357.7 2.6 pick.26
  360.3 2.0 collective-permute-start.13
  362.2 7.8 %collective-permute-start.14 = (bf16[6,64,768]{2,1,0:T(8,128)(2,1)}, bf16[6,64,768]{2,1,0:T(8,128)(2,1)S(1)}, u32[]{:S(2)}, u32[]{:S(2)}) collective-permute-start(bf16[6,64,768]{2,1,0:T(8,128)(2,1)} %get-tuple-element.373), channel_id=1, source_target_pairs={{0,96},{32,0},{64,32},{96,64},{1,97},{33,1},{65,33},{97,65},{2,98}... | collective-permute-start | bytes 1769480 | tf_op jit(solution)/shard_map/ppermute | solution.py:149
  370.0 1.7 pick.27
  371.8 4.4 collective-permute-start.15
  376.8 161.0 %while.55 = (s32[]{:T(128)}, bf16[11,64,1152]{2,1,0:T(8,128)(2,1)}, s32[]{:T(128)}, s32[3,16]{1,0:T(4,128)S(1)}, bf16[16,64,384]{2,1,0:T(8,128)(2,1)}, /*index=5...) while((s32[]{:T(128)}, bf16[11,64,1152]{2,1,0:T(8,128)(2,1)}, ...), condition=%wide.region_15.16_spmd, body=%wide.region_14.15_spmd.sunk | while | flops 2506761 | bytes 3391741 | solution.py:174
  378.1 2.3 pick.31
  380.4 10.2 %collective-permute-start.5 = (bf16[1,64,1152]{2,1,0:T(8,128)(2,1)S(1)}, bf16[1,64,1152]{2,1,0:T(8,128)(2,1)}, u32[]{:S(2)}, u32[]{:S(2)}) collective-permute-start(bf16[1,64,1152]{2,1,0:T(8,128)(2,1)S(1)} %pick.31), channel_id=1, source_target_pairs={{0,64},{32,96},{64,0},{96,32},{1,65},{33,97},{65,1},{97,33},{2,66}... | collective-permute-start | bytes 442376 | tf_op jit(solution)/shard_map/while/body/ppermute | solution.py:149
  390.6 82.9 %collective-permute-done.5 = bf16[1,64,1152]{2,1,0:T(8,128)(2,1)} collective-permute-done((bf16[1,64,1152]{2,1,0:T(8,128)(2,1)S(1)}, bf16[1,64,1152]{2,1,0:T(8,128)(2,1)}, u32[]{:S(2)}, u32[]{:S(2)}) %collective-permute-start.5) | collective-permute-done | bytes 147488 | tf_op jit(solution)/shard_map/while/body/ppermute | solution.py:149
  473.5 1.6 constant_dynamic-update-slice_fusion.17
  476.3 2.3 pick.31
  478.6 4.3 collective-permute-start.5
  483.0 31.1 %collective-permute-done.5 = bf16[1,64,1152]{2,1,0:T(8,128)(2,1)} collective-permute-done((bf16[1,64,1152]{2,1,0:T(8,128)(2,1)S(1)}, bf16[1,64,1152]{2,1,0:T(8,128)(2,1)}, u32[]{:S(2)}, u32[]{:S(2)}) %collective-permute-start.5) | collective-permute-done | bytes 147488 | tf_op jit(solution)/shard_map/while/body/ppermute | solution.py:149
  514.1 1.6 constant_dynamic-update-slice_fusion.17
  516.9 2.3 pick.31
  519.2 4.3 collective-permute-start.5
  523.6 12.0 %collective-permute-done.5 = bf16[1,64,1152]{2,1,0:T(8,128)(2,1)} collective-permute-done((bf16[1,64,1152]{2,1,0:T(8,128)(2,1)S(1)}, bf16[1,64,1152]{2,1,0:T(8,128)(2,1)}, u32[]{:S(2)}, u32[]{:S(2)}) %collective-permute-start.5) | collective-permute-done | bytes 147488 | tf_op jit(solution)/shard_map/while/body/ppermute | solution.py:149
  535.6 1.6 constant_dynamic-update-slice_fusion.17
  537.9 2.8 merge.3
  540.7 51.4 %all_to_all.42 = bf16[16,64,1152]{2,1,0:T(8,128)(2,1)S(1)} all-to-all(bf16[16,64,1152]{2,1,0:T(8,128)(2,1)S(1)} %merge.3), channel_id=1, replica_groups=mesh['x'=4,'h'=4,'y'=4,'l'=4,'c'=2] {'x','y'}, dimensions={0} | all-to-all | bytes 4718592 | tf_op jit(solution)/shard_map/all_to_all | solution.py:181
  592.1 2.8 fusion.3
  595.0 1.3 slice_bitcast_fusion
  597.1 2.9 fusion.23
  600.0 2.3 copy.19
  (124 shorter events, 13.8 us)
Async XLA Ops:
  0.6 1.5 copy-start
  0.6 17.3 %copy-start.15 = (bf16[1,1024,384]{2,1,0:T(8,128)(2,1)S(1)}, bf16[1,1024,384]{2,1,0:T(8,128)(2,1)}, u32[]{:S(2)}) copy-start(bf16[1,1024,384]{2,1,0:T(8,128)(2,1)} %param.16) | copy-start | bytes 2359300
  0.7 17.3 %copy-start.18 = (bf16[1,1024,384]{2,1,0:T(8,128)(2,1)S(1)}, bf16[1,1024,384]{2,1,0:T(8,128)(2,1)}, u32[]{:S(2)}) copy-start(bf16[1,1024,384]{2,1,0:T(8,128)(2,1)} %param.15) | copy-start | bytes 2359300
  3.7 33.2 %copy-start.28 = (bf16[2,2,128,128]{3,2,1,0:T(8,128)(2,1)}, bf16[2,2,128,128]{3,2,1,0:T(8,128)(2,1)S(1)}, u32[]{:S(2)}) copy-start(bf16[2,2,128,128]{3,2,1,0:T(8,128)(2,1)S(1)} %broadcast_select_fusion) | copy-start | bytes 393220
  18.0 0.8 copy-start.23
  18.0 1.3 copy-start.14
  18.8 1.6 copy-start.31
  19.6 9.4 %copy-start.33 = (s32[2,64]{1,0:T(2,128)S(1)}, s32[2,64]{1,0:T(2,128)}, u32[]{:S(2)}) copy-start(s32[2,64]{1,0:T(2,128)} %param.20) | copy-start | bytes 1540
  20.4 15.5 %all-to-all-start = ((bf16[8,128,128]{2,1,0:T(8,128)(2,1)}), bf16[8,128,128]{2,1,0:T(8,128)(2,1)}, u32[]{:S(2)}, u32[]{:S(2)}) async-start(bf16[8,128,128]{2,1,0:T(8,128)(2,1)} %bitcast.128), calls=%async_computation | async-start | bytes 524288 | tf_op jit(solution)/shard_map/all_to_all | solution.py:226
  29.0 21.8 %copy-start.9 = (bf16[1,384,1024]{1,2,0:T(8,128)(2,1)}, bf16[1,384,1024]{1,2,0:T(8,128)(2,1)S(1)}, u32[]{:S(2)}) copy-start(bf16[1,384,1024]{1,2,0:T(8,128)(2,1)S(1)} %copy.16) | copy-start | bytes 2359300
  48.8 0.7 copy-start.27
  50.8 19.0 %all-to-all-start.1 = ((bf16[16,64,384]{2,1,0:T(8,128)(2,1)}), bf16[16,64,384]{2,1,0:T(8,128)(2,1)S(1)}, u32[]{:S(2)}, u32[]{:S(2)}) async-start(bf16[16,64,384]{2,1,0:T(8,128)(2,1)} %bitcast.16), calls=%async_computation.1 | async-start | bytes 1572864 | tf_op jit(solution)/shard_map/all_to_all | solution.py:181
  54.4 2.1 copy-start.24
  69.8 5.6 copy-start.1
  69.8 27.5 %all-to-all-start.2 = ((bf16[16,64,768]{2,1,0:T(8,128)(2,1)}), bf16[16,64,768]{2,1,0:T(8,128)(2,1)}, u32[]{:S(2)}, u32[]{:S(2)}) async-start(bf16[16,64,768]{2,1,0:T(8,128)(2,1)} %bitcast.18), calls=%async_computation.2 | async-start | bytes 3145728 | tf_op jit(solution)/shard_map/all_to_all | solution.py:181
  74.2 0.7 copy-start.34
  76.9 46.5 %collective-permute-start.6 = (bf16[6,64,384]{2,1,0:T(8,128)(2,1)}, bf16[6,64,384]{2,1,0:T(8,128)(2,1)S(1)}, u32[]{:S(2)}, u32[]{:S(2)}) collective-permute-start(bf16[6,64,384]{2,1,0:T(8,128)(2,1)} %get-tuple-element.359), channel_id=1, source_target_pairs={{0,32},{32,64},{64,96},{96,0},{1,33},{33,65},{65,97},{97,1},{2,34}... | collective-permute-start | bytes 884744 | tf_op jit(solution)/shard_map/ppermute | solution.py:149
  84.8 38.7 %collective-permute-start.7 = (bf16[6,64,384]{2,1,0:T(8,128)(2,1)}, bf16[6,64,384]{2,1,0:T(8,128)(2,1)S(1)}, u32[]{:S(2)}, u32[]{:S(2)}) collective-permute-start(bf16[6,64,384]{2,1,0:T(8,128)(2,1)} %get-tuple-element.360), channel_id=1, source_target_pairs={{0,96},{32,0},{64,32},{96,64},{1,97},{33,1},{65,33},{97,65},{2,98}... | collective-permute-start | bytes 884744 | tf_op jit(solution)/shard_map/ppermute | solution.py:149
  97.3 13.8 %copy-start.2 = (bf16[16,64,384]{2,1,0:T(8,128)(2,1)S(1)}, bf16[16,64,384]{2,1,0:T(8,128)(2,1)}, u32[]{:S(2)}) copy-start(bf16[16,64,384]{2,1,0:T(8,128)(2,1)} %copy-done.1) | copy-start | bytes 2359300
  100.0 119.3 %collective-permute-start.8 = (bf16[6,64,768]{2,1,0:T(8,128)(2,1)}, bf16[6,64,768]{2,1,0:T(8,128)(2,1)S(1)}, u32[]{:S(2)}, u32[]{:S(2)}) collective-permute-start(bf16[6,64,768]{2,1,0:T(8,128)(2,1)} %get-tuple-element.362), channel_id=1, source_target_pairs={{0,32},{32,64},{64,96},{96,0},{1,33},{33,65},{65,97},{97,1},{2,34}... | collective-permute-start | bytes 1769480 | tf_op jit(solution)/shard_map/ppermute | solution.py:149
  106.7 112.6 %collective-permute-start.9 = (bf16[6,64,768]{2,1,0:T(8,128)(2,1)}, bf16[6,64,768]{2,1,0:T(8,128)(2,1)S(1)}, u32[]{:S(2)}, u32[]{:S(2)}) collective-permute-start(bf16[6,64,768]{2,1,0:T(8,128)(2,1)} %get-tuple-element.363), channel_id=1, source_target_pairs={{0,96},{32,0},{64,32},{96,64},{1,97},{33,1},{65,33},{97,65},{2,98}... | collective-permute-start | bytes 1769480 | tf_op jit(solution)/shard_map/ppermute | solution.py:149
  112.6 124.3 %collective-permute-start.10 = (bf16[5,64,1152]{2,1,0:T(8,128)(2,1)S(1)}, bf16[5,64,1152]{2,1,0:T(8,128)(2,1)S(1)}, u32[]{:S(2)}, u32[]{:S(2)}) collective-permute-start(bf16[5,64,1152]{2,1,0:T(8,128)(2,1)S(1)} %pick.24), channel_id=1, source_target_pairs={{0,64},{32,96},{64,0},{96,32},{1,65},{33,97},{65,1},{97,33},{2,66}... | collective-permute-start | bytes 2211848 | tf_op jit(solution)/shard_map/ppermute | solution.py:149
  239.7 38.0 %copy-start.16 = (bf16[1,1024,384]{2,1,0:T(8,128)(2,1)S(1)}, bf16[1,1024,384]{2,1,0:T(8,128)(2,1)}, u32[]{:S(2)}) copy-start(bf16[1,1024,384]{2,1,0:T(8,128)(2,1)} %param.16) | copy-start | bytes 2359300
  239.7 38.0 %copy-start.19 = (bf16[1,1024,384]{2,1,0:T(8,128)(2,1)S(1)}, bf16[1,1024,384]{2,1,0:T(8,128)(2,1)}, u32[]{:S(2)}) copy-start(bf16[1,1024,384]{2,1,0:T(8,128)(2,1)} %param.15) | copy-start | bytes 2359300
  277.6 40.4 %copy-start.4 = (bf16[16,64,1152]{2,1,0:T(8,128)(2,1)}, bf16[16,64,1152]{2,1,0:T(8,128)(2,1)S(1)}, u32[]{:S(2)}) copy-start(bf16[16,64,1152]{2,1,0:T(8,128)(2,1)S(1)} %all_to_all.40) | copy-start | bytes 7077892
  277.6 3.5 copy-start.10
  281.1 2.3 copy-start.6
  281.1 2.3 copy-start.25
  283.5 25.7 %copy-start.12 = (bf16[1024,384]{1,0:T(8,128)(2,1)}, bf16[1024,384]{1,0:T(8,128)(2,1)S(1)}, u32[]{:S(2)}) copy-start(bf16[1024,384]{1,0:T(8,128)(2,1)S(1)} %fusion.16) | copy-start | bytes 2359300
  283.9 0.7 copy-start.21
  284.6 12.6 %copy-start.29 = (bf16[2,2,128,128]{3,2,1,0:T(8,128)(2,1)S(1)}, bf16[2,2,128,128]{3,2,1,0:T(8,128)(2,1)}, u32[]{:S(2)}) copy-start(bf16[2,2,128,128]{3,2,1,0:T(8,128)(2,1)} %copy-done.28) | copy-start | bytes 393220
  309.2 3.2 copy-start.32
  312.4 19.0 %all-to-all-start.5 = ((bf16[16,64,384]{2,1,0:T(8,128)(2,1)}), bf16[16,64,384]{2,1,0:T(8,128)(2,1)S(1)}, u32[]{:S(2)}, u32[]{:S(2)}) async-start(bf16[16,64,384]{2,1,0:T(8,128)(2,1)} %bitcast.152), calls=%async_computation.5 | async-start | bytes 1572864 | tf_op jit(solution)/shard_map/all_to_all | solution.py:181
  316.2 1.8 copy-start.7
  316.2 1.9 copy-start.26
  331.4 4.6 copy-start.3
  331.4 26.3 %all-to-all-start.6 = ((bf16[16,64,768]{2,1,0:T(8,128)(2,1)}), bf16[16,64,768]{2,1,0:T(8,128)(2,1)}, u32[]{:S(2)}, u32[]{:S(2)}) async-start(bf16[16,64,768]{2,1,0:T(8,128)(2,1)} %bitcast.150), calls=%async_computation.6 | async-start | bytes 3145728 | tf_op jit(solution)/shard_map/all_to_all | solution.py:181
  337.5 38.7 %collective-permute-start.11 = (bf16[6,64,384]{2,1,0:T(8,128)(2,1)}, bf16[6,64,384]{2,1,0:T(8,128)(2,1)S(1)}, u32[]{:S(2)}, u32[]{:S(2)}) collective-permute-start(bf16[6,64,384]{2,1,0:T(8,128)(2,1)} %get-tuple-element.369), channel_id=1, source_target_pairs={{0,32},{32,64},{64,96},{96,0},{1,33},{33,65},{65,97},{97,1},{2,34}... | collective-permute-start | bytes 884744 | tf_op jit(solution)/shard_map/ppermute | solution.py:149
  339.5 36.7 %collective-permute-start.12 = (bf16[6,64,384]{2,1,0:T(8,128)(2,1)}, bf16[6,64,384]{2,1,0:T(8,128)(2,1)S(1)}, u32[]{:S(2)}, u32[]{:S(2)}) collective-permute-start(bf16[6,64,384]{2,1,0:T(8,128)(2,1)} %get-tuple-element.370), channel_id=1, source_target_pairs={{0,96},{32,0},{64,32},{96,64},{1,97},{33,1},{65,33},{97,65},{2,98}... | collective-permute-start | bytes 884744 | tf_op jit(solution)/shard_map/ppermute | solution.py:149
  360.3 177.5 %collective-permute-start.13 = (bf16[6,64,768]{2,1,0:T(8,128)(2,1)}, bf16[6,64,768]{2,1,0:T(8,128)(2,1)S(1)}, u32[]{:S(2)}, u32[]{:S(2)}) collective-permute-start(bf16[6,64,768]{2,1,0:T(8,128)(2,1)} %get-tuple-element.372), channel_id=1, source_target_pairs={{0,32},{32,64},{64,96},{96,0},{1,33},{33,65},{65,97},{97,1},{2,34}... | collective-permute-start | bytes 1769480 | tf_op jit(solution)/shard_map/ppermute | solution.py:149
  362.2 175.6 %collective-permute-start.14 = (bf16[6,64,768]{2,1,0:T(8,128)(2,1)}, bf16[6,64,768]{2,1,0:T(8,128)(2,1)S(1)}, u32[]{:S(2)}, u32[]{:S(2)}) collective-permute-start(bf16[6,64,768]{2,1,0:T(8,128)(2,1)} %get-tuple-element.373), channel_id=1, source_target_pairs={{0,96},{32,0},{64,32},{96,64},{1,97},{33,1},{65,33},{97,65},{2,98}... | collective-permute-start | bytes 1769480 | tf_op jit(solution)/shard_map/ppermute | solution.py:149
  371.8 166.1 %collective-permute-start.15 = (bf16[5,64,1152]{2,1,0:T(8,128)(2,1)S(1)}, bf16[5,64,1152]{2,1,0:T(8,128)(2,1)S(1)}, u32[]{:S(2)}, u32[]{:S(2)}) collective-permute-start(bf16[5,64,1152]{2,1,0:T(8,128)(2,1)S(1)} %pick.27), channel_id=1, source_target_pairs={{0,64},{32,96},{64,0},{96,32},{1,65},{33,97},{65,1},{97,33},{2,66}... | collective-permute-start | bytes 2211848 | tf_op jit(solution)/shard_map/ppermute | solution.py:149
  380.4 93.1 %collective-permute-start.5 = (bf16[1,64,1152]{2,1,0:T(8,128)(2,1)S(1)}, bf16[1,64,1152]{2,1,0:T(8,128)(2,1)}, u32[]{:S(2)}, u32[]{:S(2)}) collective-permute-start(bf16[1,64,1152]{2,1,0:T(8,128)(2,1)S(1)} %pick.31), channel_id=1, source_target_pairs={{0,64},{32,96},{64,0},{96,32},{1,65},{33,97},{65,1},{97,33},{2,66}... | collective-permute-start | bytes 442376 | tf_op jit(solution)/shard_map/while/body/ppermute | solution.py:149
  478.6 35.5 %collective-permute-start.5 = (bf16[1,64,1152]{2,1,0:T(8,128)(2,1)S(1)}, bf16[1,64,1152]{2,1,0:T(8,128)(2,1)}, u32[]{:S(2)}, u32[]{:S(2)}) collective-permute-start(bf16[1,64,1152]{2,1,0:T(8,128)(2,1)S(1)} %pick.31), channel_id=1, source_target_pairs={{0,64},{32,96},{64,0},{96,32},{1,65},{33,97},{65,1},{97,33},{2,66}... | collective-permute-start | bytes 442376 | tf_op jit(solution)/shard_map/while/body/ppermute | solution.py:149
  519.2 16.3 %collective-permute-start.5 = (bf16[1,64,1152]{2,1,0:T(8,128)(2,1)S(1)}, bf16[1,64,1152]{2,1,0:T(8,128)(2,1)}, u32[]{:S(2)}, u32[]{:S(2)}) collective-permute-start(bf16[1,64,1152]{2,1,0:T(8,128)(2,1)S(1)} %pick.31), channel_id=1, source_target_pairs={{0,64},{32,96},{64,0},{96,32},{1,65},{33,97},{65,1},{97,33},{2,66}... | collective-permute-start | bytes 442376 | tf_op jit(solution)/shard_map/while/body/ppermute | solution.py:149
  537.8 54.2 %copy-start.20 = (bf16[1,1024,384]{2,1,0:T(8,128)(2,1)S(1)}, bf16[1,1024,384]{2,1,0:T(8,128)(2,1)}, u32[]{:S(2)}) copy-start(bf16[1,1024,384]{2,1,0:T(8,128)(2,1)} %param.15) | copy-start | bytes 2359300
  537.9 54.2 %copy-start.22 = (bf16[1024,768]{1,0:T(8,128)(2,1)S(1)}, bf16[1024,768]{1,0:T(8,128)(2,1)}, u32[]{:S(2)}) copy-start(bf16[1024,768]{1,0:T(8,128)(2,1)} %get-tuple-element.466) | copy-start | bytes 4718596
  540.7 51.4 %copy-start.5 = (bf16[16,64,1152]{2,1,0:T(8,128)(2,1)S(1)}, bf16[16,64,1152]{2,1,0:T(8,128)(2,1)}, u32[]{:S(2)}) copy-start(bf16[16,64,1152]{2,1,0:T(8,128)(2,1)} %copy-done.4) | copy-start | bytes 7077892
  540.7 51.4 %copy-start.8 = (bf16[1024,768]{1,0:T(8,128)(2,1)S(1)}, bf16[1024,768]{1,0:T(8,128)(2,1)}, u32[]{:S(2)}) copy-start(bf16[1024,768]{1,0:T(8,128)(2,1)} %copy-done.6) | copy-start | bytes 4718596
  540.7 51.4 %copy-start.17 = (bf16[1,1024,384]{2,1,0:T(8,128)(2,1)S(1)}, bf16[1,1024,384]{2,1,0:T(8,128)(2,1)}, u32[]{:S(2)}) copy-start(bf16[1,1024,384]{2,1,0:T(8,128)(2,1)} %param.16) | copy-start | bytes 2359300
  594.9 1.3 copy-start.11
  595.0 1.9 copy-start.13
  595.0 2.2 copy-start.30

commit v7 on v5

--- a/solution.py
+++ b/solution.py
@@ -125,6 +125,15 @@
     return kernel_call(kernel, out_shape, (where,), args, "merge", len(spare), scratch)[0]
 
 
+def room(n, like):
+    return pl.pallas_call(
+        lambda out: None,
+        out_shape=jax.ShapeDtypeStruct((PLANE - n, *like), jnp.bfloat16),
+        out_specs=pl.BlockSpec(memory_space=pl.ANY),
+        name="room",
+    )()
+
+
 def step_by(n):
     return [(i, (i + n) % PLANES) for i in range(PLANES)]
 
@@ -152,9 +161,6 @@
     send_index, _, next_trips, far_trips = route
     start, _ = lax.optimization_barrier((jnp.int32(0), after))
     depth, width = shares[0].shape[1], sum(s.shape[2] for s in shares)
-
-    def room(n):
-        return jnp.zeros((PLANE - n, depth, width), shares[0].dtype)
 
     def trip(first, steps, slots):
         def one(state):
@@ -174,11 +180,11 @@
     _, near = lax.while_loop(
         lambda s: s[0] < next_trips,
         trip(0, (3, 1), NEXT),
-        (start, {1: room(NEXT), 3: room(NEXT)}),
+        (start, {1: room(NEXT, (depth, width)), 3: room(NEXT, (depth, width))}),
     )
     start, _ = lax.optimization_barrier((start, near))
     _, far = lax.while_loop(
-        lambda s: s[0] < far_trips, trip(2, (2,), FAR), (start, {2: room(FAR)})
+        lambda s: s[0] < far_trips, trip(2, (2,), FAR), (start, {2: room(FAR, (depth, width))})
     )
     return {**near, **far}
 
@@ -202,7 +208,7 @@
         parts, spare = tie((parts, spare))
         placed.append(merge(route[1], {0: share, **parts}, spare, column))
         column += share.shape[2]
-    placed[0], _ = tie((placed[0], came))
+    placed[0], _ = tie((placed[0], (came[0], came[1][1], came[1][3])))
     done = [over_plane(p) for p in placed]
     return [d.reshape(a.shape) for d, a in zip(done, arrays)]
 
@@ -289,9 +295,10 @@
     stepped = local_step(weights, inputs[1], in_cols[1], out_cols[1])
     shares = tuple(make_share(s, m) for s, m in zip(stepped, moments))
     theirs = partner_copy(last, shares)
-    new = [final_update(*each) for each in zip(weights, stepped, moments, theirs)]
-    both, down = new
-    return both[None, :, :HID], both[None, :, HID:], down.T[None]
+    both, down = zip(weights, stepped, moments, theirs)
+    gate = final_update(*(a[:, :HID] for a in both))
+    up = final_update(*(a[:, HID:] for a in both))
+    return gate[None], up[None], final_update(*(a.T for a in down))[None]
 
 
 def solution(mesh):

time: 551 us -> 567 us (1.029)
  the two profiles are of different devices: /device:TPU:1 before, /device:TPU:32 now
where the time goes in v7:
time: 567 us; the launch traced here: 566 us
  waiting for transfers between devices  258 us (46%)
  starting transfers between devices  170 us (30%)
  blocking collectives  66.8 us (12%)
  Pallas kernels  21.4 us (4%)
  other arithmetic  16.7 us (3%)
  matrix products  15.2 us (3%)
  local copies, waits for them, and re-layouts  13.5 us (2%)
    ppermute x14, waiting for transfers between devices, hop(): lax.ppermute(s, 'h', step_by(steps[k]))  198 us
    ppermute x14, starting transfers between devices, hop(): lax.ppermute(s, 'h', step_by(steps[k]))  111 us
    all_to_all x8, waiting for transfers between devices, over_plane(): return lax.all_to_all(chunks, FLAT, 0, 0, tiled=True)  52.8 us
    all_to_all x8, starting transfers between devices, over_plane(): return lax.all_to_all(chunks, FLAT, 0, 0, tiled=True)  51.9 us
    all_to_all x1, blocking collectives, local_step(): terms = lax.all_to_all(blocks, TENSOR, 0, 0, tiled=True)  25.7 us
    all_gather x2, blocking collectives, local_step(): errors = lax.all_gather(error_cols, TENSOR, axis=1, tiled=True)  24.7 us
    pallas_call x9, Pallas kernels, kernel_call(): pl.pallas_call(kernel, out_shape=out_shape, in_specs=scalars + inside + [...  21.4 us
    all_gather x1, blocking collectives, body(): inputs = lax.all_gather(in_cols, TENSOR, axis=2, tiled=True)  16.4 us
  transfers between devices with their start and end apart: 23, of which 13 were waited for; matrix products, arithmetic and copies ran while one was open for 4% of the time, Pallas kernels for 4%

profile of v7, /device:TPU:32, one launch (start us, length us, event | category | flops | bytes accessed | tf_op | source)
XLA Modules:
  0.0 565.9 jit_solution(5755296028907771848)
XLA Ops:
  2.2 1.3 gather_fusion
  3.7 16.4 %all-gather = bf16[2,1,128,1024]{3,2,1,0:T(8,128)(2,1)S(1)} all-gather(bf16[2,1,128,128]{3,2,1,0:T(8,128)(2,1)S(1)} %slice.121), channel_id=2, replica_groups=mesh['x'=4,'h'=4,'y'=4,'l'=4,'c'=2] {'l','c'}, dimensions={3}, use_global_device_ids=true | all-gather | bytes 589824 | tf_op jit(solution)/shard_map/all_gather | solution.py:287
  22.6 6.4 %all-to-all-start = ((bf16[8,128,128]{2,1,0:T(8,128)(2,1)}), bf16[8,128,128]{2,1,0:T(8,128)(2,1)S(1)}, u32[]{:S(2)}, u32[]{:S(2)}) async-start(bf16[8,128,128]{2,1,0:T(8,128)(2,1)} %bitcast.135), calls=%async_computation | async-start | bytes 524288 | tf_op jit(solution)/shard_map/all_to_all | solution.py:235
  29.5 7.4 %all-to-all-done = bf16[8,128,128]{2,1,0:T(8,128)(2,1)S(1)} async-done(((bf16[8,128,128]{2,1,0:T(8,128)(2,1)}), bf16[8,128,128]{2,1,0:T(8,128)(2,1)S(1)}, u32[]{:S(2)}, u32[]{:S(2)}) %all-to-all-start) | async-done | bytes 262176 | tf_op jit(solution)/shard_map/all_to_all | solution.py:235
  37.0 12.4 %all_gather.10 = bf16[128,1024]{1,0:T(8,128)(2,1)S(1)} all-gather(bf16[128,128]{1,0:T(8,128)(2,1)S(1)} %fusion.35), channel_id=1, replica_groups=mesh['x'=4,'h'=4,'y'=4,'l'=4,'c'=2] {'l','c'}, dimensions={1}, use_global_device_ids=true | all-gather | bytes 294912 | tf_op jit(solution)/shard_map/all_gather | solution.py:240
  49.3 1.3 fusion.15
  50.6 3.6 all-to-all-start.1
  54.4 1.5 multiply_convert_fusion.4
  55.9 1.8 fusion
  57.7 11.9 %all-to-all-done.1.chunks.refs_0_ = bf16[16,64,384]{2,1,0:T(8,128)(2,1)S(1)} async-done(((bf16[16,64,384]{2,1,0:T(8,128)(2,1)}), bf16[16,64,384]{2,1,0:T(8,128)(2,1)S(1)}, u32[]{:S(2)}, u32[]{:S(2)}) %all-to-all-start.1) | async-done | bytes 786464 | tf_op jit(solution)/shard_map/all_to_all | solution.py:193
  69.6 4.5 all-to-all-start.2
  74.8 1.7 pick.21
  76.5 10.4 %collective-permute-start.9 = (bf16[6,64,384]{2,1,0:T(8,128)(2,1)}, bf16[6,64,384]{2,1,0:T(8,128)(2,1)S(1)}, u32[]{:S(2)}, u32[]{:S(2)}) collective-permute-start(bf16[6,64,384]{2,1,0:T(8,128)(2,1)} %get-tuple-element.393), channel_id=1, source_target_pairs={{0,96},{32,0},{64,32},{96,64},{1,97},{33,1},{65,33},{97,65},{2,98}... | collective-permute-start | bytes 884744 | tf_op jit(solution)/shard_map/ppermute | solution.py:143
  86.9 5.0 collective-permute-start.10
  91.9 7.8 %collective-permute-start.11 = (bf16[6,64,384]{2,1,0:T(8,128)(2,1)}, bf16[6,64,384]{2,1,0:T(8,128)(2,1)S(1)}, u32[]{:S(2)}, u32[]{:S(2)}) collective-permute-start(bf16[6,64,384]{2,1,0:T(8,128)(2,1)} %get-tuple-element.395), channel_id=1, source_target_pairs={{0,32},{32,64},{64,96},{96,0},{1,33},{33,65},{65,97},{97,1},{2,34}... | collective-permute-start | bytes 884744 | tf_op jit(solution)/shard_map/ppermute | solution.py:143
  101.0 1.6 pick.20
  103.4 5.4 collective-permute-start.6
  108.9 4.3 collective-permute-start.8
  113.2 22.1 %collective-permute-done.10.refs_2_ = bf16[5,64,384]{2,1,0:T(8,128)(2,1)S(1)} collective-permute-done((bf16[5,64,384]{2,1,0:T(8,128)(2,1)}, bf16[5,64,384]{2,1,0:T(8,128)(2,1)S(1)}, u32[]{:S(2)}, u32[]{:S(2)}) %collective-permute-start.10) | collective-permute-done | bytes 245792 | tf_op jit(solution)/shard_map/ppermute | solution.py:143
  135.3 11.2 %collective-permute-done.11.refs_3_ = bf16[6,64,384]{2,1,0:T(8,128)(2,1)S(1)} collective-permute-done((bf16[6,64,384]{2,1,0:T(8,128)(2,1)}, bf16[6,64,384]{2,1,0:T(8,128)(2,1)S(1)}, u32[]{:S(2)}, u32[]{:S(2)}) %collective-permute-start.11) | collective-permute-done | bytes 294944 | tf_op jit(solution)/shard_map/ppermute | solution.py:143
  146.5 40.2 %while.52 = (s32[]{:T(128)}, bf16[10,64,1152]{2,1,0:T(8,128)(2,1)}, bf16[10,64,1152]{2,1,0:T(8,128)(2,1)}, s32[]{:T(128)}, s32[3,16]{1,0:T(4,128)S(1)}, /*index=...) while((s32[]{:T(128)}, bf16[10,64,1152]{2,1,0:T(8,128)(2,1)}, ...), condition=%wide.region_7.8_spmd, body=%wide.region_6.7_spmd.sunk | while | flops 2654217 | bytes 4423993 | solution.py:180
  147.2 2.4 pick.24
  149.6 10.6 %collective-permute-start = (bf16[1,64,1152]{2,1,0:T(8,128)(2,1)}, bf16[1,64,1152]{2,1,0:T(8,128)(2,1)}, u32[]{:S(2)}, u32[]{:S(2)}) collective-permute-start(bf16[1,64,1152]{2,1,0:T(8,128)(2,1)} %get-tuple-element.675), channel_id=1, source_target_pairs={{0,96},{32,0},{64,32},{96,64},{1,97},{33,1},{65,33},{97,65},{2,98}... | collective-permute-start | bytes 442376 | tf_op jit(solution)/shard_map/while/body/ppermute | solution.py:143
  160.2 1.9 collective-permute-start.1
  162.1 20.7 %collective-permute-done = bf16[1,64,1152]{2,1,0:T(8,128)(2,1)} collective-permute-done((bf16[1,64,1152]{2,1,0:T(8,128)(2,1)}, bf16[1,64,1152]{2,1,0:T(8,128)(2,1)}, u32[]{:S(2)}, u32[]{:S(2)}) %collective-permute-start) | collective-permute-done | bytes 147488 | tf_op jit(solution)/shard_map/while/body/ppermute | solution.py:143
  182.9 1.6 constant_dynamic-update-slice_fusion.12
  184.5 1.6 constant_dynamic-update-slice_fusion.13
  187.3 2.8 merge.5
  190.1 12.1 %all-to-all-start.4 = ((bf16[16,64,384]{2,1,0:T(8,128)(2,1)}), bf16[16,64,384]{2,1,0:T(8,128)(2,1)S(1)}, u32[]{:S(2)}, u32[]{:S(2)}) async-start(bf16[16,64,384]{2,1,0:T(8,128)(2,1)} %merge.5), calls=%async_computation.4 | async-start | bytes 1572864 | tf_op jit(solution)/shard_map/all_to_all | solution.py:193
  202.3 24.9 %collective-permute-start.7 = (bf16[5,64,768]{2,1,0:T(8,128)(2,1)S(1)}, bf16[5,64,768]{2,1,0:T(8,128)(2,1)S(1)}, u32[]{:S(2)}, u32[]{:S(2)}) collective-permute-start(bf16[5,64,768]{2,1,0:T(8,128)(2,1)S(1)} %copy-done.4), channel_id=1, source_target_pairs={{0,64},{32,96},{64,0},{96,32},{1,65},{33,97},{65,1},{97,33},{2,66}... | collective-permute-start | bytes 1474568 | tf_op jit(solution)/shard_map/ppermute | solution.py:143
  227.2 26.0 %collective-permute-done.7.refs_2_ = bf16[5,64,768]{2,1,0:T(8,128)(2,1)S(1)} collective-permute-done((bf16[5,64,768]{2,1,0:T(8,128)(2,1)S(1)}, bf16[5,64,768]{2,1,0:T(8,128)(2,1)S(1)}, u32[]{:S(2)}, u32[]{:S(2)}) %collective-permute-start.7) | collective-permute-done | bytes 491552 | tf_op jit(solution)/shard_map/ppermute | solution.py:143
  253.3 3.4 merge.4
  256.7 6.5 %all-to-all-start.3 = ((bf16[16,64,768]{2,1,0:T(8,128)(2,1)}), bf16[16,64,768]{2,1,0:T(8,128)(2,1)}, u32[]{:S(2)}, u32[]{:S(2)}) async-start(bf16[16,64,768]{2,1,0:T(8,128)(2,1)} %merge.4), calls=%async_computation.3 | async-start | bytes 3145728 | tf_op jit(solution)/shard_map/all_to_all | solution.py:193
  263.2 2.6 fusion.12
  265.8 13.6 %all-to-all-done.3 = bf16[16,64,768]{2,1,0:T(8,128)(2,1)} async-done(((bf16[16,64,768]{2,1,0:T(8,128)(2,1)}), bf16[16,64,768]{2,1,0:T(8,128)(2,1)}, u32[]{:S(2)}, u32[]{:S(2)}) %all-to-all-start.3) | async-done | bytes 1572896 | tf_op jit(solution)/shard_map/all_to_all | solution.py:193
  279.4 3.5 fusion.1
  285.1 25.7 %all_to_all.50 = bf16[8,128,128]{2,1,0:T(8,128)(2,1)S(1)} all-to-all(bf16[8,128,128]{2,1,0:T(8,128)(2,1)S(1)} %bitcast.142), channel_id=1, replica_groups=mesh['x'=4,'h'=4,'y'=4,'l'=4,'c'=2] {'l','c'}, dimensions={0} | all-to-all | bytes 524288 | tf_op jit(solution)/shard_map/all_to_all | solution.py:235
  310.9 12.4 %all_gather.11 = bf16[128,1024]{1,0:T(8,128)(2,1)S(1)} all-gather(bf16[128,128]{1,0:T(8,128)(2,1)S(1)} %fusion.34), channel_id=1, replica_groups=mesh['x'=4,'h'=4,'y'=4,'l'=4,'c'=2] {'l','c'}, dimensions={1}, use_global_device_ids=true | all-gather | bytes 294912 | tf_op jit(solution)/shard_map/all_gather | solution.py:240
  323.3 3.2 subtract_convert_fusion.2
  326.5 4.0 all-to-all-start.6
  330.5 1.5 multiply_convert_fusion.1
  332.2 4.6 subtract_convert_fusion
  336.7 8.8 %all-to-all-done.6.chunks.refs_0_ = bf16[16,64,384]{2,1,0:T(8,128)(2,1)S(1)} async-done(((bf16[16,64,384]{2,1,0:T(8,128)(2,1)}), bf16[16,64,384]{2,1,0:T(8,128)(2,1)S(1)}, u32[]{:S(2)}, u32[]{:S(2)}) %all-to-all-start.6) | async-done | bytes 786464 | tf_op jit(solution)/shard_map/all_to_all | solution.py:193
  345.6 4.4 all-to-all-start.7
  350.0 1.7 pick.23
  351.7 9.2 %collective-permute-start.15 = (bf16[6,64,384]{2,1,0:T(8,128)(2,1)}, bf16[6,64,384]{2,1,0:T(8,128)(2,1)S(1)}, u32[]{:S(2)}, u32[]{:S(2)}) collective-permute-start(bf16[6,64,384]{2,1,0:T(8,128)(2,1)} %get-tuple-element.418), channel_id=1, source_target_pairs={{0,96},{32,0},{64,32},{96,64},{1,97},{33,1},{65,33},{97,65},{2,98}... | collective-permute-start | bytes 884744 | tf_op jit(solution)/shard_map/ppermute | solution.py:143
  361.0 4.0 collective-permute-start.17
  365.0 7.3 %collective-permute-start.16 = (bf16[5,64,384]{2,1,0:T(8,128)(2,1)}, bf16[5,64,384]{2,1,0:T(8,128)(2,1)S(1)}, u32[]{:S(2)}, u32[]{:S(2)}) collective-permute-start(bf16[5,64,384]{2,1,0:T(8,128)(2,1)} %get-tuple-element.419), channel_id=1, source_target_pairs={{0,64},{32,96},{64,0},{96,32},{1,65},{33,97},{65,1},{97,33},{2,66}... | collective-permute-start | bytes 737288 | tf_op jit(solution)/shard_map/ppermute | solution.py:143
  372.3 1.6 pick.22
  374.8 9.1 %collective-permute-start.12 = (bf16[6,64,768]{2,1,0:T(8,128)(2,1)S(1)}, bf16[6,64,768]{2,1,0:T(8,128)(2,1)S(1)}, u32[]{:S(2)}, u32[]{:S(2)}) collective-permute-start(bf16[6,64,768]{2,1,0:T(8,128)(2,1)S(1)} %get-tuple-element.415), channel_id=1, source_target_pairs={{0,96},{32,0},{64,32},{96,64},{1,97},{33,1},{65,33},{97,65},{2,98}... | collective-permute-start | bytes 1769480 | tf_op jit(solution)/shard_map/ppermute | solution.py:143
  383.8 4.0 collective-permute-start.14
  387.9 8.3 %collective-permute-done.16.refs_2_ = bf16[5,64,384]{2,1,0:T(8,128)(2,1)S(1)} collective-permute-done((bf16[5,64,384]{2,1,0:T(8,128)(2,1)}, bf16[5,64,384]{2,1,0:T(8,128)(2,1)S(1)}, u32[]{:S(2)}, u32[]{:S(2)}) %collective-permute-start.16) | collective-permute-done | bytes 245792 | tf_op jit(solution)/shard_map/ppermute | solution.py:143
  397.5 2.8 merge.7
  400.3 5.2 collective-permute-done.12.refs_1_
  405.5 57.1 %collective-permute-done.14.refs_3_ = bf16[6,64,768]{2,1,0:T(8,128)(2,1)S(1)} collective-permute-done((bf16[6,64,768]{2,1,0:T(8,128)(2,1)S(1)}, bf16[6,64,768]{2,1,0:T(8,128)(2,1)S(1)}, u32[]{:S(2)}, u32[]{:S(2)}) %collective-permute-start.14) | collective-permute-done | bytes 589856 | tf_op jit(solution)/shard_map/ppermute | solution.py:143
  462.5 9.6 %all-to-all-start.9 = ((bf16[16,64,384]{2,1,0:T(8,128)(2,1)}), bf16[16,64,384]{2,1,0:T(8,128)(2,1)S(1)}, u32[]{:S(2)}, u32[]{:S(2)}) async-start(bf16[16,64,384]{2,1,0:T(8,128)(2,1)} %merge.7), calls=%async_computation.9 | async-start | bytes 1572864 | tf_op jit(solution)/shard_map/all_to_all | solution.py:193
  472.2 7.4 %collective-permute-start.13 = (bf16[5,64,768]{2,1,0:T(8,128)(2,1)S(1)}, bf16[5,64,768]{2,1,0:T(8,128)(2,1)S(1)}, u32[]{:S(2)}, u32[]{:S(2)}) collective-permute-start(bf16[5,64,768]{2,1,0:T(8,128)(2,1)S(1)} %copy-done.2), channel_id=1, source_target_pairs={{0,64},{32,96},{64,0},{96,32},{1,65},{33,97},{65,1},{97,33},{2,66}... | collective-permute-start | bytes 1474568 | tf_op jit(solution)/shard_map/ppermute | solution.py:143
  479.6 47.1 %collective-permute-done.13.refs_2_ = bf16[5,64,768]{2,1,0:T(8,128)(2,1)S(1)} collective-permute-done((bf16[5,64,768]{2,1,0:T(8,128)(2,1)S(1)}, bf16[5,64,768]{2,1,0:T(8,128)(2,1)S(1)}, u32[]{:S(2)}, u32[]{:S(2)}) %collective-permute-start.13) | collective-permute-done | bytes 491552 | tf_op jit(solution)/shard_map/ppermute | solution.py:143
  526.7 3.4 merge.6
  530.1 7.1 %all-to-all-start.8 = ((bf16[16,64,768]{2,1,0:T(8,128)(2,1)}), bf16[16,64,768]{2,1,0:T(8,128)(2,1)}, u32[]{:S(2)}, u32[]{:S(2)}) async-start(bf16[16,64,768]{2,1,0:T(8,128)(2,1)} %merge.6), calls=%async_computation.8 | async-start | bytes 3145728 | tf_op jit(solution)/shard_map/all_to_all | solution.py:193
  537.3 3.1 fusion.23
  540.4 2.4 copy.19
  542.8 18.5 %all-to-all-done.8 = bf16[16,64,768]{2,1,0:T(8,128)(2,1)} async-done(((bf16[16,64,768]{2,1,0:T(8,128)(2,1)}), bf16[16,64,768]{2,1,0:T(8,128)(2,1)}, u32[]{:S(2)}, u32[]{:S(2)}) %all-to-all-start.8) | async-done | bytes 1572896 | tf_op jit(solution)/shard_map/all_to_all | solution.py:193
  561.3 4.6 fusion.22
  (118 shorter events, 12.9 us)
Async XLA Ops:
  0.6 1.5 copy-start
  0.6 19.5 %copy-start.24 = (bf16[1,1024,384]{2,1,0:T(8,128)(2,1)S(1)}, bf16[1,1024,384]{2,1,0:T(8,128)(2,1)}, u32[]{:S(2)}) copy-start(bf16[1,1024,384]{2,1,0:T(8,128)(2,1)} %param.16) | copy-start | bytes 2359300
  0.7 19.4 %copy-start.26 = (bf16[1,1024,384]{2,1,0:T(8,128)(2,1)S(1)}, bf16[1,1024,384]{2,1,0:T(8,128)(2,1)}, u32[]{:S(2)}) copy-start(bf16[1,1024,384]{2,1,0:T(8,128)(2,1)} %param.15) | copy-start | bytes 2359300
  3.7 33.2 %copy-start.22 = (bf16[2,2,128,128]{3,2,1,0:T(8,128)(2,1)}, bf16[2,2,128,128]{3,2,1,0:T(8,128)(2,1)S(1)}, u32[]{:S(2)}) copy-start(bf16[2,2,128,128]{3,2,1,0:T(8,128)(2,1)S(1)} %broadcast_select_fusion) | copy-start | bytes 393220
  20.1 35.8 %copy-start.19 = (bf16[2,1,128,1024]{3,2,1,0:T(8,128)(2,1)}, bf16[2,1,128,1024]{3,2,1,0:T(8,128)(2,1)S(1)}, u32[]{:S(2)}) copy-start(bf16[2,1,128,1024]{3,2,1,0:T(8,128)(2,1)S(1)} %all-gather) | copy-start | bytes 1572868
  20.1 1.4 copy-start.17
  20.5 2.1 copy-start.29
  21.8 7.6 %copy-start.30 = (s32[2,64]{1,0:T(2,128)S(1)}, s32[2,64]{1,0:T(2,128)}, u32[]{:S(2)}) copy-start(s32[2,64]{1,0:T(2,128)} %param.20) | copy-start | bytes 1540
  22.6 14.3 %all-to-all-start = ((bf16[8,128,128]{2,1,0:T(8,128)(2,1)}), bf16[8,128,128]{2,1,0:T(8,128)(2,1)S(1)}, u32[]{:S(2)}, u32[]{:S(2)}) async-start(bf16[8,128,128]{2,1,0:T(8,128)(2,1)} %bitcast.135), calls=%async_computation | async-start | bytes 524288 | tf_op jit(solution)/shard_map/all_to_all | solution.py:235
  29.3 21.3 %copy-start.9 = (bf16[1,384,1024]{1,2,0:T(8,128)(2,1)}, bf16[1,384,1024]{1,2,0:T(8,128)(2,1)S(1)}, u32[]{:S(2)}) copy-start(bf16[1,384,1024]{1,2,0:T(8,128)(2,1)S(1)} %copy.16) | copy-start | bytes 2359300
  50.6 19.0 %all-to-all-start.1 = ((bf16[16,64,384]{2,1,0:T(8,128)(2,1)}), bf16[16,64,384]{2,1,0:T(8,128)(2,1)S(1)}, u32[]{:S(2)}, u32[]{:S(2)}) async-start(bf16[16,64,384]{2,1,0:T(8,128)(2,1)} %bitcast.17), calls=%async_computation.1 | async-start | bytes 1572864 | tf_op jit(solution)/shard_map/all_to_all | solution.py:193
  54.2 1.7 copy-start.27
  69.6 5.2 copy-start.5
  69.6 4.6 copy-start.31
  69.6 31.4 %all-to-all-start.2 = ((bf16[16,64,768]{2,1,0:T(8,128)(2,1)}), bf16[16,64,768]{2,1,0:T(8,128)(2,1)}, u32[]{:S(2)}, u32[]{:S(2)}) async-start(bf16[16,64,768]{2,1,0:T(8,128)(2,1)} %bitcast.15), calls=%async_computation.2 | async-start | bytes 3145728 | tf_op jit(solution)/shard_map/all_to_all | solution.py:193
  76.5 58.8 %collective-permute-start.9 = (bf16[6,64,384]{2,1,0:T(8,128)(2,1)}, bf16[6,64,384]{2,1,0:T(8,128)(2,1)S(1)}, u32[]{:S(2)}, u32[]{:S(2)}) collective-permute-start(bf16[6,64,384]{2,1,0:T(8,128)(2,1)} %get-tuple-element.393), channel_id=1, source_target_pairs={{0,96},{32,0},{64,32},{96,64},{1,97},{33,1},{65,33},{97,65},{2,98}... | collective-permute-start | bytes 884744 | tf_op jit(solution)/shard_map/ppermute | solution.py:143
  86.9 48.4 %collective-permute-start.10 = (bf16[5,64,384]{2,1,0:T(8,128)(2,1)}, bf16[5,64,384]{2,1,0:T(8,128)(2,1)S(1)}, u32[]{:S(2)}, u32[]{:S(2)}) collective-permute-start(bf16[5,64,384]{2,1,0:T(8,128)(2,1)} %get-tuple-element.394), channel_id=1, source_target_pairs={{0,64},{32,96},{64,0},{96,32},{1,65},{33,97},{65,1},{97,33},{2,66}... | collective-permute-start | bytes 737288 | tf_op jit(solution)/shard_map/ppermute | solution.py:143
  91.9 54.6 %collective-permute-start.11 = (bf16[6,64,384]{2,1,0:T(8,128)(2,1)}, bf16[6,64,384]{2,1,0:T(8,128)(2,1)S(1)}, u32[]{:S(2)}, u32[]{:S(2)}) collective-permute-start(bf16[6,64,384]{2,1,0:T(8,128)(2,1)} %get-tuple-element.395), channel_id=1, source_target_pairs={{0,32},{32,64},{64,96},{96,0},{1,33},{33,65},{65,97},{97,1},{2,34}... | collective-permute-start | bytes 884744 | tf_op jit(solution)/shard_map/ppermute | solution.py:143
  102.6 0.8 copy-start.3
  103.4 86.7 %collective-permute-start.6 = (bf16[6,64,768]{2,1,0:T(8,128)(2,1)S(1)}, bf16[6,64,768]{2,1,0:T(8,128)(2,1)S(1)}, u32[]{:S(2)}, u32[]{:S(2)}) collective-permute-start(bf16[6,64,768]{2,1,0:T(8,128)(2,1)S(1)} %get-tuple-element.390), channel_id=1, source_target_pairs={{0,96},{32,0},{64,32},{96,64},{1,97},{33,1},{65,33},{97,65},{2,98}... | collective-permute-start | bytes 1769480 | tf_op jit(solution)/shard_map/ppermute | solution.py:143
  108.9 81.3 %collective-permute-start.8 = (bf16[6,64,768]{2,1,0:T(8,128)(2,1)S(1)}, bf16[6,64,768]{2,1,0:T(8,128)(2,1)S(1)}, u32[]{:S(2)}, u32[]{:S(2)}) collective-permute-start(bf16[6,64,768]{2,1,0:T(8,128)(2,1)S(1)} %get-tuple-element.392), channel_id=1, source_target_pairs={{0,32},{32,64},{64,96},{96,0},{1,33},{33,65},{65,97},{97,1},{2,34}... | collective-permute-start | bytes 1769480 | tf_op jit(solution)/shard_map/ppermute | solution.py:143
  149.6 33.3 %collective-permute-start = (bf16[1,64,1152]{2,1,0:T(8,128)(2,1)}, bf16[1,64,1152]{2,1,0:T(8,128)(2,1)}, u32[]{:S(2)}, u32[]{:S(2)}) collective-permute-start(bf16[1,64,1152]{2,1,0:T(8,128)(2,1)} %get-tuple-element.675), channel_id=1, source_target_pairs={{0,96},{32,0},{64,32},{96,64},{1,97},{33,1},{65,33},{97,65},{2,98}... | collective-permute-start | bytes 442376 | tf_op jit(solution)/shard_map/while/body/ppermute | solution.py:143
  160.2 24.2 %collective-permute-start.1 = (bf16[1,64,1152]{2,1,0:T(8,128)(2,1)S(1)}, bf16[1,64,1152]{2,1,0:T(8,128)(2,1)}, u32[]{:S(2)}, u32[]{:S(2)}) collective-permute-start(bf16[1,64,1152]{2,1,0:T(8,128)(2,1)S(1)} %get-tuple-element.676), channel_id=1, source_target_pairs={{0,32},{32,64},{64,96},{96,0},{1,33},{33,65},{65,97},{97,1},{2,34}... | collective-permute-start | bytes 442376 | tf_op jit(solution)/shard_map/while/body/ppermute | solution.py:143
  190.1 12.2 %copy-start.4 = (bf16[5,64,768]{2,1,0:T(8,128)(2,1)S(1)}, bf16[5,64,768]{2,1,0:T(8,128)(2,1)}, u32[]{:S(2)}) copy-start(bf16[5,64,768]{2,1,0:T(8,128)(2,1)} %copy-done.3) | copy-start | bytes 1474564
  190.1 66.5 %all-to-all-start.4 = ((bf16[16,64,384]{2,1,0:T(8,128)(2,1)}), bf16[16,64,384]{2,1,0:T(8,128)(2,1)S(1)}, u32[]{:S(2)}, u32[]{:S(2)}) async-start(bf16[16,64,384]{2,1,0:T(8,128)(2,1)} %merge.5), calls=%async_computation.4 | async-start | bytes 1572864 | tf_op jit(solution)/shard_map/all_to_all | solution.py:193
  202.3 51.0 %collective-permute-start.7 = (bf16[5,64,768]{2,1,0:T(8,128)(2,1)S(1)}, bf16[5,64,768]{2,1,0:T(8,128)(2,1)S(1)}, u32[]{:S(2)}, u32[]{:S(2)}) collective-permute-start(bf16[5,64,768]{2,1,0:T(8,128)(2,1)S(1)} %copy-done.4), channel_id=1, source_target_pairs={{0,64},{32,96},{64,0},{96,32},{1,65},{33,97},{65,1},{97,33},{2,66}... | collective-permute-start | bytes 1474568 | tf_op jit(solution)/shard_map/ppermute | solution.py:143
  256.6 6.5 %copy-start.10 = (bf16[1,384,1024]{1,2,0:T(8,128)(2,1)S(1)}, bf16[1,384,1024]{1,2,0:T(8,128)(2,1)}, u32[]{:S(2)}) copy-start(bf16[1,384,1024]{1,2,0:T(8,128)(2,1)} %copy-done.9) | copy-start | bytes 2359300
  256.7 66.6 %copy-start.12 = (bf16[16,64,384]{2,1,0:T(8,128)(2,1)}, bf16[16,64,384]{2,1,0:T(8,128)(2,1)S(1)}, u32[]{:S(2)}) copy-start(bf16[16,64,384]{2,1,0:T(8,128)(2,1)S(1)} %all-to-all-done.4) | copy-start | bytes 2359300
  256.7 22.7 %all-to-all-start.3 = ((bf16[16,64,768]{2,1,0:T(8,128)(2,1)}), bf16[16,64,768]{2,1,0:T(8,128)(2,1)}, u32[]{:S(2)}, u32[]{:S(2)}) async-start(bf16[16,64,768]{2,1,0:T(8,128)(2,1)} %merge.4), calls=%async_computation.3 | async-start | bytes 3145728 | tf_op jit(solution)/shard_map/all_to_all | solution.py:193
  279.4 3.5 copy-start.20
  282.9 49.0 %copy-start.7 = (bf16[1024,768]{1,0:T(8,128)(2,1)}, bf16[1024,768]{1,0:T(8,128)(2,1)S(1)}, u32[]{:S(2)}) copy-start(bf16[1024,768]{1,0:T(8,128)(2,1)S(1)} %fusion.1) | copy-start | bytes 4718596
  282.9 1.7 copy-start.14
  283.3 0.8 copy-start.18
  284.1 26.7 %copy-start.23 = (bf16[2,2,128,128]{3,2,1,0:T(8,128)(2,1)S(1)}, bf16[2,2,128,128]{3,2,1,0:T(8,128)(2,1)}, u32[]{:S(2)}) copy-start(bf16[2,2,128,128]{3,2,1,0:T(8,128)(2,1)} %copy-done.22) | copy-start | bytes 393220
  326.5 4.0 copy-start.15
  326.5 19.1 %all-to-all-start.6 = ((bf16[16,64,384]{2,1,0:T(8,128)(2,1)}), bf16[16,64,384]{2,1,0:T(8,128)(2,1)S(1)}, u32[]{:S(2)}, u32[]{:S(2)}) async-start(bf16[16,64,384]{2,1,0:T(8,128)(2,1)} %bitcast.151), calls=%async_computation.6 | async-start | bytes 1572864 | tf_op jit(solution)/shard_map/all_to_all | solution.py:193
  330.4 1.5 copy-start.21
  330.5 1.5 copy-start.25
  330.5 1.7 copy-start.28
  345.6 4.4 copy-start.6
  345.6 26.7 %all-to-all-start.7 = ((bf16[16,64,768]{2,1,0:T(8,128)(2,1)}), bf16[16,64,768]{2,1,0:T(8,128)(2,1)}, u32[]{:S(2)}, u32[]{:S(2)}) async-start(bf16[16,64,768]{2,1,0:T(8,128)(2,1)} %bitcast.141), calls=%async_computation.7 | async-start | bytes 3145728 | tf_op jit(solution)/shard_map/all_to_all | solution.py:193
  351.7 44.4 %collective-permute-start.15 = (bf16[6,64,384]{2,1,0:T(8,128)(2,1)}, bf16[6,64,384]{2,1,0:T(8,128)(2,1)S(1)}, u32[]{:S(2)}, u32[]{:S(2)}) collective-permute-start(bf16[6,64,384]{2,1,0:T(8,128)(2,1)} %get-tuple-element.418), channel_id=1, source_target_pairs={{0,96},{32,0},{64,32},{96,64},{1,97},{33,1},{65,33},{97,65},{2,98}... | collective-permute-start | bytes 884744 | tf_op jit(solution)/shard_map/ppermute | solution.py:143
  361.0 35.2 %collective-permute-start.17 = (bf16[6,64,384]{2,1,0:T(8,128)(2,1)}, bf16[6,64,384]{2,1,0:T(8,128)(2,1)S(1)}, u32[]{:S(2)}, u32[]{:S(2)}) collective-permute-start(bf16[6,64,384]{2,1,0:T(8,128)(2,1)} %get-tuple-element.420), channel_id=1, source_target_pairs={{0,32},{32,64},{64,96},{96,0},{1,33},{33,65},{65,97},{97,1},{2,34}... | collective-permute-start | bytes 884744 | tf_op jit(solution)/shard_map/ppermute | solution.py:143
  365.0 31.1 %collective-permute-start.16 = (bf16[5,64,384]{2,1,0:T(8,128)(2,1)}, bf16[5,64,384]{2,1,0:T(8,128)(2,1)S(1)}, u32[]{:S(2)}, u32[]{:S(2)}) collective-permute-start(bf16[5,64,384]{2,1,0:T(8,128)(2,1)} %get-tuple-element.419), channel_id=1, source_target_pairs={{0,64},{32,96},{64,0},{96,32},{1,65},{33,97},{65,1},{97,33},{2,66}... | collective-permute-start | bytes 737288 | tf_op jit(solution)/shard_map/ppermute | solution.py:143
  373.9 0.8 copy-start.1
  374.8 30.7 %collective-permute-start.12 = (bf16[6,64,768]{2,1,0:T(8,128)(2,1)S(1)}, bf16[6,64,768]{2,1,0:T(8,128)(2,1)S(1)}, u32[]{:S(2)}, u32[]{:S(2)}) collective-permute-start(bf16[6,64,768]{2,1,0:T(8,128)(2,1)S(1)} %get-tuple-element.415), channel_id=1, source_target_pairs={{0,96},{32,0},{64,32},{96,64},{1,97},{33,1},{65,33},{97,65},{2,98}... | collective-permute-start | bytes 1769480 | tf_op jit(solution)/shard_map/ppermute | solution.py:143
  383.8 78.7 %collective-permute-start.14 = (bf16[6,64,768]{2,1,0:T(8,128)(2,1)S(1)}, bf16[6,64,768]{2,1,0:T(8,128)(2,1)S(1)}, u32[]{:S(2)}, u32[]{:S(2)}) collective-permute-start(bf16[6,64,768]{2,1,0:T(8,128)(2,1)S(1)} %get-tuple-element.417), channel_id=1, source_target_pairs={{0,32},{32,64},{64,96},{96,0},{1,33},{33,65},{65,97},{97,1},{2,34}... | collective-permute-start | bytes 1769480 | tf_op jit(solution)/shard_map/ppermute | solution.py:143
  400.3 71.9 %copy-start.2 = (bf16[5,64,768]{2,1,0:T(8,128)(2,1)S(1)}, bf16[5,64,768]{2,1,0:T(8,128)(2,1)}, u32[]{:S(2)}) copy-start(bf16[5,64,768]{2,1,0:T(8,128)(2,1)} %copy-done.1) | copy-start | bytes 1474564
  462.5 67.6 %all-to-all-start.9 = ((bf16[16,64,384]{2,1,0:T(8,128)(2,1)}), bf16[16,64,384]{2,1,0:T(8,128)(2,1)S(1)}, u32[]{:S(2)}, u32[]{:S(2)}) async-start(bf16[16,64,384]{2,1,0:T(8,128)(2,1)} %merge.7), calls=%async_computation.9 | async-start | bytes 1572864 | tf_op jit(solution)/shard_map/all_to_all | solution.py:193
  472.2 54.5 %collective-permute-start.13 = (bf16[5,64,768]{2,1,0:T(8,128)(2,1)S(1)}, bf16[5,64,768]{2,1,0:T(8,128)(2,1)S(1)}, u32[]{:S(2)}, u32[]{:S(2)}) collective-permute-start(bf16[5,64,768]{2,1,0:T(8,128)(2,1)S(1)} %copy-done.2), channel_id=1, source_target_pairs={{0,64},{32,96},{64,0},{96,32},{1,65},{33,97},{65,1},{97,33},{2,66}... | collective-permute-start | bytes 1474568 | tf_op jit(solution)/shard_map/ppermute | solution.py:143
  530.1 7.2 %copy-start.11 = (bf16[1,384,1024]{1,2,0:T(8,128)(2,1)S(1)}, bf16[1,384,1024]{1,2,0:T(8,128)(2,1)}, u32[]{:S(2)}) copy-start(bf16[1,384,1024]{1,2,0:T(8,128)(2,1)} %copy-done.9) | copy-start | bytes 2359300
  530.1 7.2 %copy-start.13 = (bf16[16,64,384]{2,1,0:T(8,128)(2,1)S(1)}, bf16[16,64,384]{2,1,0:T(8,128)(2,1)}, u32[]{:S(2)}) copy-start(bf16[16,64,384]{2,1,0:T(8,128)(2,1)} %copy-done.12) | copy-start | bytes 2359300
  530.1 7.2 %copy-start.16 = (bf16[1024,384]{1,0:T(8,128)(2,1)S(1)}, bf16[1024,384]{1,0:T(8,128)(2,1)}, u32[]{:S(2)}) copy-start(bf16[1024,384]{1,0:T(8,128)(2,1)} %fusion.12) | copy-start | bytes 2359300
  530.1 31.2 %all-to-all-start.8 = ((bf16[16,64,768]{2,1,0:T(8,128)(2,1)}), bf16[16,64,768]{2,1,0:T(8,128)(2,1)}, u32[]{:S(2)}, u32[]{:S(2)}) async-start(bf16[16,64,768]{2,1,0:T(8,128)(2,1)} %merge.6), calls=%async_computation.8 | async-start | bytes 3145728 | tf_op jit(solution)/shard_map/all_to_all | solution.py:193
  540.4 20.9 %copy-start.8 = (bf16[1024,768]{1,0:T(8,128)(2,1)S(1)}, bf16[1024,768]{1,0:T(8,128)(2,1)}, u32[]{:S(2)}) copy-start(bf16[1024,768]{1,0:T(8,128)(2,1)} %copy-done.7) | copy-start | bytes 4718596
